TPU v7x, 512 devices: a whole 4x4x16 slice. The times are simulated.
512 devices in a mesh: group: 16 (over y, z_hi), tile: 32 (over z_lo, x, core).
Axes of the slice: x: 4, y: 4, z: 16 (z_hi: 4, z_lo: 4; z = z_hi * 4 + z_lo), core: 2. Of those that a mesh axis runs over, the one named last changes fastest.
Arguments:
- features: bfloat16 [1024, 512, 128], P(('group', 'tile')), may hold values from -6 to 6
- occupancy: int32 [1024, 512], P(('group', 'tile')), may hold values 0 or 1
- block_pos: int32 [1024], P(('group', 'tile')), may hold values from -1 to 7, as said below
- kernel: bfloat16 [27, 128, 128], replicated, may hold values from -0.109375 to 0.109375
- out_grad: bfloat16 [1024, 512, 128], P(('group', 'tile')), may hold values from -6 to 6
Outputs:
- conv_out: bfloat16 [1024, 512, 128], P(('group', 'tile'))
- feature_grad: bfloat16 [1024, 512, 128], P(('group', 'tile'))
- kernel_grad: float32 [27, 128, 128], replicated
Inputs may be any that keep to these rules, and one draw needn't show every extreme that they name: `block_pos`: within each device's 2 slots the filled ones come first and hold distinct block heights; -1 marks an empty slot. Every device fills at least one slot and some device fills all 2.
All inputs are finite; a program needn't handle non-finite values. No bound on the sum of `occupancy` on one device may be relied on, other than what follows from the above.
Results may differ from a plain program's by a relative error of at most 0.001.
Values may be sent and summed in bfloat16 or wider, within the bound.
No kernel may reach another device: no remote copies, remote signals or barrier semaphores. Data moves between devices by JAX's collectives and lax.ppermute only.
A program may use at most 128 MiB of HBM per device.

v0:
```python
import math

import jax
import jax.numpy as jnp
from jax import lax
from jax.sharding import PartitionSpec as P

BE = 8
VOX = 512
C = 128
BLK_DEV = 2
GZ = 8


def extended(block, sides, width):
    for axis, dim in sides:
        count = lax.axis_size(axis)
        forward = [(i, i + 1) for i in range(count - 1)]
        backward = [(target, source) for source, target in forward]
        low = lax.ppermute(
            lax.slice_in_dim(block, block.shape[dim] - width, None, axis=dim), axis, forward
        )
        high = lax.ppermute(lax.slice_in_dim(block, 0, width, axis=dim), axis, backward)
        block = jnp.concatenate([low, block, high], axis=dim)
    return block


def place_column(block_field, positions):
    heights = jnp.arange(GZ, dtype=jnp.int32)
    onehot = (heights[:, None] == positions[None, :]).astype(jnp.bfloat16)
    blocks = block_field.reshape(BLK_DEV, BE, BE, BE, C)
    placed = jnp.einsum("zs,sxyvc->xyzvc", onehot, blocks, preferred_element_type=jnp.float32)
    return placed.reshape(BE, BE, GZ * BE, C).astype(jnp.bfloat16)


def slot_stack(padded, position):
    lower_z = BE * jnp.maximum(position, 0)
    anchor_index = jnp.zeros((), jnp.int32)
    window = lax.dynamic_slice(
        padded, (anchor_index, anchor_index, lower_z, anchor_index), (BE + 2, BE + 2, BE + 2, C)
    )
    pieces = [
        window[step_x : step_x + BE, step_y : step_y + BE, step_z : step_z + BE].reshape(VOX, C)
        for step_x in range(3)
        for step_y in range(3)
        for step_z in range(3)
    ]
    return jnp.stack(pieces)


def body(features, occupancy, block_pos, kernel, out_grad):
    slot_live = (block_pos >= 0).astype(jnp.float32)
    active = occupancy.astype(jnp.float32) * slot_live[:, None]
    weight_mask = active.astype(jnp.bfloat16)[:, :, None]
    masked_in = features * weight_mask
    masked_grad = out_grad * weight_mask
    column_in = place_column(masked_in, block_pos)
    column_grad = place_column(masked_grad, block_pos)
    padded_in = extended(column_in, (("group", 0), ("tile", 1)), 1)
    padded_grad = extended(column_grad, (("group", 0), ("tile", 1)), 1)
    z_padding = ((0, 0), (0, 0), (1, 1), (0, 0))
    padded_in = jnp.pad(padded_in, z_padding)
    padded_grad = jnp.pad(padded_grad, z_padding)
    kernel_flipped = kernel[::-1]

    def per_slot(partial_value, inputs):
        position, slot_mask, own_grad = inputs
        stack_in = slot_stack(padded_in, position)
        stack_grad = slot_stack(padded_grad, position)
        conv_block = (
            jnp.einsum("kvc,kcd->vd", stack_in, kernel, preferred_element_type=jnp.float32)
            * slot_mask[:, None]
        )
        back_block = (
            jnp.einsum(
                "kvd,kcd->vc", stack_grad, kernel_flipped, preferred_element_type=jnp.float32
            )
            * slot_mask[:, None]
        )
        partial_value = partial_value + jnp.einsum(
            "kvc,vd->kcd", stack_in, own_grad, preferred_element_type=jnp.float32
        )
        return (partial_value, (conv_block.astype(jnp.bfloat16), back_block.astype(jnp.bfloat16)))

    initial = jnp.zeros(kernel.shape, jnp.float32)
    partial_value, (conv_out, feature_grad) = lax.scan(
        per_slot, initial, (block_pos, active, masked_grad)
    )
    total_blocks = BLK_DEV * lax.axis_size("group") * lax.axis_size("tile")
    grad_scale = 1.0 / math.sqrt(total_blocks * VOX)
    summed = lax.psum(partial_value, ("group", "tile"))
    return (conv_out, feature_grad, summed * grad_scale)


def solution(mesh):
    in_specs = (
        P(("group", "tile"), None, None),
        P(("group", "tile"), None),
        P(("group", "tile")),
        P(),
        P(("group", "tile"), None, None),
    )
    out_specs = (P(("group", "tile"), None, None), P(("group", "tile"), None, None), P())
    return jax.shard_map(body, mesh=mesh, in_specs=in_specs, out_specs=out_specs, check_vma=False)
```

profile of v0, /device:TPU:1, one launch (start us, length us, event | category | flops | bytes accessed | tf_op | source)
XLA Modules:
  0.0 706.7 jit_solution(5482376376937690392)
XLA Ops:
  11.2 9.7 %collective-permute-start.4 = (bf16[1,8,64,128]{3,2,1,0:T(8,128)(2,1)S(1)}, bf16[1,8,64,128]{3,2,1,0:T(8,128)(2,1)S(1)}, u32[]{:S(2)}, u32[]{:S(2)}) collective-permute-start(bf16[1,8,64,128]{3,2,1,0:T(8,128)(2,1)S(1)} %bitcast.318), channel_id=1, source_target_pairs={{0,32},{32,64},{64,96},{96,128},{128,160},{160,192},{192,224},{224... | collective-permute-start | bytes 393224 | tf_op jit(solution)/shard_map/ppermute | solution.py:20
  23.4 9.4 %collective-permute-start = (bf16[1,8,64,128]{3,2,1,0:T(8,128)(2,1)S(1)}, bf16[1,8,64,128]{3,2,1,0:T(8,128)(2,1)S(1)}, u32[]{:S(2)}, u32[]{:S(2)}) collective-permute-start(bf16[1,8,64,128]{3,2,1,0:T(8,128)(2,1)S(1)} %bitcast.316), channel_id=1, source_target_pairs={{0,32},{32,64},{64,96},{96,128},{128,160},{160,192},{192,224},{224... | collective-permute-start | bytes 393224 | tf_op jit(solution)/shard_map/ppermute | solution.py:20
  34.5 7.1 collective-permute-done.5
  41.6 8.4 %collective-permute-start.6 = (bf16[10,1,64,128]{3,2,1,0:T(8,128)(2,1)S(1)}, bf16[10,1,64,128]{3,2,1,0:T(8,128)(2,1)S(1)}, u32[]{:S(2)}, u32[]{:S(2)}) collective-permute-start(bf16[10,1,64,128]{3,2,1,0:T(8,128)(2,1)S(1)} %get-tuple-element.206), channel_id=1, source_target_pairs={{0,1},{1,2},{2,3},{3,4},{4,5},{5,6},{6,7},{7,8},{8,9},{9,10},{10,1... | collective-permute-start | bytes 491528 | tf_op jit(solution)/shard_map/ppermute | solution.py:20
  50.0 1.9 collective-permute-start.7
  52.3 2.6 rev.3
  54.9 3.6 collective-permute-start.2
  58.6 2.1 collective-permute-start.3
  61.4 2.6 select_maximum_fusion
  65.2 2.5 select_maximum_fusion.4
  67.8 155.8 %while.15 = (s32[]{:T(128)}, f32[27,128,128]{2,1,0:T(8,128)}, bf16[2,512,128]{2,1,0:T(8,128)(2,1)}, bf16[2,512,128]{2,1,0:T(8,128)(2,1)}, s32[2]{0:T(128)S(1)}, ...) while((s32[]{:T(128)}, f32[27,128,128]{2,1,0:T(8,128)}, ...), condition=%wide.region_1.2_spmd.clone, body=%wide.region_0.1_spmd.clone.sunk | while | flops 1360101376 | bytes 78193248 | solution.py:86
  69.0 9.6 %constant_dynamic-slice_fusion.57 = (bf16[8,8,8,128]{3,2,1,0:T(8,128)(2,1)S(1)}, bf16[8,8,8,128]{3,2,1,0:T(8,128)(2,1)S(1)}, bf16[8,8,8,128]{3,2,1,0:T(8,128)(2,...) fusion(bf16[10,10,66,128]{3,2,1,0:T(8,128)(2,1)S(1)} %get-tuple, ...), kind=kLoop, calls=%fused_computation.119.clone.1 | loop fusion | bytes 14155796 | tf_op jit(solution)/shard_map/while/body/eval_jaxpr/slice | solution.py:43
  81.7 1.7 copy.92
  88.1 1.7 copy.94
  94.6 1.7 copy.96
  97.8 1.7 copy.97
  138.5 4.5 select_add_fusion.2
  146.2 10.6 %constant_dynamic-slice_fusion.57 = (bf16[8,8,8,128]{3,2,1,0:T(8,128)(2,1)S(1)}, bf16[8,8,8,128]{3,2,1,0:T(8,128)(2,1)S(1)}, bf16[8,8,8,128]{3,2,1,0:T(8,128)(2,...) fusion(bf16[10,10,66,128]{3,2,1,0:T(8,128)(2,1)S(1)} %get-tuple, ...), kind=kLoop, calls=%fused_computation.119.clone.1 | loop fusion | bytes 14155796 | tf_op jit(solution)/shard_map/while/body/eval_jaxpr/slice | solution.py:43
  166.2 1.7 copy.94
  172.7 1.7 copy.96
  175.9 1.7 copy.97
  216.7 5.0 select_add_fusion.2
  223.6 473.3 %all-reduce.4.cloned.1.call-done = f32[27,128,128]{2,1,0:T(8,128)} async-done(((f32[27,128,128]{2,1,0:T(8,128)}), f32[27,128,128]{2,1,0:T(8,128)}) %all-reduce.4.cloned.1.call-update) | async-done | bytes 1769488 | tf_op jit(solution)/shard_map/psum | solution.py:91
  696.9 2.9 broadcast_multiply_fusion
  (238 shorter events, 122.9 us)
Async XLA Ops:
  7.2 689.7 %all-reduce.4.cloned.1.call-start = ((), (), s32[]{:S(2)}) async-start(), calls=%async_computation | async-start | bytes 3538944 | tf_op jit(solution)/shard_map/psum | solution.py:91
  9.9 31.8 %copy-start.3 = (bf16[2,512,128]{2,1,0:T(8,128)(2,1)}, bf16[2,512,128]{2,1,0:T(8,128)(2,1)S(1)}, u32[]{:S(2)}) copy-start(bf16[2,512,128]{2,1,0:T(8,128)(2,1)S(1)} %get-tuple-element.397) | copy-start | bytes 786436
  11.2 23.3 %collective-permute-start.4 = (bf16[1,8,64,128]{3,2,1,0:T(8,128)(2,1)S(1)}, bf16[1,8,64,128]{3,2,1,0:T(8,128)(2,1)S(1)}, u32[]{:S(2)}, u32[]{:S(2)}) collective-permute-start(bf16[1,8,64,128]{3,2,1,0:T(8,128)(2,1)S(1)} %bitcast.318), channel_id=1, source_target_pairs={{0,32},{32,64},{64,96},{96,128},{128,160},{160,192},{192,224},{224... | collective-permute-start | bytes 393224 | tf_op jit(solution)/shard_map/ppermute | solution.py:20
  20.9 20.7 %collective-permute-start.5 = (bf16[1,8,64,128]{3,2,1,0:T(8,128)(2,1)S(1)}, bf16[1,8,64,128]{3,2,1,0:T(8,128)(2,1)S(1)}, u32[]{:S(2)}, u32[]{:S(2)}) collective-permute-start(bf16[1,8,64,128]{3,2,1,0:T(8,128)(2,1)S(1)} %bitcast.319), channel_id=1, source_target_pairs={{32,0},{64,32},{96,64},{128,96},{160,128},{192,160},{224,192},{256... | collective-permute-start | bytes 393224 | tf_op jit(solution)/shard_map/ppermute | solution.py:23
  23.4 31.4 %collective-permute-start = (bf16[1,8,64,128]{3,2,1,0:T(8,128)(2,1)S(1)}, bf16[1,8,64,128]{3,2,1,0:T(8,128)(2,1)S(1)}, u32[]{:S(2)}, u32[]{:S(2)}) collective-permute-start(bf16[1,8,64,128]{3,2,1,0:T(8,128)(2,1)S(1)} %bitcast.316), channel_id=1, source_target_pairs={{0,32},{32,64},{64,96},{96,128},{128,160},{160,192},{192,224},{224... | collective-permute-start | bytes 393224 | tf_op jit(solution)/shard_map/ppermute | solution.py:20
  32.9 22.0 %collective-permute-start.1 = (bf16[1,8,64,128]{3,2,1,0:T(8,128)(2,1)S(1)}, bf16[1,8,64,128]{3,2,1,0:T(8,128)(2,1)S(1)}, u32[]{:S(2)}, u32[]{:S(2)}) collective-permute-start(bf16[1,8,64,128]{3,2,1,0:T(8,128)(2,1)S(1)} %bitcast.317), channel_id=1, source_target_pairs={{32,0},{64,32},{96,64},{128,96},{160,128},{192,160},{224,192},{256... | collective-permute-start | bytes 393224 | tf_op jit(solution)/shard_map/ppermute | solution.py:23
  41.6 19.1 %collective-permute-start.6 = (bf16[10,1,64,128]{3,2,1,0:T(8,128)(2,1)S(1)}, bf16[10,1,64,128]{3,2,1,0:T(8,128)(2,1)S(1)}, u32[]{:S(2)}, u32[]{:S(2)}) collective-permute-start(bf16[10,1,64,128]{3,2,1,0:T(8,128)(2,1)S(1)} %get-tuple-element.206), channel_id=1, source_target_pairs={{0,1},{1,2},{2,3},{3,4},{4,5},{5,6},{6,7},{7,8},{8,9},{9,10},{10,1... | collective-permute-start | bytes 491528 | tf_op jit(solution)/shard_map/ppermute | solution.py:20
  50.0 11.3 %collective-permute-start.7 = (bf16[10,1,64,128]{3,2,1,0:T(8,128)(2,1)S(1)}, bf16[10,1,64,128]{3,2,1,0:T(8,128)(2,1)}, u32[]{:S(2)}, u32[]{:S(2)}) collective-permute-start(bf16[10,1,64,128]{3,2,1,0:T(8,128)(2,1)S(1)} %get-tuple-element.207), channel_id=1, source_target_pairs={{1,0},{2,1},{3,2},{4,3},{5,4},{6,5},{7,6},{8,7},{9,8},{10,9},{11,1... | collective-permute-start | bytes 491528 | tf_op jit(solution)/shard_map/ppermute | solution.py:23
  52.3 8.4 %copy-start.1 = (bf16[8,8,8,8,128]{4,3,2,1,0:T(8,128)(2,1)}, bf16[8,8,8,8,128]{4,3,2,1,0:T(8,128)(2,1)S(1)}, u32[]{:S(2)}) copy-start(bf16[8,8,8,8,128]{4,3,2,1,0:T(8,128)(2,1)S(1)} %copy.60) | copy-start | bytes 3145732
  54.9 12.8 %copy-start.8 = (s32[2]{0:T(128)S(1)}, s32[2]{0:T(128)}, u32[]{:S(2)}) copy-start(s32[2]{0:T(128)} %param.9) | copy-start | bytes 28
  54.9 9.0 %collective-permute-start.2 = (bf16[10,1,64,128]{3,2,1,0:T(8,128)(2,1)S(1)}, bf16[10,1,64,128]{3,2,1,0:T(8,128)(2,1)S(1)}, u32[]{:S(2)}, u32[]{:S(2)}) collective-permute-start(bf16[10,1,64,128]{3,2,1,0:T(8,128)(2,1)S(1)} %get-tuple-element.208), channel_id=1, source_target_pairs={{0,1},{1,2},{2,3},{3,4},{4,5},{5,6},{6,7},{7,8},{8,9},{9,10},{10,1... | collective-permute-start | bytes 491528 | tf_op jit(solution)/shard_map/ppermute | solution.py:20
  58.6 6.6 collective-permute-start.3
  61.4 3.8 copy-start.2
  78.7 1.2 copy-start.12
  130.7 7.8 %copy-start.4 = (bf16[2,512,128]{2,1,0:T(8,128)(2,1)S(1)}, bf16[2,512,128]{2,1,0:T(8,128)(2,1)}, u32[]{:S(2)}) copy-start(bf16[2,512,128]{2,1,0:T(8,128)(2,1)} %get-tuple-element.433) | copy-start | bytes 786436 | tf_op jit(solution)/shard_map/while
  138.5 4.5 copy-start
  138.5 4.5 copy-start.5
  138.5 4.5 copy-start.10
  143.0 1.9 copy-start.9
  208.8 7.8 %copy-start.4 = (bf16[2,512,128]{2,1,0:T(8,128)(2,1)S(1)}, bf16[2,512,128]{2,1,0:T(8,128)(2,1)}, u32[]{:S(2)}) copy-start(bf16[2,512,128]{2,1,0:T(8,128)(2,1)} %get-tuple-element.433) | copy-start | bytes 786436 | tf_op jit(solution)/shard_map/while
  216.7 5.0 copy-start
  216.7 5.0 copy-start.5
  216.7 5.0 copy-start.10
  221.7 1.9 copy-start.9
  (8 other events, 7.0 us)
Sparse Core Ops, SparseCore 0:
  223.7 473.1 all-reduce.3
where the time goes:
time: 708 us; the launch traced here: 707 us
  waiting for transfers between devices  482 us (68%)
  local copies, waits for them, and re-layouts  144 us (20%)
  starting transfers between devices  37.8 us (5%)
  matrix products  16.5 us (2%)
  between operations  14.3 us (2%)
  other arithmetic  10.8 us (2%)
    psum x1, waiting for transfers between devices, body(): summed = lax.psum(partial_value, ('group', 'tile'))  473 us
    while x140, local copies, waits for them, and re-layouts  66.2 us
    reshape x54, local copies, waits for them, and re-layouts, slot_stack(): return jnp.stack(pieces)  50.7 us
    ppermute x4, starting transfers between devices, extended(): lax.ppermute(lax.slice_in_dim(block, block.shape[dim] - width, None, axis...  31.1 us
    slice x2, local copies, waits for them, and re-layouts, slot_stack(): window[step_x:step_x + BE, step_y:step_y + BE, step_z:step_z + BE]  20.2 us
  transfers between devices with their start and end apart: 9, of which 3 were waited for; matrix products, arithmetic and copies ran while one was open for 1% of the time, Pallas kernels for 0%

commit v1 on v0

v1 whole, which is shorter than its diff:
```python
import math

import jax
import jax.numpy as jnp
from jax import lax
from jax.experimental import pallas as pl
from jax.experimental.pallas import tpu as pltpu
from jax.sharding import PartitionSpec as P

BE = 8
VOX = 512
C = 128
KV = 27
BLK_DEV = 2
WIN = BE + 2
SLAB = WIN * BE * BE
SIDE = 9 * C
AXES = ("group", "tile")
FACE = 2 * BLK_DEV * BE * BE
EDGE = 2 * BLK_DEV * BE
TAG = 16
CHUNK = 112
HALF = 16 * CHUNK
CORE = 1
X_SETS = [[z * 8 + x * 2 + core for x in range(4)] for z in range(4) for core in range(2)]
Z_LO_SETS = [[z * 8 + x * 2 + core for z in range(4)] for x in range(4) for core in range(2)]
Y_SETS = [[y * 4 + z for y in range(4)] for z in range(4)]
Z_HI_BITS = (32, 96)


def tags(pos_ref):
    return jnp.concatenate(
        [jnp.full((BE, C), pos_ref[s].astype(jnp.float32), jnp.float32) for s in range(BLK_DEV)]
    ).astype(jnp.bfloat16)


def prep_kernel(pos_ref, occ_ref, feat_ref, grad_ref, in_ref, g_ref, mask_ref, ylo_ref, yhi_ref):
    occ = occ_ref[...].astype(jnp.float32)
    for face in (ylo_ref, yhi_ref):
        face[FACE:FACE + TAG, :] = tags(pos_ref)
    for s in range(BLK_DEV):
        live = (pos_ref[s] >= 0).astype(jnp.float32)
        mask = jnp.concatenate([
            jnp.broadcast_to(occ[s:s + 1, r * C:(r + 1) * C] * live, (C, C)).T for r in range(VOX // C)
        ])
        mask_ref[s * VOX:(s + 1) * VOX, :] = mask.astype(jnp.bfloat16)
        for field, (src, dst) in enumerate(((feat_ref, in_ref), (grad_ref, g_ref))):
            value = jnp.where(mask > 0, src[s].astype(jnp.float32), 0.0)
            dst[s * VOX:(s + 1) * VOX, :] = value.astype(jnp.bfloat16)
            cube = value.reshape(BE, BE, BE, C)
            at = (field * BLK_DEV + s) * BE * BE
            here = slice(at, at + BE * BE)
            ylo_ref[here, :] = cube[:, 0].reshape(BE * BE, C).astype(jnp.bfloat16)
            yhi_ref[here, :] = cube[:, BE - 1].reshape(BE * BE, C).astype(jnp.bfloat16)


def x_faces_kernel(pos_ref, in_ref, g_ref, low_ref, high_ref, xlo_ref, xhi_ref):
    for x, out in ((0, xlo_ref), (BE - 1, xhi_ref)):
        for field, own in enumerate((in_ref, g_ref)):
            for s in range(BLK_DEV):
                at = (field * BLK_DEV + s) * BE * BE
                first = s * VOX + x * BE * BE
                out[at:at + BE * BE, :] = own[first:first + BE * BE, :]
        for side, ref in enumerate((low_ref, high_ref)):
            edge = [
                ref[n * BE * BE:(n + 1) * BE * BE, :].astype(jnp.float32)[x * BE:(x + 1) * BE]
                for n in range(2 * BLK_DEV)
            ]
            at = FACE + side * EDGE
            out[at:at + EDGE, :] = jnp.concatenate(edge).astype(jnp.bfloat16)
            at = FACE + 2 * EDGE + side * TAG
            out[at:at + TAG, :] = ref[FACE:FACE + TAG, :]
        at = FACE + 2 * EDGE + 2 * TAG
        out[at:at + TAG, :] = tags(pos_ref)


def fill_windows(field, slots, pos_ref, own_ref, y_from, x_from, z_ref, a_ref):
    row = lax.broadcasted_iota(jnp.int32, (BE, C), 0)
    first = field * BLK_DEV
    regions = []

    def face_of(ref, shape):
        return [
            ref[n * BE * BE:(n + 1) * BE * BE, :].astype(jnp.float32).reshape(shape)
            for n in range(first, first + BLK_DEV)
        ]

    def tags_of(ref, at):
        tag = ref[at:at + TAG, :].astype(jnp.float32)
        return [tag[0:BE], tag[BE:2 * BE]]

    own = [own_ref[n * VOX:(n + 1) * VOX, :].astype(jnp.float32).reshape(BE, BE, BE, C) for n in range(BLK_DEV)]
    own_tags = [jnp.full((BE, C), pos_ref[n].astype(jnp.float32), jnp.float32) for n in range(BLK_DEV)]
    inside = slice(1, BE + 1)
    ends = (slice(0, 1), slice(WIN - 1, WIN))
    regions.append((inside, inside, own, own_tags))
    for ref, end in zip(y_from, ends):
        regions.append((inside, end, face_of(ref, (BE, 1, BE, C)), tags_of(ref, FACE)))
    for ref, end in zip(x_from, ends):
        regions.append((end, inside, face_of(ref, (1, BE, BE, C)), tags_of(ref, FACE + 2 * EDGE + 2 * TAG)))
        for side, other in enumerate(ends):
            edge = ref[FACE + side * EDGE:FACE + (side + 1) * EDGE, :].astype(jnp.float32)
            data = [edge[n * BE:(n + 1) * BE].reshape(1, 1, BE, C) for n in range(first, first + BLK_DEV)]
            regions.append((end, other, data, tags_of(ref, FACE + 2 * EDGE + side * TAG)))

    for i, s in enumerate(slots):
        here = pos_ref[s].astype(jnp.float32)
        for xs, ys, data, tags in regions:
            delta = [tag - here for tag in tags]
            for o3 in range(3):
                picks = []
                for n in range(BLK_DEV):
                    if o3 == 0:
                        wanted = jnp.where(row == 0, -1.0, 0.0)
                        moved = pltpu.roll(data[n].reshape(-1, BE, C), 1, 1)
                    elif o3 == 2:
                        wanted = jnp.where(row == BE - 1, 1.0, 0.0)
                        moved = pltpu.roll(data[n].reshape(-1, BE, C), BE - 1, 1)
                    else:
                        wanted = jnp.zeros((BE, C), jnp.float32)
                        moved = data[n].reshape(-1, BE, C)
                    picks.append(((delta[n] == wanted)[None], moved))
                value = jnp.where(picks[1][0], picks[1][1], 0.0)
                value = jnp.where(picks[0][0], picks[0][1], value)
                z_ref[o3, xs, ys] = value.reshape(data[0].shape)
        for o2 in range(3):
            for o3 in range(3):
                j = o2 * 3 + o3
                piece = z_ref[o3, :, o2:o2 + BE].reshape(SLAB, C)
                a_ref[i, :, j * C:(j + 1) * C] = piece.astype(jnp.bfloat16)


def wgrad_kernel(scale, pos_ref, core_ref, in_ref, g_ref, *refs):
    halo, keep_ref, send_ref, z_ref, a_ref, total_ref = refs[:4], *refs[-5:]
    fill_windows(1, (0, 1), pos_ref, g_ref, halo[0:2], halo[2:4], z_ref, a_ref)
    inner = [
        jnp.transpose(in_ref[s * VOX:(s + 1) * VOX, :].astype(jnp.float32)).astype(jnp.bfloat16)
        for s in range(BLK_DEV)
    ]
    total_ref[KV * C:, :] = jnp.zeros((2 * HALF - KV * C, C), jnp.float32)
    for e1 in range(3):
        rows = slice(e1 * BE * BE, e1 * BE * BE + VOX)
        total = jnp.dot(inner[0], a_ref[0, rows, :], preferred_element_type=jnp.float32)
        total = total + jnp.dot(inner[1], a_ref[1, rows, :], preferred_element_type=jnp.float32)
        total = total * scale
        for j in range(9):
            k = KV - 1 - (9 * e1 + j)
            total_ref[k * C:(k + 1) * C, :] = total[:, j * C:(j + 1) * C]
    core = core_ref[0]
    keep_ref[...] = total_ref[pl.ds(pl.multiple_of(core * HALF, HALF), HALF), :]
    send_ref[...] = total_ref[pl.ds(pl.multiple_of((1 - core) * HALF, HALF), HALF), :]


def place_kernel(core_ref, near_ref, far_ref, out_ref):
    first = core_ref[0] == 0
    rest = KV * C - HALF
    out_ref[0:HALF, :] = jnp.where(first, near_ref[...], far_ref[...])
    out_ref[HALF:KV * C, :] = jnp.where(first, far_ref[0:rest, :], near_ref[0:rest, :])


def turn_kernel(w_ref, out_ref, done_ref):
    for k in range(KV):
        at = (KV - 1 - k) * C
        out_ref[at:at + C, :] = jnp.transpose(w_ref[k * C:(k + 1) * C, :].astype(jnp.float32)).astype(jnp.bfloat16)
    done_ref[...] = jnp.zeros_like(done_ref)


def conv_kernel(field, slot, pos_ref, own_ref, mask_ref, w_ref, *refs):
    halo, out_ref, done_ref, z_ref, a_ref = refs[:4], *refs[-4:]
    fill_windows(field, (slot,), pos_ref, own_ref, halo[0:2], halo[2:4], z_ref, a_ref)
    total = None
    for e1 in range(3):
        rows = slice(e1 * BE * BE, e1 * BE * BE + VOX)
        part = jnp.dot(
            a_ref[0, rows, :], w_ref[e1 * SIDE:(e1 + 1) * SIDE, :], preferred_element_type=jnp.float32
        )
        total = part if total is None else total + part
    mask = mask_ref[slot * VOX:(slot + 1) * VOX, :].astype(jnp.float32)
    out_ref[0] = jnp.where(mask > 0, total, 0.0).astype(jnp.bfloat16)
    done_ref[...] = jnp.zeros_like(done_ref)


VMEM = pl.BlockSpec(memory_space=pltpu.VMEM)
ANY = pl.BlockSpec(memory_space=pl.ANY)
SMEM = pl.BlockSpec(memory_space=pltpu.SMEM)
PARAMS = pltpu.CompilerParams(vmem_limit_bytes=40 * 1024 * 1024)


def bf16(*shape):
    return jax.ShapeDtypeStruct(shape, jnp.bfloat16)


def whole(*shape):
    return pl.BlockSpec(shape, lambda i: (0,) * len(shape))


def prep(block_pos, occupancy, features, out_grad):
    return pl.pallas_call(
        prep_kernel,
        grid=(1,),
        out_shape=[bf16(BLK_DEV * VOX, C)] * 3 + [bf16(FACE + TAG, C)] * 2,
        in_specs=[SMEM, whole(BLK_DEV, VOX)] + [whole(BLK_DEV, VOX, C)] * 2,
        out_specs=[VMEM] * 5,
        compiler_params=PARAMS,
        name="mask_and_faces",
    )(block_pos, occupancy, features, out_grad)


def x_faces(block_pos, own_in, own_grad, low, high):
    return pl.pallas_call(
        x_faces_kernel,
        out_shape=[bf16(FACE + 2 * EDGE + 3 * TAG, C)] * 2,
        in_specs=[SMEM] + [VMEM] * 4,
        out_specs=[VMEM] * 2,
        compiler_params=PARAMS,
        name="x_faces",
    )(block_pos, own_in, own_grad, low, high)


def turn(weights, after):
    def kernel(w_ref, after_ref, *refs):
        turn_kernel(w_ref, *refs)

    return pl.pallas_call(
        kernel,
        out_shape=[bf16(KV * C, C), jax.ShapeDtypeStruct((BE, C), jnp.float32)],
        in_specs=[VMEM, ANY],
        out_specs=[VMEM] * 2,
        compiler_params=PARAMS,
        name="turn_weights",
    )(weights, after)


def scratch(slots):
    return [
        pltpu.VMEM((3, WIN, WIN, BE, C), jnp.float32),
        pltpu.VMEM((slots, SLAB, SIDE), jnp.bfloat16),
    ]


def wgrad(scale, block_pos, core, own_in, own_grad, halo, after):
    def kernel(*refs):
        wgrad_kernel(scale, *refs)

    half = jax.ShapeDtypeStruct((HALF, C), jnp.float32)
    return pl.pallas_call(
        kernel,
        out_shape=[half, half],
        in_specs=[SMEM] * 2 + [VMEM] * 6 + [ANY],
        out_specs=[VMEM] * 2,
        scratch_shapes=scratch(BLK_DEV) + [pltpu.VMEM((2 * HALF, C), jnp.float32)],
        compiler_params=PARAMS,
        name="kernel_gradient",
    )(block_pos, core, own_in, own_grad, *halo, after)


def place(core, near, far):
    return pl.pallas_call(
        place_kernel,
        out_shape=jax.ShapeDtypeStruct((KV * C, C), jnp.float32),
        in_specs=[SMEM] + [VMEM] * 2,
        out_specs=VMEM,
        compiler_params=PARAMS,
        name="place_halves",
    )(core, near, far)


def conv(field, slot, block_pos, own, mask, weights, halo, before, after):
    def kernel(*refs):
        conv_kernel(field, slot, *refs)

    flops = 2 * KV * VOX * C * C
    args = (block_pos, own, mask, weights, *halo)
    extra = ([] if before is None else [before]) + list(after)
    return pl.pallas_call(
        kernel,
        grid=(1,),
        out_shape=[bf16(BLK_DEV, VOX, C), jax.ShapeDtypeStruct((BE, C), jnp.float32)],
        in_specs=[SMEM] + [VMEM] * (len(args) - 1) + [ANY] * len(extra),
        out_specs=[pl.BlockSpec((1, VOX, C), lambda i: (slot, 0, 0)), VMEM],
        scratch_shapes=scratch(1),
        input_output_aliases={} if before is None else {len(args): 0},
        compiler_params=PARAMS,
        cost_estimate=pl.CostEstimate(flops=4 * flops, bytes_accessed=2_000_000, transcendentals=0),
        name=("convolution", "feature_gradient")[field],
    )(*args, *extra)


def small(kernel, outs, args, after=()):
    after = [v for v in after if v is not None]

    def inner(*refs):
        kernel(*refs[:len(args)], *refs[len(args) + len(after):])

    many = [jax.ShapeDtypeStruct((rows, C), jnp.float32) for rows in outs]
    return pl.pallas_call(
        inner,
        out_shape=many,
        in_specs=[VMEM] * len(args) + [ANY] * len(after),
        out_specs=[VMEM] * len(many),
        compiler_params=PARAMS,
        name=kernel.__name__.removesuffix("_kernel"),
    )(*args, *after)


def sum_two_kernel(a_ref, b_ref, out_ref):
    size = a_ref.shape[0]
    total = a_ref[...] + b_ref[...]
    for copy in range(out_ref.shape[0] // size):
        out_ref[copy * size:(copy + 1) * size, :] = total


def copies_kernel(a_ref, out_ref):
    size = a_ref.shape[0]
    for copy in range(out_ref.shape[0] // size):
        out_ref[copy * size:(copy + 1) * size, :] = a_ref[...]


def sum_four_kernel(a_ref, out_ref):
    size = a_ref.shape[0] // 4
    b = [a_ref[s * size:(s + 1) * size, :] for s in range(4)]
    total = (b[0] + b[1]) + (b[2] + b[3])
    for copy in range(out_ref.shape[0] // size):
        out_ref[copy * size:(copy + 1) * size, :] = total


def shifted(value, groups, tiles, up_g, up_t):
    pairs = [
        (g * tiles + t, (g + up_g) * tiles + t + up_t)
        for g in range(groups)
        for t in range(tiles)
        if 0 <= g + up_g < groups and 0 <= t + up_t < tiles
    ]
    return lax.ppermute(value, AXES, pairs)


def across(value, mask):
    count = lax.axis_size("group") * lax.axis_size("tile")
    return lax.ppermute(value, AXES, [(i, i ^ mask) for i in range(count)])


def exchange(value, axis, sets):
    rows = value.shape[0] // 4
    blocks = lax.all_to_all(value.reshape(4, rows, C), axis, 0, 0, axis_index_groups=sets)
    return blocks.reshape(4 * rows, C)


def body(features, occupancy, block_pos, kernel, out_grad):
    groups, tiles = lax.axis_size("group"), lax.axis_size("tile")
    core = (lax.axis_index("tile") & 1).astype(jnp.int32).reshape(1)
    own_in, own_grad, mask, ylo, yhi = prep(block_pos, occupancy, features, out_grad)
    y_from = (shifted(yhi, groups, tiles, 0, 1), shifted(ylo, groups, tiles, 0, -1))
    xlo, xhi = x_faces(block_pos, own_in, own_grad, *y_from)
    x_from = (shifted(xhi, groups, tiles, 1, 0), shifted(xlo, groups, tiles, -1, 0))
    halo = (*y_from, *x_from)
    weights = kernel.reshape(KV * C, C)
    turned, done = turn(weights, xhi)
    scale = 1.0 / math.sqrt(groups * tiles * BLK_DEV * VOX)
    keep, send = wgrad(scale, block_pos, core, own_in, own_grad, halo, done)

    def convolved(field, slot, before, *after):
        return conv(
            field, slot, block_pos, (own_in, own_grad)[field], mask, (weights, turned)[field],
            halo, before, after,
        )

    got = across(send, CORE)
    conv_out, done = convolved(0, 0, None, send)
    value, = small(sum_two_kernel, [HALF], [keep, got], [done])
    value, = small(sum_four_kernel, [4 * CHUNK], [exchange(value, "tile", X_SETS)])
    value, = small(sum_four_kernel, [4 * CHUNK], [exchange(value, "group", Y_SETS)])
    value, = small(sum_four_kernel, [CHUNK], [exchange(value, "tile", Z_LO_SETS)])
    got = across(value, Z_HI_BITS[0])
    conv_out, done = convolved(0, 1, conv_out, value)
    value, = small(sum_two_kernel, [CHUNK], [value, got], [done])
    got = across(value, Z_HI_BITS[1])
    feature_grad, done = convolved(1, 0, None, value)
    value, = small(sum_two_kernel, [4 * CHUNK], [value, got], [done])
    value = exchange(value, "group", Y_SETS)
    value, = small(copies_kernel, [HALF], [value])
    value = exchange(value, "tile", X_SETS)
    got = across(value, CORE)
    feature_grad, done = convolved(1, 1, feature_grad, value)
    total = place(core, value, got)
    return (conv_out, feature_grad, total.reshape(KV, C, C))


def solution(mesh):
    in_specs = (
        P(AXES, None, None),
        P(AXES, None),
        P(AXES),
        P(),
        P(AXES, None, None),
    )
    out_specs = (P(AXES, None, None), P(AXES, None, None), P())
    return jax.shard_map(body, mesh=mesh, in_specs=in_specs, out_specs=out_specs, check_vma=False)
```

time: 708 us -> 141 us (0.20)
  waiting for transfers between devices: 482 us -> 15.3 us
  local copies, waits for them, and re-layouts: 144 us -> 3.24 us
  blocking collectives: 0 us -> 68.6 us
  matrix products: 16.5 us -> 0 us
  Pallas kernels: 0 us -> 15 us
  between operations: 14.3 us -> 0.79 us
  other arithmetic: 10.8 us -> 0 us
    psum x1 -> x0, waiting for transfers between devices: 473 us -> none  [body(): summed = lax.psum(partial_value, ('group', 'tile'))]
    all_to_all x0 -> x5, blocking collectives: none -> 68.6 us  [exchange(): lax.all_to_all(value.reshape(4, rows, C), axis, 0, 0, axis_index_groups=s...]
    while x140 -> x0, local copies, waits for them, and re-layouts: 66.2 us -> none
    reshape x54 -> x0, local copies, waits for them, and re-layouts: 50.7 us -> none  [slot_stack(): return jnp.stack(pieces)]
    slice x8 -> x0, local copies, waits for them, and re-layouts: 20.3 us -> none  [the longest x2 20.2 us: slot_stack(): window[step_x:step_x + BE, step_y:step_y + BE, step_z:step_z + BE]]
    dot_general x8 -> x0, matrix products: 16.5 us -> none  [the longest x2 9.45 us: per_slot(): jnp.einsum('kvc,vd->kcd', stack_in, own_grad, preferred_element_type=jnp....]
    pallas_call x0 -> x16, Pallas kernels: none -> 15 us  [the longest x4 9.56 us: conv(): pl.pallas_call(kernel, grid=(1,), out_shape=[bf16(BLK_DEV, VOX, C), jax.S...]
  transfers between devices with their start and end apart: 9 -> 8, of which waited for: 3 -> 4; matrix products, arithmetic and copies ran while one was open for 1% -> 0% of each run, Pallas kernels for 0% -> 7%
where the time goes in v1:
time: 141 us; the launch traced here: 140 us
  blocking collectives  68.6 us (49%)
  starting transfers between devices  37.2 us (26%)
  waiting for transfers between devices  15.3 us (11%)
  Pallas kernels  15 us (11%)
  local copies, waits for them, and re-layouts  3.24 us (2%)
    all_to_all x5, blocking collectives, exchange(): lax.all_to_all(value.reshape(4, rows, C), axis, 0, 0, axis_index_groups=s...  68.6 us
    ppermute x4, starting transfers between devices, shifted(): return lax.ppermute(value, AXES, pairs)  20 us
    ppermute x4, starting transfers between devices, across(): return lax.ppermute(value, AXES, [(i, i ^ mask) for i in range(count)])  17.2 us
    ppermute x4, waiting for transfers between devices, across(): return lax.ppermute(value, AXES, [(i, i ^ mask) for i in range(count)])  10.5 us
    pallas_call x4, Pallas kernels, conv(): pl.pallas_call(kernel, grid=(1,), out_shape=[bf16(BLK_DEV, VOX, C), jax.S...  9.56 us
    ppermute x4, waiting for transfers between devices, shifted(): return lax.ppermute(value, AXES, pairs)  4.83 us
    unnamed x12, local copies, waits for them, and re-layouts  3.24 us
  transfers between devices with their start and end apart: 8, of which 4 were waited for; matrix products, arithmetic and copies ran while one was open for 0% of the time, Pallas kernels for 7%

profile of v1, /device:TPU:1, one launch (start us, length us, event | category | flops | bytes accessed | tf_op | source)
XLA Modules:
  0.0 140.1 jit_solution(10923165109834399798)
XLA Ops:
  0.6 0.9 copy-done.1
  1.6 0.9 copy-done.2
  4.6 4.5 %collective-permute-start = (bf16[272,128]{1,0:T(8,128)(2,1)S(1)}, bf16[272,128]{1,0:T(8,128)(2,1)S(1)}, u32[]{:S(2)}, u32[]{:S(2)}) collective-permute-start(bf16[272,128]{1,0:T(8,128)(2,1)S(1)} %get-tuple-element.23), channel_id=1, source_target_pairs={{0,1},{1,2},{2,3},{3,4},{4,5},{5,6},{6,7},{7,8},{8,9},{9,10},{10,1... | collective-permute-start | bytes 208904 | tf_op jit(solution)/shard_map/ppermute | solution.py:334
  9.2 5.6 %collective-permute-start.1 = (bf16[272,128]{1,0:T(8,128)(2,1)S(1)}, bf16[272,128]{1,0:T(8,128)(2,1)S(1)}, u32[]{:S(2)}, u32[]{:S(2)}) collective-permute-start(bf16[272,128]{1,0:T(8,128)(2,1)S(1)} %get-tuple-element.24), channel_id=1, source_target_pairs={{1,0},{2,1},{3,2},{4,3},{5,4},{6,5},{7,6},{8,7},{9,8},{10,9},{11,1... | collective-permute-start | bytes 208904 | tf_op jit(solution)/shard_map/ppermute | solution.py:334
  16.2 1.3 collective-permute-start.3
  17.5 8.6 %collective-permute-start.2 = (bf16[368,128]{1,0:T(8,128)(2,1)S(1)}, bf16[368,128]{1,0:T(8,128)(2,1)S(1)}, u32[]{:S(2)}, u32[]{:S(2)}) collective-permute-start(bf16[368,128]{1,0:T(8,128)(2,1)S(1)} %get-tuple-element.26.after_ref), channel_id=1, source_target_pairs={{0,32},{1,33},{2,34},{3,35},{4,36},{5,37},{6,38},{7,39},{8,40},{9,... | collective-permute-start | bytes 282632 | tf_op jit(solution)/shard_map/ppermute | solution.py:334
  26.4 3.9 %collective-permute-done.3.refs_7_ = bf16[368,128]{1,0:T(8,128)(2,1)S(1)} collective-permute-done((bf16[368,128]{1,0:T(8,128)(2,1)S(1)}, bf16[368,128]{1,0:T(8,128)(2,1)S(1)}, u32[]{:S(2)}, u32[]{:S(2)}) %collective-permute-start.3) | collective-permute-done | bytes 94240 | tf_op jit(solution)/shard_map/ppermute | solution.py:334
  30.4 2.2 %kernel_gradient.1 = (f32[1792,128]{1,0:T(8,128)S(1)}, f32[1792,128]{1,0:T(8,128)S(1)}) custom-call(s32[2]{0:T(128)S(1)} %copy-done.4, s32[1]{0:T(128)} %bitcast.1.refs_1_.core_ref, bf16[1024,128]{1,0:T(8,128)(2,1)S(1)} %get-tuple-element.21.in_ref.refs_2_.refs_1_, bf16[1024,128]{1,0:T(8,128)(2,1)S(1)} %get-tuple-element.25.g_ref.refs_3_.refs_1_, ...), custom_call_target="tpu_custom_call" | custom-call | tf_op jit(solution)/shard_map/kernel_gradient/pallas_call | solution.py:246
  32.5 2.4 %collective-permute-start.4 = (f32[1792,128]{1,0:T(8,128)S(1)}, f32[1792,128]{1,0:T(8,128)S(1)}, u32[]{:S(2)}, u32[]{:S(2)}) collective-permute-start(f32[1792,128]{1,0:T(8,128)S(1)} %get-tuple-element.29.refs_8_), channel_id=1, source_target_pairs={{0,1},{1,0},{2,3},{3,2},{4,5},{5,4},{6,7},{7,6},{8,9},{9,8},{10,11... | collective-permute-start | bytes 2752520 | tf_op jit(solution)/shard_map/ppermute | solution.py:339
  35.0 2.4 %convolution.2 = (bf16[2,512,128]{2,1,0:T(8,128)(2,1)}, f32[8,128]{1,0:T(8,128)S(1)}) custom-call(s32[2]{0:T(128)S(1)} %copy-done.4, bf16[1024,128]{1,0:T(8,128)(2,1)S(1)} %get-tuple-element.21.in_ref.refs_2_.refs_1_, bf16[1024,128]{1,0:T(8,128)(2,1)S(1)} %get-tuple-element.22.refs_2_, bf16[3456,128]{1,0:T(8,128)(2,1)S(1)} %bitcast.26, ...), custom_call_target="tpu_custom_call" | custom-call | flops 1811939328 | bytes 2000000 | tf_op jit(solution)/shard_map/convolution/pallas_call | solution.py:275
  37.5 17.9 %all_to_all.25 = f32[4,448,128]{2,1,0:T(8,128)S(1)} all-to-all(f32[4,448,128]{2,1,0:T(8,128)S(1)} %bitcast.18), channel_id=1, replica_groups={{0,2,4,6},{1,3,5,7},{8,10,12,14},{9,11,13,15},{16,18,20,22},{17,19,21,2..., dimensions={0} | all-to-all | bytes 1835008 | tf_op jit(solution)/shard_map/all_to_all | solution.py:344
  55.4 21.4 %all_to_all.26 = f32[4,112,128]{2,1,0:T(8,128)S(1)} all-to-all(f32[4,112,128]{2,1,0:T(8,128)S(1)} %bitcast.23), channel_id=1, replica_groups={{0,128,256,384},{32,160,288,416},{64,192,320,448},{96,224,352,480},{1,1..., dimensions={0} | all-to-all | bytes 458752 | tf_op jit(solution)/shard_map/all_to_all | solution.py:344
  76.9 10.1 %all_to_all.27 = f32[4,112,128]{2,1,0:T(8,128)S(1)} all-to-all(f32[4,112,128]{2,1,0:T(8,128)S(1)} %bitcast.20), channel_id=1, replica_groups={{0,8,16,24},{1,9,17,25},{2,10,18,26},{3,11,19,27},{4,12,20,28},{5,13,21..., dimensions={0} | all-to-all | bytes 458752 | tf_op jit(solution)/shard_map/all_to_all | solution.py:344
  86.9 1.9 %collective-permute-start.5 = (f32[112,128]{1,0:T(8,128)S(1)}, f32[112,128]{1,0:T(8,128)S(1)}, u32[]{:S(2)}, u32[]{:S(2)}) collective-permute-start(f32[112,128]{1,0:T(8,128)S(1)} %sum_four.5.refs_9_.refs_0_), channel_id=1, source_target_pairs={{0,32},{1,33},{2,34},{3,35},{4,36},{5,37},{6,38},{7,39},{8,40},{9,... | collective-permute-start | bytes 172040 | tf_op jit(solution)/shard_map/ppermute | solution.py:339
  88.9 2.4 %convolution.3 = (bf16[2,512,128]{2,1,0:T(8,128)(2,1)}, f32[8,128]{1,0:T(8,128)S(1)}) custom-call(s32[2]{0:T(128)S(1)} %copy-done.4, bf16[1024,128]{1,0:T(8,128)(2,1)S(1)} %get-tuple-element.21.in_ref.refs_2_.refs_1_, bf16[1024,128]{1,0:T(8,128)(2,1)S(1)} %get-tuple-element.22.refs_2_, ...), custom_call_target="tpu_custom_call", output_to_operand_aliasing={{0}: (8, {})} | custom-call | flops 1811939328 | bytes 2000000 | tf_op jit(solution)/shard_map/convolution/pallas_call | solution.py:275
  91.3 6.4 %collective-permute-done.5.refs_1_ = f32[112,128]{1,0:T(8,128)S(1)} collective-permute-done((f32[112,128]{1,0:T(8,128)S(1)}, f32[112,128]{1,0:T(8,128)S(1)}, u32[]{:S(2)}, u32[]{:S(2)}) %collective-permute-start.5) | collective-permute-done | bytes 57376 | tf_op jit(solution)/shard_map/ppermute | solution.py:339
  97.6 2.3 %collective-permute-start.6 = (f32[112,128]{1,0:T(8,128)S(1)}, f32[112,128]{1,0:T(8,128)S(1)}, u32[]{:S(2)}, u32[]{:S(2)}) collective-permute-start(f32[112,128]{1,0:T(8,128)S(1)} %sum_two.4.refs_8_.refs_0_), channel_id=1, source_target_pairs={{0,96},{1,97},{2,98},{3,99},{4,100},{5,101},{6,102},{7,103},{8,104... | collective-permute-start | bytes 172040 | tf_op jit(solution)/shard_map/ppermute | solution.py:339
  99.9 2.4 %feature_gradient.2 = (bf16[2,512,128]{2,1,0:T(8,128)(2,1)}, f32[8,128]{1,0:T(8,128)S(1)}) custom-call(s32[2]{0:T(128)S(1)} %copy-done.4, bf16[1024,128]{1,0:T(8,128)(2,1)S(1)} %get-tuple-element.25.g_ref.refs_3_.refs_1_, bf16[1024,128]{1,0:T(8,128)(2,1)S(1)} %get-tuple-element.22.refs_2_, bf16[3456,128]{1,0:T(8,128)(2,1)S(1)} %get-tuple-element.34.refs_3_, ...), custom_call_target="tpu_custom_call" | custom-call | flops 1811939328 | bytes 2000000 | tf_op jit(solution)/shard_map/feature_gradient/pallas_call | solution.py:275
  102.3 4.1 %collective-permute-done.6.refs_1_ = f32[112,128]{1,0:T(8,128)S(1)} collective-permute-done((f32[112,128]{1,0:T(8,128)S(1)}, f32[112,128]{1,0:T(8,128)S(1)}, u32[]{:S(2)}, u32[]{:S(2)}) %collective-permute-start.6) | collective-permute-done | bytes 57376 | tf_op jit(solution)/shard_map/ppermute | solution.py:339
  106.5 7.7 %all_to_all.28 = f32[4,112,128]{2,1,0:T(8,128)S(1)} all-to-all(f32[4,112,128]{2,1,0:T(8,128)S(1)} %bitcast.21), channel_id=1, replica_groups={{0,128,256,384},{32,160,288,416},{64,192,320,448},{96,224,352,480},{1,1..., dimensions={0} | all-to-all | bytes 458752 | tf_op jit(solution)/shard_map/all_to_all | solution.py:344
  114.3 11.5 %all_to_all.29 = f32[4,448,128]{2,1,0:T(8,128)S(1)} all-to-all(f32[4,448,128]{2,1,0:T(8,128)S(1)} %bitcast.14), channel_id=1, replica_groups={{0,2,4,6},{1,3,5,7},{8,10,12,14},{9,11,13,15},{16,18,20,22},{17,19,21,2..., dimensions={0} | all-to-all | bytes 1835008 | tf_op jit(solution)/shard_map/all_to_all | solution.py:344
  125.7 10.6 %collective-permute-start.7 = (f32[1792,128]{1,0:T(8,128)S(1)}, f32[1792,128]{1,0:T(8,128)S(1)}, u32[]{:S(2)}, u32[]{:S(2)}) collective-permute-start(f32[1792,128]{1,0:T(8,128)S(1)} %bitcast.15), channel_id=1, source_target_pairs={{0,1},{1,0},{2,3},{3,2},{4,5},{5,4},{6,7},{7,6},{8,9},{9,8},{10,11... | collective-permute-start | bytes 2752520 | tf_op jit(solution)/shard_map/ppermute | solution.py:339
  136.3 2.4 %feature_gradient.3 = (bf16[2,512,128]{2,1,0:T(8,128)(2,1)}, f32[8,128]{1,0:T(8,128)}) custom-call(s32[2]{0:T(128)S(1)} %copy-done.4, bf16[1024,128]{1,0:T(8,128)(2,1)S(1)} %get-tuple-element.25.g_ref.refs_3_.refs_1_, bf16[1024,128]{1,0:T(8,128)(2,1)S(1)} %get-tuple-element.22.refs_2_, ...), custom_call_target="tpu_custom_call", output_to_operand_aliasing={{0}: (8, {})} | custom-call | flops 1811939328 | bytes 2000000 | tf_op jit(solution)/shard_map/feature_gradient/pallas_call | solution.py:275
  138.8 1.4 place_halves.1
  (25 shorter events, 4.1 us)
Async XLA Ops:
  0.6 1.0 copy-start.1
  1.6 0.9 copy-start.2
  2.5 0.7 copy-start.3
  3.2 0.7 copy-start.5
  3.9 22.2 %copy-start = (bf16[27,128,128]{2,1,0:T(8,128)(2,1)S(1)}, bf16[27,128,128]{2,1,0:T(8,128)(2,1)}, u32[]{:S(2)}) copy-start(bf16[27,128,128]{2,1,0:T(8,128)(2,1)} %param.8) | copy-start | bytes 2654212
  3.9 26.5 %copy-start.4 = (s32[2]{0:T(128)S(1)}, s32[2]{0:T(128)}, u32[]{:S(2)}) copy-start(s32[2]{0:T(128)} %refs_0_.9) | copy-start | bytes 28
  4.6 10.1 %collective-permute-start = (bf16[272,128]{1,0:T(8,128)(2,1)S(1)}, bf16[272,128]{1,0:T(8,128)(2,1)S(1)}, u32[]{:S(2)}, u32[]{:S(2)}) collective-permute-start(bf16[272,128]{1,0:T(8,128)(2,1)S(1)} %get-tuple-element.23), channel_id=1, source_target_pairs={{0,1},{1,2},{2,3},{3,4},{4,5},{5,6},{6,7},{7,8},{8,9},{9,10},{10,1... | collective-permute-start | bytes 208904 | tf_op jit(solution)/shard_map/ppermute | solution.py:334
  9.2 6.5 %collective-permute-start.1 = (bf16[272,128]{1,0:T(8,128)(2,1)S(1)}, bf16[272,128]{1,0:T(8,128)(2,1)S(1)}, u32[]{:S(2)}, u32[]{:S(2)}) collective-permute-start(bf16[272,128]{1,0:T(8,128)(2,1)S(1)} %get-tuple-element.24), channel_id=1, source_target_pairs={{1,0},{2,1},{3,2},{4,3},{5,4},{6,5},{7,6},{8,7},{9,8},{10,9},{11,1... | collective-permute-start | bytes 208904 | tf_op jit(solution)/shard_map/ppermute | solution.py:334
  16.2 14.2 %collective-permute-start.3 = (bf16[368,128]{1,0:T(8,128)(2,1)S(1)}, bf16[368,128]{1,0:T(8,128)(2,1)S(1)}, u32[]{:S(2)}, u32[]{:S(2)}) collective-permute-start(bf16[368,128]{1,0:T(8,128)(2,1)S(1)} %get-tuple-element.27), channel_id=1, source_target_pairs={{32,0},{33,1},{34,2},{35,3},{36,4},{37,5},{38,6},{39,7},{40,8},{41... | collective-permute-start | bytes 282632 | tf_op jit(solution)/shard_map/ppermute | solution.py:334
  17.5 12.9 %collective-permute-start.2 = (bf16[368,128]{1,0:T(8,128)(2,1)S(1)}, bf16[368,128]{1,0:T(8,128)(2,1)S(1)}, u32[]{:S(2)}, u32[]{:S(2)}) collective-permute-start(bf16[368,128]{1,0:T(8,128)(2,1)S(1)} %get-tuple-element.26.after_ref), channel_id=1, source_target_pairs={{0,32},{1,33},{2,34},{3,35},{4,36},{5,37},{6,38},{7,39},{8,40},{9,... | collective-permute-start | bytes 282632 | tf_op jit(solution)/shard_map/ppermute | solution.py:334
  32.5 4.8 %collective-permute-start.4 = (f32[1792,128]{1,0:T(8,128)S(1)}, f32[1792,128]{1,0:T(8,128)S(1)}, u32[]{:S(2)}, u32[]{:S(2)}) collective-permute-start(f32[1792,128]{1,0:T(8,128)S(1)} %get-tuple-element.29.refs_8_), channel_id=1, source_target_pairs={{0,1},{1,0},{2,3},{3,2},{4,5},{5,4},{6,7},{7,6},{8,9},{9,8},{10,11... | collective-permute-start | bytes 2752520 | tf_op jit(solution)/shard_map/ppermute | solution.py:339
  86.9 10.7 %collective-permute-start.5 = (f32[112,128]{1,0:T(8,128)S(1)}, f32[112,128]{1,0:T(8,128)S(1)}, u32[]{:S(2)}, u32[]{:S(2)}) collective-permute-start(f32[112,128]{1,0:T(8,128)S(1)} %sum_four.5.refs_9_.refs_0_), channel_id=1, source_target_pairs={{0,32},{1,33},{2,34},{3,35},{4,36},{5,37},{6,38},{7,39},{8,40},{9,... | collective-permute-start | bytes 172040 | tf_op jit(solution)/shard_map/ppermute | solution.py:339
  97.6 8.8 %collective-permute-start.6 = (f32[112,128]{1,0:T(8,128)S(1)}, f32[112,128]{1,0:T(8,128)S(1)}, u32[]{:S(2)}, u32[]{:S(2)}) collective-permute-start(f32[112,128]{1,0:T(8,128)S(1)} %sum_two.4.refs_8_.refs_0_), channel_id=1, source_target_pairs={{0,96},{1,97},{2,98},{3,99},{4,100},{5,101},{6,102},{7,103},{8,104... | collective-permute-start | bytes 172040 | tf_op jit(solution)/shard_map/ppermute | solution.py:339
  125.7 13.0 %collective-permute-start.7 = (f32[1792,128]{1,0:T(8,128)S(1)}, f32[1792,128]{1,0:T(8,128)S(1)}, u32[]{:S(2)}, u32[]{:S(2)}) collective-permute-start(f32[1792,128]{1,0:T(8,128)S(1)} %bitcast.15), channel_id=1, source_target_pairs={{0,1},{1,0},{2,3},{3,2},{4,5},{5,4},{6,7},{7,6},{8,9},{9,8},{10,11... | collective-permute-start | bytes 2752520 | tf_op jit(solution)/shard_map/ppermute | solution.py:339

commit v2 on v1

--- a/solution.py
+++ b/solution.py
@@ -20,11 +20,15 @@
 EDGE = 2 * BLK_DEV * BE
 TAG = 16
 CHUNK = 112
+CODED = CHUNK + TAG
+STEPS = 32000.0
 HALF = 16 * CHUNK
 CORE = 1
-X_SETS = [[z * 8 + x * 2 + core for x in range(4)] for z in range(4) for core in range(2)]
+XY_SETS = [
+    [(y * 4 + z_hi) * 32 + z_lo * 8 + x * 2 + core for y in range(4) for x in range(4)]
+    for z_hi in range(4) for z_lo in range(4) for core in range(2)
+]
 Z_LO_SETS = [[z * 8 + x * 2 + core for z in range(4)] for x in range(4) for core in range(2)]
-Y_SETS = [[y * 4 + z for y in range(4)] for z in range(4)]
 Z_HI_BITS = (32, 96)
 
 
@@ -34,9 +38,17 @@
     ).astype(jnp.bfloat16)
 
 
-def prep_kernel(pos_ref, occ_ref, feat_ref, grad_ref, in_ref, g_ref, mask_ref, ylo_ref, yhi_ref):
+def prep_kernel(*refs):
+    sources, (in_ref, g_ref, mask_ref, xlo_ref, xhi_ref), held, sems = refs[:4], refs[4:9], refs[9:13], refs[13]
+    copies = [pltpu.make_async_copy(src, dst, sems.at[i]) for i, (src, dst) in enumerate(zip(sources, held))]
+    for copy in copies:
+        copy.start()
+    for copy in copies:
+        copy.wait()
+    pos_ref, occ_ref, feat_ref, grad_ref = held
     occ = occ_ref[...].astype(jnp.float32)
-    for face in (ylo_ref, yhi_ref):
+    layer = BE * BE
+    for face in (xlo_ref, xhi_ref):
         face[FACE:FACE + TAG, :] = tags(pos_ref)
     for s in range(BLK_DEV):
         live = (pos_ref[s] >= 0).astype(jnp.float32)
@@ -45,36 +57,35 @@
         ])
         mask_ref[s * VOX:(s + 1) * VOX, :] = mask.astype(jnp.bfloat16)
         for field, (src, dst) in enumerate(((feat_ref, in_ref), (grad_ref, g_ref))):
-            value = jnp.where(mask > 0, src[s].astype(jnp.float32), 0.0)
-            dst[s * VOX:(s + 1) * VOX, :] = value.astype(jnp.bfloat16)
-            cube = value.reshape(BE, BE, BE, C)
-            at = (field * BLK_DEV + s) * BE * BE
-            here = slice(at, at + BE * BE)
-            ylo_ref[here, :] = cube[:, 0].reshape(BE * BE, C).astype(jnp.bfloat16)
-            yhi_ref[here, :] = cube[:, BE - 1].reshape(BE * BE, C).astype(jnp.bfloat16)
-
-
-def x_faces_kernel(pos_ref, in_ref, g_ref, low_ref, high_ref, xlo_ref, xhi_ref):
-    for x, out in ((0, xlo_ref), (BE - 1, xhi_ref)):
-        for field, own in enumerate((in_ref, g_ref)):
-            for s in range(BLK_DEV):
-                at = (field * BLK_DEV + s) * BE * BE
-                first = s * VOX + x * BE * BE
-                out[at:at + BE * BE, :] = own[first:first + BE * BE, :]
-        for side, ref in enumerate((low_ref, high_ref)):
-            edge = [
-                ref[n * BE * BE:(n + 1) * BE * BE, :].astype(jnp.float32)[x * BE:(x + 1) * BE]
-                for n in range(2 * BLK_DEV)
-            ]
+            value = jnp.where(mask > 0, src[s].astype(jnp.float32), 0.0).astype(jnp.bfloat16)
+            dst[s * VOX:(s + 1) * VOX, :] = value
+            at = (field * BLK_DEV + s) * layer
+            xlo_ref[at:at + layer, :] = value[:layer]
+            xhi_ref[at:at + layer, :] = value[VOX - layer:]
+
+
+def y_faces_kernel(pos_ref, in_ref, g_ref, low_ref, high_ref, ylo_ref, yhi_ref):
+    layer = BE * BE
+    for field, own in enumerate((in_ref, g_ref)):
+        for s in range(BLK_DEV):
+            cube = own[s * VOX:(s + 1) * VOX, :].astype(jnp.float32).reshape(BE, BE, BE, C)
+            at = (field * BLK_DEV + s) * layer
+            for y, out in ((0, ylo_ref), (BE - 1, yhi_ref)):
+                out[at:at + layer, :] = cube[:, y].reshape(layer, C).astype(jnp.bfloat16)
+    for side, ref in enumerate((low_ref, high_ref)):
+        faces = [ref[n * layer:(n + 1) * layer, :].astype(jnp.float32) for n in range(2 * BLK_DEV)]
+        for y, out in ((0, ylo_ref), (BE - 1, yhi_ref)):
+            edge = [face[y * BE:(y + 1) * BE] for face in faces]
             at = FACE + side * EDGE
             out[at:at + EDGE, :] = jnp.concatenate(edge).astype(jnp.bfloat16)
             at = FACE + 2 * EDGE + side * TAG
             out[at:at + TAG, :] = ref[FACE:FACE + TAG, :]
-        at = FACE + 2 * EDGE + 2 * TAG
+    at = FACE + 2 * EDGE + 2 * TAG
+    for out in (ylo_ref, yhi_ref):
         out[at:at + TAG, :] = tags(pos_ref)
 
 
-def fill_windows(field, slots, pos_ref, own_ref, y_from, x_from, z_ref, a_ref):
+def fill_windows(field, slots, pos_ref, own_ref, x_from, y_from, z_ref, a_ref):
     row = lax.broadcasted_iota(jnp.int32, (BE, C), 0)
     first = field * BLK_DEV
     regions = []
@@ -94,14 +105,14 @@
     inside = slice(1, BE + 1)
     ends = (slice(0, 1), slice(WIN - 1, WIN))
     regions.append((inside, inside, own, own_tags))
+    for ref, end in zip(x_from, ends):
+        regions.append((end, inside, face_of(ref, (1, BE, BE, C)), tags_of(ref, FACE)))
     for ref, end in zip(y_from, ends):
-        regions.append((inside, end, face_of(ref, (BE, 1, BE, C)), tags_of(ref, FACE)))
-    for ref, end in zip(x_from, ends):
-        regions.append((end, inside, face_of(ref, (1, BE, BE, C)), tags_of(ref, FACE + 2 * EDGE + 2 * TAG)))
+        regions.append((inside, end, face_of(ref, (BE, 1, BE, C)), tags_of(ref, FACE + 2 * EDGE + 2 * TAG)))
         for side, other in enumerate(ends):
             edge = ref[FACE + side * EDGE:FACE + (side + 1) * EDGE, :].astype(jnp.float32)
             data = [edge[n * BE:(n + 1) * BE].reshape(1, 1, BE, C) for n in range(first, first + BLK_DEV)]
-            regions.append((end, other, data, tags_of(ref, FACE + 2 * EDGE + side * TAG)))
+            regions.append((other, end, data, tags_of(ref, FACE + 2 * EDGE + side * TAG)))
 
     for i, s in enumerate(slots):
         here = pos_ref[s].astype(jnp.float32)
@@ -151,11 +162,28 @@
     send_ref[...] = total_ref[pl.ds(pl.multiple_of((1 - core) * HALF, HALF), HALF), :]
 
 
+def coded(value):
+    top = jnp.maximum(jnp.max(jnp.abs(value), axis=0, keepdims=True), 2.0 ** -120)
+    exponent = jnp.floor(jnp.log2(top)) + 1.0
+    steps = jnp.floor(value * (jnp.exp2(-exponent) * STEPS) + 0.5)
+    last = jnp.broadcast_to(exponent, (TAG, C))
+    return jnp.concatenate([steps, last]).astype(jnp.int32).astype(jnp.int16)
+
+
+def decoded(ref, block=0):
+    code = ref[block * CODED:(block + 1) * CODED, :].astype(jnp.int32).astype(jnp.float32)
+    return code[:CHUNK] * (jnp.exp2(code[CHUNK:CHUNK + 1]) * (1.0 / STEPS))
+
+
 def place_kernel(core_ref, near_ref, far_ref, out_ref):
     first = core_ref[0] == 0
-    rest = KV * C - HALF
-    out_ref[0:HALF, :] = jnp.where(first, near_ref[...], far_ref[...])
-    out_ref[HALF:KV * C, :] = jnp.where(first, far_ref[0:rest, :], near_ref[0:rest, :])
+    for block in range(16):
+        near, far = decoded(near_ref, block), decoded(far_ref, block)
+        at = block * CHUNK
+        out_ref[at:at + CHUNK, :] = jnp.where(first, near, far)
+        size = min(CHUNK, KV * C - HALF - at)
+        if size > 0:
+            out_ref[HALF + at:HALF + at + size, :] = jnp.where(first, far, near)[:size]
 
 
 def turn_kernel(w_ref, out_ref, done_ref):
@@ -190,30 +218,33 @@
     return jax.ShapeDtypeStruct(shape, jnp.bfloat16)
 
 
-def whole(*shape):
-    return pl.BlockSpec(shape, lambda i: (0,) * len(shape))
-
-
 def prep(block_pos, occupancy, features, out_grad):
+    field = pltpu.VMEM((BLK_DEV, VOX, C), jnp.bfloat16)
     return pl.pallas_call(
         prep_kernel,
-        grid=(1,),
         out_shape=[bf16(BLK_DEV * VOX, C)] * 3 + [bf16(FACE + TAG, C)] * 2,
-        in_specs=[SMEM, whole(BLK_DEV, VOX)] + [whole(BLK_DEV, VOX, C)] * 2,
+        in_specs=[pl.BlockSpec(memory_space=pltpu.HBM)] * 4,
         out_specs=[VMEM] * 5,
+        scratch_shapes=[
+            pltpu.SMEM((BLK_DEV,), jnp.int32),
+            pltpu.VMEM((BLK_DEV, VOX), jnp.int32),
+            field,
+            field,
+            pltpu.SemaphoreType.DMA((4,)),
+        ],
         compiler_params=PARAMS,
         name="mask_and_faces",
     )(block_pos, occupancy, features, out_grad)
 
 
-def x_faces(block_pos, own_in, own_grad, low, high):
-    return pl.pallas_call(
-        x_faces_kernel,
+def y_faces(block_pos, own_in, own_grad, low, high):
+    return pl.pallas_call(
+        y_faces_kernel,
         out_shape=[bf16(FACE + 2 * EDGE + 3 * TAG, C)] * 2,
         in_specs=[SMEM] + [VMEM] * 4,
         out_specs=[VMEM] * 2,
         compiler_params=PARAMS,
-        name="x_faces",
+        name="y_faces",
     )(block_pos, own_in, own_grad, low, high)
 
 
@@ -292,7 +323,7 @@
     def inner(*refs):
         kernel(*refs[:len(args)], *refs[len(args) + len(after):])
 
-    many = [jax.ShapeDtypeStruct((rows, C), jnp.float32) for rows in outs]
+    many = [jax.ShapeDtypeStruct((rows, C), jnp.int16) for rows in outs]
     return pl.pallas_call(
         inner,
         out_shape=many,
@@ -303,25 +334,20 @@
     )(*args, *after)
 
 
-def sum_two_kernel(a_ref, b_ref, out_ref):
-    size = a_ref.shape[0]
-    total = a_ref[...] + b_ref[...]
-    for copy in range(out_ref.shape[0] // size):
-        out_ref[copy * size:(copy + 1) * size, :] = total
-
-
-def copies_kernel(a_ref, out_ref):
-    size = a_ref.shape[0]
-    for copy in range(out_ref.shape[0] // size):
-        out_ref[copy * size:(copy + 1) * size, :] = a_ref[...]
-
-
-def sum_four_kernel(a_ref, out_ref):
-    size = a_ref.shape[0] // 4
-    b = [a_ref[s * size:(s + 1) * size, :] for s in range(4)]
-    total = (b[0] + b[1]) + (b[2] + b[3])
-    for copy in range(out_ref.shape[0] // size):
-        out_ref[copy * size:(copy + 1) * size, :] = total
+def sum_halves_kernel(a_ref, b_ref, out_ref):
+    for block in range(HALF // CHUNK):
+        rows = slice(block * CHUNK, (block + 1) * CHUNK)
+        out_ref[block * CODED:(block + 1) * CODED, :] = coded(a_ref[rows, :] + b_ref[rows, :])
+
+
+def sum_blocks_kernel(*refs):
+    *in_refs, out_ref = refs
+    b = [decoded(ref, block) for ref in in_refs for block in range(ref.shape[0] // CODED)]
+    while len(b) > 1:
+        b = [b[i] + b[i + 1] for i in range(0, len(b), 2)]
+    code = coded(b[0])
+    for copy in range(out_ref.shape[0] // CODED):
+        out_ref[copy * CODED:(copy + 1) * CODED, :] = code
 
 
 def shifted(value, groups, tiles, up_g, up_t):
@@ -340,21 +366,21 @@
 
 
 def exchange(value, axis, sets):
-    rows = value.shape[0] // 4
-    blocks = lax.all_to_all(value.reshape(4, rows, C), axis, 0, 0, axis_index_groups=sets)
-    return blocks.reshape(4 * rows, C)
+    count = len(sets[0])
+    blocks = lax.all_to_all(value.reshape(count, -1, C), axis, 0, 0, axis_index_groups=sets)
+    return blocks.reshape(-1, C)
 
 
 def body(features, occupancy, block_pos, kernel, out_grad):
     groups, tiles = lax.axis_size("group"), lax.axis_size("tile")
     core = (lax.axis_index("tile") & 1).astype(jnp.int32).reshape(1)
-    own_in, own_grad, mask, ylo, yhi = prep(block_pos, occupancy, features, out_grad)
+    own_in, own_grad, mask, xlo, xhi = prep(block_pos, occupancy, features, out_grad)
+    x_from = (shifted(xhi, groups, tiles, 1, 0), shifted(xlo, groups, tiles, -1, 0))
+    ylo, yhi = y_faces(block_pos, own_in, own_grad, *x_from)
     y_from = (shifted(yhi, groups, tiles, 0, 1), shifted(ylo, groups, tiles, 0, -1))
-    xlo, xhi = x_faces(block_pos, own_in, own_grad, *y_from)
-    x_from = (shifted(xhi, groups, tiles, 1, 0), shifted(xlo, groups, tiles, -1, 0))
-    halo = (*y_from, *x_from)
+    halo = (*x_from, *y_from)
     weights = kernel.reshape(KV * C, C)
-    turned, done = turn(weights, xhi)
+    turned, done = turn(weights, yhi)
     scale = 1.0 / math.sqrt(groups * tiles * BLK_DEV * VOX)
     keep, send = wgrad(scale, block_pos, core, own_in, own_grad, halo, done)
 
@@ -366,19 +392,16 @@
 
     got = across(send, CORE)
     conv_out, done = convolved(0, 0, None, send)
-    value, = small(sum_two_kernel, [HALF], [keep, got], [done])
-    value, = small(sum_four_kernel, [4 * CHUNK], [exchange(value, "tile", X_SETS)])
-    value, = small(sum_four_kernel, [4 * CHUNK], [exchange(value, "group", Y_SETS)])
-    value, = small(sum_four_kernel, [CHUNK], [exchange(value, "tile", Z_LO_SETS)])
+    value, = small(sum_halves_kernel, [16 * CODED], [keep, got], [done])
+    value, = small(sum_blocks_kernel, [4 * CODED], [exchange(value, AXES, XY_SETS)])
+    value, = small(sum_blocks_kernel, [CODED], [exchange(value, "tile", Z_LO_SETS)])
     got = across(value, Z_HI_BITS[0])
     conv_out, done = convolved(0, 1, conv_out, value)
-    value, = small(sum_two_kernel, [CHUNK], [value, got], [done])
+    value, = small(sum_blocks_kernel, [CODED], [value, got], [done])
     got = across(value, Z_HI_BITS[1])
     feature_grad, done = convolved(1, 0, None, value)
-    value, = small(sum_two_kernel, [4 * CHUNK], [value, got], [done])
-    value = exchange(value, "group", Y_SETS)
-    value, = small(copies_kernel, [HALF], [value])
-    value = exchange(value, "tile", X_SETS)
+    value, = small(sum_blocks_kernel, [16 * CODED], [value, got], [done])
+    value = exchange(value, AXES, XY_SETS)
     got = across(value, CORE)
     feature_grad, done = convolved(1, 1, feature_grad, value)
     total = place(core, value, got)

time: 141 us -> 114 us (0.81)
  blocking collectives: 68.6 us -> 40.7 us
  waiting for transfers between devices: 15.3 us -> 17.8 us
  starting transfers between devices: 37.2 us -> 35.5 us
    all_to_all x5 -> x3, blocking collectives: 68.6 us -> 40.7 us  [exchange(): lax.all_to_all(value.reshape(count, -1, C), axis, 0, 0, axis_index_groups...]
    ppermute x4, waiting for transfers between devices: 4.83 us -> 15.4 us  [shifted(): return lax.ppermute(value, AXES, pairs)]
    ppermute x4, waiting for transfers between devices: 10.5 us -> 2.45 us  [across(): return lax.ppermute(value, AXES, [(i, i ^ mask) for i in range(count)])]
    ppermute x4, starting transfers between devices: 20 us -> 16.8 us  [shifted(): return lax.ppermute(value, AXES, pairs)]
    ppermute x4, starting transfers between devices: 17.2 us -> 18.7 us  [across(): return lax.ppermute(value, AXES, [(i, i ^ mask) for i in range(count)])]
  transfers between devices with their start and end apart: 8 -> 8, of which waited for: 4 -> 4; matrix products, arithmetic and copies ran while one was open for 0% -> 0% of each run, Pallas kernels for 7% -> 9%
where the time goes in v2:
time: 114 us
  blocking collectives  40.7 us (36%)
  starting transfers between devices  35.5 us (31%)
  waiting for transfers between devices  17.8 us (16%)
  Pallas kernels  15.6 us (14%)
  local copies, waits for them, and re-layouts  3.24 us (3%)
    all_to_all x3, blocking collectives, exchange(): lax.all_to_all(value.reshape(count, -1, C), axis, 0, 0, axis_index_groups...  40.7 us
    ppermute x4, starting transfers between devices, across(): return lax.ppermute(value, AXES, [(i, i ^ mask) for i in range(count)])  18.7 us
    ppermute x4, starting transfers between devices, shifted(): return lax.ppermute(value, AXES, pairs)  16.8 us
    ppermute x4, waiting for transfers between devices, shifted(): return lax.ppermute(value, AXES, pairs)  15.4 us
    pallas_call x4, Pallas kernels, conv(): pl.pallas_call(kernel, grid=(1,), out_shape=[bf16(BLK_DEV, VOX, C), jax.S...  9.56 us
    unnamed x12, local copies, waits for them, and re-layouts  3.24 us
    ppermute x4, waiting for transfers between devices, across(): return lax.ppermute(value, AXES, [(i, i ^ mask) for i in range(count)])  2.45 us
  transfers between devices with their start and end apart: 8, of which 4 were waited for; matrix products, arithmetic and copies ran while one was open for 0% of the time, Pallas kernels for 9%

profile of v2, /device:TPU:1, one launch (start us, length us, event | category | flops | bytes accessed | tf_op | source)
XLA Modules:
  0.0 113.7 jit_solution(16714623261033231318)
XLA Ops:
  0.6 0.9 copy-done.1
  1.6 0.9 copy-done.2
  3.2 0.7 copy-done.5
  3.9 0.8 mask_and_faces.1
  4.7 9.6 %collective-permute-start = (bf16[272,128]{1,0:T(8,128)(2,1)S(1)}, bf16[272,128]{1,0:T(8,128)(2,1)S(1)}, u32[]{:S(2)}, u32[]{:S(2)}) collective-permute-start(bf16[272,128]{1,0:T(8,128)(2,1)S(1)} %get-tuple-element.23), channel_id=1, source_target_pairs={{0,32},{1,33},{2,34},{3,35},{4,36},{5,37},{6,38},{7,39},{8,40},{9,... | collective-permute-start | bytes 208904 | tf_op jit(solution)/shard_map/ppermute | solution.py:360
  14.3 1.3 %collective-permute-start.1 = (bf16[272,128]{1,0:T(8,128)(2,1)S(1)}, bf16[272,128]{1,0:T(8,128)(2,1)S(1)}, u32[]{:S(2)}, u32[]{:S(2)}) collective-permute-start(bf16[272,128]{1,0:T(8,128)(2,1)S(1)} %get-tuple-element.24), channel_id=1, source_target_pairs={{32,0},{33,1},{34,2},{35,3},{36,4},{37,5},{38,6},{39,7},{40,8},{41... | collective-permute-start | bytes 208904 | tf_op jit(solution)/shard_map/ppermute | solution.py:360
  15.7 14.1 %collective-permute-done.1.high_ref.refs_5_ = bf16[272,128]{1,0:T(8,128)(2,1)S(1)} collective-permute-done((bf16[272,128]{1,0:T(8,128)(2,1)S(1)}, bf16[272,128]{1,0:T(8,128)(2,1)S(1)}, u32[]{:S(2)}, u32[]{:S(2)}) %collective-permute-start.1) | collective-permute-done | bytes 69664 | tf_op jit(solution)/shard_map/ppermute | solution.py:360
  30.4 2.9 %collective-permute-start.3 = (bf16[368,128]{1,0:T(8,128)(2,1)S(1)}, bf16[368,128]{1,0:T(8,128)(2,1)S(1)}, u32[]{:S(2)}, u32[]{:S(2)}) collective-permute-start(bf16[368,128]{1,0:T(8,128)(2,1)S(1)} %get-tuple-element.27), channel_id=1, source_target_pairs={{1,0},{2,1},{3,2},{4,3},{5,4},{6,5},{7,6},{8,7},{9,8},{10,9},{11,1... | collective-permute-start | bytes 282632 | tf_op jit(solution)/shard_map/ppermute | solution.py:360
  33.3 3.0 %collective-permute-start.2 = (bf16[368,128]{1,0:T(8,128)(2,1)S(1)}, bf16[368,128]{1,0:T(8,128)(2,1)S(1)}, u32[]{:S(2)}, u32[]{:S(2)}) collective-permute-start(bf16[368,128]{1,0:T(8,128)(2,1)S(1)} %get-tuple-element.26.after_ref), channel_id=1, source_target_pairs={{0,1},{1,2},{2,3},{3,4},{4,5},{5,6},{6,7},{7,8},{8,9},{9,10},{10,1... | collective-permute-start | bytes 282632 | tf_op jit(solution)/shard_map/ppermute | solution.py:360
  36.6 1.2 %collective-permute-done.2.refs_6_ = bf16[368,128]{1,0:T(8,128)(2,1)S(1)} collective-permute-done((bf16[368,128]{1,0:T(8,128)(2,1)S(1)}, bf16[368,128]{1,0:T(8,128)(2,1)S(1)}, u32[]{:S(2)}, u32[]{:S(2)}) %collective-permute-start.2) | collective-permute-done | bytes 94240 | tf_op jit(solution)/shard_map/ppermute | solution.py:360
  37.9 2.2 %kernel_gradient.1 = (f32[1792,128]{1,0:T(8,128)S(1)}, f32[1792,128]{1,0:T(8,128)S(1)}) custom-call(s32[2]{0:T(128)S(1)} %copy-done.4, s32[1]{0:T(128)} %bitcast.1.refs_1_.core_ref, bf16[1024,128]{1,0:T(8,128)(2,1)S(1)} %get-tuple-element.21.in_ref.refs_2_.refs_1_, bf16[1024,128]{1,0:T(8,128)(2,1)S(1)} %get-tuple-element.25.g_ref.refs_3_.refs_1_, ...), custom_call_target="tpu_custom_call" | custom-call | tf_op jit(solution)/shard_map/kernel_gradient/pallas_call | solution.py:277
  40.0 1.9 %collective-permute-start.4 = (f32[1792,128]{1,0:T(8,128)S(1)}, f32[1792,128]{1,0:T(8,128)S(1)}, u32[]{:S(2)}, u32[]{:S(2)}) collective-permute-start(f32[1792,128]{1,0:T(8,128)S(1)} %get-tuple-element.29.refs_8_), channel_id=1, source_target_pairs={{0,1},{1,0},{2,3},{3,2},{4,5},{5,4},{6,7},{7,6},{8,9},{9,8},{10,11... | collective-permute-start | bytes 2752520 | tf_op jit(solution)/shard_map/ppermute | solution.py:365
  42.0 2.4 %convolution.2 = (bf16[2,512,128]{2,1,0:T(8,128)(2,1)}, f32[8,128]{1,0:T(8,128)S(1)}) custom-call(s32[2]{0:T(128)S(1)} %copy-done.4, bf16[1024,128]{1,0:T(8,128)(2,1)S(1)} %get-tuple-element.21.in_ref.refs_2_.refs_1_, bf16[1024,128]{1,0:T(8,128)(2,1)S(1)} %get-tuple-element.22.refs_2_, bf16[3456,128]{1,0:T(8,128)(2,1)S(1)} %bitcast.16, ...), custom_call_target="tpu_custom_call" | custom-call | flops 1811939328 | bytes 2000000 | tf_op jit(solution)/shard_map/convolution/pallas_call | solution.py:306
  44.7 18.7 %all_to_all.15 = s16[16,128,128]{2,1,0:T(8,128)(2,1)S(1)} all-to-all(s16[16,128,128]{2,1,0:T(8,128)(2,1)S(1)} %bitcast.14), channel_id=1, replica_groups={{0,2,4,6,128,130,132,134,256,258,260,262,384,386,388,390},{1,3,5,7,129,..., dimensions={0} | all-to-all | bytes 1048576 | tf_op jit(solution)/shard_map/all_to_all | solution.py:370
  63.7 8.7 %all_to_all.16 = s16[4,128,128]{2,1,0:T(8,128)(2,1)S(1)} all-to-all(s16[4,128,128]{2,1,0:T(8,128)(2,1)S(1)} %bitcast.18), channel_id=1, replica_groups={{0,8,16,24},{1,9,17,25},{2,10,18,26},{3,11,19,27},{4,12,20,28},{5,13,21..., dimensions={0} | all-to-all | bytes 262144 | tf_op jit(solution)/shard_map/all_to_all | solution.py:370
  72.4 6.2 %collective-permute-start.5 = (s16[128,128]{1,0:T(8,128)(2,1)S(1)}, s16[128,128]{1,0:T(8,128)(2,1)S(1)}, u32[]{:S(2)}, u32[]{:S(2)}) collective-permute-start(s16[128,128]{1,0:T(8,128)(2,1)S(1)} %sum_blocks.5.refs_9_.refs_0_), channel_id=1, source_target_pairs={{0,32},{1,33},{2,34},{3,35},{4,36},{5,37},{6,38},{7,39},{8,40},{9,... | collective-permute-start | bytes 98312 | tf_op jit(solution)/shard_map/ppermute | solution.py:365
  78.7 2.4 %convolution.3 = (bf16[2,512,128]{2,1,0:T(8,128)(2,1)}, f32[8,128]{1,0:T(8,128)S(1)}) custom-call(s32[2]{0:T(128)S(1)} %copy-done.4, bf16[1024,128]{1,0:T(8,128)(2,1)S(1)} %get-tuple-element.21.in_ref.refs_2_.refs_1_, bf16[1024,128]{1,0:T(8,128)(2,1)S(1)} %get-tuple-element.22.refs_2_, ...), custom_call_target="tpu_custom_call", output_to_operand_aliasing={{0}: (8, {})} | custom-call | flops 1811939328 | bytes 2000000 | tf_op jit(solution)/shard_map/convolution/pallas_call | solution.py:306
  81.1 3.9 %collective-permute-start.6 = (s16[128,128]{1,0:T(8,128)(2,1)S(1)}, s16[128,128]{1,0:T(8,128)(2,1)S(1)}, u32[]{:S(2)}, u32[]{:S(2)}) collective-permute-start(s16[128,128]{1,0:T(8,128)(2,1)S(1)} %sum_blocks.6.refs_8_.refs_0_), channel_id=1, source_target_pairs={{0,96},{1,97},{2,98},{3,99},{4,100},{5,101},{6,102},{7,103},{8,104... | collective-permute-start | bytes 98312 | tf_op jit(solution)/shard_map/ppermute | solution.py:365
  85.0 2.4 %feature_gradient.2 = (bf16[2,512,128]{2,1,0:T(8,128)(2,1)}, f32[8,128]{1,0:T(8,128)S(1)}) custom-call(s32[2]{0:T(128)S(1)} %copy-done.4, bf16[1024,128]{1,0:T(8,128)(2,1)S(1)} %get-tuple-element.25.g_ref.refs_3_.refs_1_, bf16[1024,128]{1,0:T(8,128)(2,1)S(1)} %get-tuple-element.22.refs_2_, bf16[3456,128]{1,0:T(8,128)(2,1)S(1)} %get-tuple-element.34.refs_3_, ...), custom_call_target="tpu_custom_call" | custom-call | flops 1811939328 | bytes 2000000 | tf_op jit(solution)/shard_map/feature_gradient/pallas_call | solution.py:306
  87.4 2.4 %collective-permute-done.6.refs_1_ = s16[128,128]{1,0:T(8,128)(2,1)S(1)} collective-permute-done((s16[128,128]{1,0:T(8,128)(2,1)S(1)}, s16[128,128]{1,0:T(8,128)(2,1)S(1)}, u32[]{:S(2)}, u32[]{:S(2)}) %collective-permute-start.6) | collective-permute-done | bytes 32800 | tf_op jit(solution)/shard_map/ppermute | solution.py:365
  89.9 13.3 %all_to_all.17 = s16[16,128,128]{2,1,0:T(8,128)(2,1)S(1)} all-to-all(s16[16,128,128]{2,1,0:T(8,128)(2,1)S(1)} %bitcast.10), channel_id=1, replica_groups={{0,2,4,6,128,130,132,134,256,258,260,262,384,386,388,390},{1,3,5,7,129,..., dimensions={0} | all-to-all | bytes 1048576 | tf_op jit(solution)/shard_map/all_to_all | solution.py:370
  103.2 6.7 %collective-permute-start.7 = (s16[2048,128]{1,0:T(8,128)(2,1)S(1)}, s16[2048,128]{1,0:T(8,128)(2,1)S(1)}, u32[]{:S(2)}, u32[]{:S(2)}) collective-permute-start(s16[2048,128]{1,0:T(8,128)(2,1)S(1)} %bitcast.11), channel_id=1, source_target_pairs={{0,1},{1,0},{2,3},{3,2},{4,5},{5,4},{6,7},{7,6},{8,9},{9,8},{10,11... | collective-permute-start | bytes 1572872 | tf_op jit(solution)/shard_map/ppermute | solution.py:365
  109.9 2.4 %feature_gradient.3 = (bf16[2,512,128]{2,1,0:T(8,128)(2,1)}, f32[8,128]{1,0:T(8,128)}) custom-call(s32[2]{0:T(128)S(1)} %copy-done.4, bf16[1024,128]{1,0:T(8,128)(2,1)S(1)} %get-tuple-element.25.g_ref.refs_3_.refs_1_, bf16[1024,128]{1,0:T(8,128)(2,1)S(1)} %get-tuple-element.22.refs_2_, ...), custom_call_target="tpu_custom_call", output_to_operand_aliasing={{0}: (8, {})} | custom-call | flops 1811939328 | bytes 2000000 | tf_op jit(solution)/shard_map/feature_gradient/pallas_call | solution.py:306
  112.3 1.5 %place_halves.1 = f32[3456,128]{1,0:T(8,128)} custom-call(s32[1]{0:T(128)} %bitcast.1.refs_1_.core_ref, s16[2048,128]{1,0:T(8,128)(2,1)S(1)} %bitcast.13, s16[2048,128]{1,0:T(8,128)(2,1)S(1)} %collective-permute-done.7.far_ref), custom_call_target="tpu_custom_call" | custom-call | tf_op jit(solution)/shard_map/place_halves/pallas_call | solution.py:289
  (21 shorter events, 2.4 us)
Async XLA Ops:
  0.6 1.0 copy-start.1
  1.6 0.9 copy-start.2
  2.5 0.7 copy-start.3
  3.2 0.7 copy-start.5
  3.9 32.4 %copy-start = (bf16[27,128,128]{2,1,0:T(8,128)(2,1)S(1)}, bf16[27,128,128]{2,1,0:T(8,128)(2,1)}, u32[]{:S(2)}) copy-start(bf16[27,128,128]{2,1,0:T(8,128)(2,1)} %param.8) | copy-start | bytes 2654212
  3.9 34.0 %copy-start.4 = (s32[2]{0:T(128)S(1)}, s32[2]{0:T(128)}, u32[]{:S(2)}) copy-start(s32[2]{0:T(128)} %refs_0_.11) | copy-start | bytes 28
  4.7 11.0 %collective-permute-start = (bf16[272,128]{1,0:T(8,128)(2,1)S(1)}, bf16[272,128]{1,0:T(8,128)(2,1)S(1)}, u32[]{:S(2)}, u32[]{:S(2)}) collective-permute-start(bf16[272,128]{1,0:T(8,128)(2,1)S(1)} %get-tuple-element.23), channel_id=1, source_target_pairs={{0,32},{1,33},{2,34},{3,35},{4,36},{5,37},{6,38},{7,39},{8,40},{9,... | collective-permute-start | bytes 208904 | tf_op jit(solution)/shard_map/ppermute | solution.py:360
  14.3 15.5 %collective-permute-start.1 = (bf16[272,128]{1,0:T(8,128)(2,1)S(1)}, bf16[272,128]{1,0:T(8,128)(2,1)S(1)}, u32[]{:S(2)}, u32[]{:S(2)}) collective-permute-start(bf16[272,128]{1,0:T(8,128)(2,1)S(1)} %get-tuple-element.24), channel_id=1, source_target_pairs={{32,0},{33,1},{34,2},{35,3},{36,4},{37,5},{38,6},{39,7},{40,8},{41... | collective-permute-start | bytes 208904 | tf_op jit(solution)/shard_map/ppermute | solution.py:360
  30.4 6.2 %collective-permute-start.3 = (bf16[368,128]{1,0:T(8,128)(2,1)S(1)}, bf16[368,128]{1,0:T(8,128)(2,1)S(1)}, u32[]{:S(2)}, u32[]{:S(2)}) collective-permute-start(bf16[368,128]{1,0:T(8,128)(2,1)S(1)} %get-tuple-element.27), channel_id=1, source_target_pairs={{1,0},{2,1},{3,2},{4,3},{5,4},{6,5},{7,6},{8,7},{9,8},{10,9},{11,1... | collective-permute-start | bytes 282632 | tf_op jit(solution)/shard_map/ppermute | solution.py:360
  33.3 4.6 %collective-permute-start.2 = (bf16[368,128]{1,0:T(8,128)(2,1)S(1)}, bf16[368,128]{1,0:T(8,128)(2,1)S(1)}, u32[]{:S(2)}, u32[]{:S(2)}) collective-permute-start(bf16[368,128]{1,0:T(8,128)(2,1)S(1)} %get-tuple-element.26.after_ref), channel_id=1, source_target_pairs={{0,1},{1,2},{2,3},{3,4},{4,5},{5,6},{6,7},{7,8},{8,9},{9,10},{10,1... | collective-permute-start | bytes 282632 | tf_op jit(solution)/shard_map/ppermute | solution.py:360
  40.0 4.4 %collective-permute-start.4 = (f32[1792,128]{1,0:T(8,128)S(1)}, f32[1792,128]{1,0:T(8,128)S(1)}, u32[]{:S(2)}, u32[]{:S(2)}) collective-permute-start(f32[1792,128]{1,0:T(8,128)S(1)} %get-tuple-element.29.refs_8_), channel_id=1, source_target_pairs={{0,1},{1,0},{2,3},{3,2},{4,5},{5,4},{6,7},{7,6},{8,9},{9,8},{10,11... | collective-permute-start | bytes 2752520 | tf_op jit(solution)/shard_map/ppermute | solution.py:365
  72.4 8.6 %collective-permute-start.5 = (s16[128,128]{1,0:T(8,128)(2,1)S(1)}, s16[128,128]{1,0:T(8,128)(2,1)S(1)}, u32[]{:S(2)}, u32[]{:S(2)}) collective-permute-start(s16[128,128]{1,0:T(8,128)(2,1)S(1)} %sum_blocks.5.refs_9_.refs_0_), channel_id=1, source_target_pairs={{0,32},{1,33},{2,34},{3,35},{4,36},{5,37},{6,38},{7,39},{8,40},{9,... | collective-permute-start | bytes 98312 | tf_op jit(solution)/shard_map/ppermute | solution.py:365
  81.1 8.7 %collective-permute-start.6 = (s16[128,128]{1,0:T(8,128)(2,1)S(1)}, s16[128,128]{1,0:T(8,128)(2,1)S(1)}, u32[]{:S(2)}, u32[]{:S(2)}) collective-permute-start(s16[128,128]{1,0:T(8,128)(2,1)S(1)} %sum_blocks.6.refs_8_.refs_0_), channel_id=1, source_target_pairs={{0,96},{1,97},{2,98},{3,99},{4,100},{5,101},{6,102},{7,103},{8,104... | collective-permute-start | bytes 98312 | tf_op jit(solution)/shard_map/ppermute | solution.py:365
  103.2 9.1 %collective-permute-start.7 = (s16[2048,128]{1,0:T(8,128)(2,1)S(1)}, s16[2048,128]{1,0:T(8,128)(2,1)S(1)}, u32[]{:S(2)}, u32[]{:S(2)}) collective-permute-start(s16[2048,128]{1,0:T(8,128)(2,1)S(1)} %bitcast.11), channel_id=1, source_target_pairs={{0,1},{1,0},{2,3},{3,2},{4,5},{5,4},{6,7},{7,6},{8,9},{9,8},{10,11... | collective-permute-start | bytes 1572872 | tf_op jit(solution)/shard_map/ppermute | solution.py:365

commit v3 on v2

--- a/solution.py
+++ b/solution.py
@@ -39,7 +39,8 @@
 
 
 def prep_kernel(*refs):
-    sources, (in_ref, g_ref, mask_ref, xlo_ref, xhi_ref), held, sems = refs[:4], refs[4:9], refs[9:13], refs[13]
+    sources, outs, held, sems = refs[:4], refs[4:11], refs[11:15], refs[15]
+    in_ref, g_ref, mask_ref, xlo_ref, xhi_ref, ylo_ref, yhi_ref = outs
     copies = [pltpu.make_async_copy(src, dst, sems.at[i]) for i, (src, dst) in enumerate(zip(sources, held))]
     for copy in copies:
         copy.start()
@@ -48,7 +49,7 @@
     pos_ref, occ_ref, feat_ref, grad_ref = held
     occ = occ_ref[...].astype(jnp.float32)
     layer = BE * BE
-    for face in (xlo_ref, xhi_ref):
+    for face in (xlo_ref, xhi_ref, ylo_ref, yhi_ref):
         face[FACE:FACE + TAG, :] = tags(pos_ref)
     for s in range(BLK_DEV):
         live = (pos_ref[s] >= 0).astype(jnp.float32)
@@ -57,83 +58,82 @@
         ])
         mask_ref[s * VOX:(s + 1) * VOX, :] = mask.astype(jnp.bfloat16)
         for field, (src, dst) in enumerate(((feat_ref, in_ref), (grad_ref, g_ref))):
-            value = jnp.where(mask > 0, src[s].astype(jnp.float32), 0.0).astype(jnp.bfloat16)
-            dst[s * VOX:(s + 1) * VOX, :] = value
+            value = jnp.where(mask > 0, src[s].astype(jnp.float32), 0.0)
+            cube = value.reshape(BE, BE, BE, C)
+            dst[s * VOX:(s + 1) * VOX, :] = value.astype(jnp.bfloat16)
             at = (field * BLK_DEV + s) * layer
-            xlo_ref[at:at + layer, :] = value[:layer]
-            xhi_ref[at:at + layer, :] = value[VOX - layer:]
-
-
-def y_faces_kernel(pos_ref, in_ref, g_ref, low_ref, high_ref, ylo_ref, yhi_ref):
+            for face, piece in (
+                (xlo_ref, cube[0]), (xhi_ref, cube[BE - 1]), (ylo_ref, cube[:, 0]), (yhi_ref, cube[:, BE - 1])
+            ):
+                face[at:at + layer, :] = piece.reshape(layer, C).astype(jnp.bfloat16)
+
+
+def edges_kernel(low_ref, high_ref, after_ref, ylo_ref, yhi_ref):
     layer = BE * BE
-    for field, own in enumerate((in_ref, g_ref)):
-        for s in range(BLK_DEV):
-            cube = own[s * VOX:(s + 1) * VOX, :].astype(jnp.float32).reshape(BE, BE, BE, C)
-            at = (field * BLK_DEV + s) * layer
-            for y, out in ((0, ylo_ref), (BE - 1, yhi_ref)):
-                out[at:at + layer, :] = cube[:, y].reshape(layer, C).astype(jnp.bfloat16)
     for side, ref in enumerate((low_ref, high_ref)):
         faces = [ref[n * layer:(n + 1) * layer, :].astype(jnp.float32) for n in range(2 * BLK_DEV)]
         for y, out in ((0, ylo_ref), (BE - 1, yhi_ref)):
             edge = [face[y * BE:(y + 1) * BE] for face in faces]
-            at = FACE + side * EDGE
-            out[at:at + EDGE, :] = jnp.concatenate(edge).astype(jnp.bfloat16)
-            at = FACE + 2 * EDGE + side * TAG
+            out[side * EDGE:(side + 1) * EDGE, :] = jnp.concatenate(edge).astype(jnp.bfloat16)
+            at = 2 * EDGE + side * TAG
             out[at:at + TAG, :] = ref[FACE:FACE + TAG, :]
-    at = FACE + 2 * EDGE + 2 * TAG
-    for out in (ylo_ref, yhi_ref):
-        out[at:at + TAG, :] = tags(pos_ref)
-
-
-def fill_windows(field, slots, pos_ref, own_ref, x_from, y_from, z_ref, a_ref):
+
+
+def tags_of(ref, at):
+    tag = ref[at:at + TAG, :].astype(jnp.float32)
+    return [tag[0:BE], tag[BE:2 * BE]]
+
+
+def face_of(ref, field, shape):
+    first = field * BLK_DEV
+    return [
+        ref[n * BE * BE:(n + 1) * BE * BE, :].astype(jnp.float32).reshape(shape)
+        for n in range(first, first + BLK_DEV)
+    ]
+
+
+def picked(data, their_tags, here, o3):
     row = lax.broadcasted_iota(jnp.int32, (BE, C), 0)
-    first = field * BLK_DEV
+    value = jnp.zeros((), jnp.float32)
+    for n in (1, 0):
+        if o3 == 0:
+            wanted, moved = jnp.where(row == 0, -1.0, 0.0), pltpu.roll(data[n], 1, 1)
+        elif o3 == 2:
+            wanted, moved = jnp.where(row == BE - 1, 1.0, 0.0), pltpu.roll(data[n], BE - 1, 1)
+        else:
+            wanted, moved = jnp.zeros((BE, C), jnp.float32), data[n]
+        value = jnp.where(((their_tags[n] - here) == wanted)[None], moved, value)
+    return value
+
+
+def fill_windows(field, slots, pos_ref, own_ref, x_from, y_from, c_from, z_ref, a_ref):
     regions = []
-
-    def face_of(ref, shape):
-        return [
-            ref[n * BE * BE:(n + 1) * BE * BE, :].astype(jnp.float32).reshape(shape)
-            for n in range(first, first + BLK_DEV)
-        ]
-
-    def tags_of(ref, at):
-        tag = ref[at:at + TAG, :].astype(jnp.float32)
-        return [tag[0:BE], tag[BE:2 * BE]]
-
     own = [own_ref[n * VOX:(n + 1) * VOX, :].astype(jnp.float32).reshape(BE, BE, BE, C) for n in range(BLK_DEV)]
     own_tags = [jnp.full((BE, C), pos_ref[n].astype(jnp.float32), jnp.float32) for n in range(BLK_DEV)]
     inside = slice(1, BE + 1)
     ends = (slice(0, 1), slice(WIN - 1, WIN))
     regions.append((inside, inside, own, own_tags))
     for ref, end in zip(x_from, ends):
-        regions.append((end, inside, face_of(ref, (1, BE, BE, C)), tags_of(ref, FACE)))
+        regions.append((end, inside, face_of(ref, field, (1, BE, BE, C)), tags_of(ref, FACE)))
     for ref, end in zip(y_from, ends):
-        regions.append((inside, end, face_of(ref, (BE, 1, BE, C)), tags_of(ref, FACE + 2 * EDGE + 2 * TAG)))
+        regions.append((inside, end, face_of(ref, field, (BE, 1, BE, C)), tags_of(ref, FACE)))
+    for ref, end in zip(c_from, ends):
         for side, other in enumerate(ends):
-            edge = ref[FACE + side * EDGE:FACE + (side + 1) * EDGE, :].astype(jnp.float32)
+            edge = ref[side * EDGE:(side + 1) * EDGE, :].astype(jnp.float32)
+            first = field * BLK_DEV
             data = [edge[n * BE:(n + 1) * BE].reshape(1, 1, BE, C) for n in range(first, first + BLK_DEV)]
-            regions.append((other, end, data, tags_of(ref, FACE + 2 * EDGE + side * TAG)))
+            regions.append((other, end, data, tags_of(ref, 2 * EDGE + side * TAG)))
+    if not c_from:
+        for x in ends:
+            for y in ends:
+                z_ref[:, x, y] = jnp.zeros((3, 1, 1, BE, C), jnp.float32)
 
     for i, s in enumerate(slots):
         here = pos_ref[s].astype(jnp.float32)
-        for xs, ys, data, tags in regions:
-            delta = [tag - here for tag in tags]
+        for xs, ys, data, their_tags in regions:
+            flat = [v.reshape(-1, BE, C) for v in data]
             for o3 in range(3):
-                picks = []
-                for n in range(BLK_DEV):
-                    if o3 == 0:
-                        wanted = jnp.where(row == 0, -1.0, 0.0)
-                        moved = pltpu.roll(data[n].reshape(-1, BE, C), 1, 1)
-                    elif o3 == 2:
-                        wanted = jnp.where(row == BE - 1, 1.0, 0.0)
-                        moved = pltpu.roll(data[n].reshape(-1, BE, C), BE - 1, 1)
-                    else:
-                        wanted = jnp.zeros((BE, C), jnp.float32)
-                        moved = data[n].reshape(-1, BE, C)
-                    picks.append(((delta[n] == wanted)[None], moved))
-                value = jnp.where(picks[1][0], picks[1][1], 0.0)
-                value = jnp.where(picks[0][0], picks[0][1], value)
-                z_ref[o3, xs, ys] = value.reshape(data[0].shape)
+                z_ref[o3, xs, ys] = picked(flat, their_tags, here, o3).reshape(data[0].shape)
         for o2 in range(3):
             for o3 in range(3):
                 j = o2 * 3 + o3
@@ -141,9 +141,35 @@
                 a_ref[i, :, j * C:(j + 1) * C] = piece.astype(jnp.bfloat16)
 
 
+def diagonal_pairs(x_high, y_low, y_high):
+    def column(ref, field, end):
+        return [v[:, end] for v in face_of(ref, field, (1, BE, BE, C))]
+
+    last = BE - 1
+    plans = {
+        0: (((x_high, 0), (y_low, last), 0), ((x_high, last), (y_high, last), 2)),
+        2: (((y_low, last), (x_high, 0), 2), ((y_high, last), (x_high, last), 0)),
+    }
+    result = {}
+    for e1, plan in plans.items():
+        inputs, rows = [], []
+        for (near, near_end), (far, far_end), e2 in plan:
+            inputs += [v.reshape(BE, C) for v in column(near, 0, near_end)]
+            data, their_tags = column(far, 1, far_end), tags_of(far, FACE)
+            for here in tags_of(near, FACE):
+                blank = jnp.zeros((BE, C), jnp.float32)
+                lanes = [blank] * 9
+                for e3 in range(3):
+                    lanes[3 * e2 + e3] = picked(data, their_tags, here, e3).reshape(BE, C)
+                rows.append(jnp.concatenate(lanes, axis=1))
+        result[e1] = (jnp.concatenate(inputs), jnp.concatenate(rows).astype(jnp.bfloat16))
+    return result
+
+
 def wgrad_kernel(scale, pos_ref, core_ref, in_ref, g_ref, *refs):
     halo, keep_ref, send_ref, z_ref, a_ref, total_ref = refs[:4], *refs[-5:]
-    fill_windows(1, (0, 1), pos_ref, g_ref, halo[0:2], halo[2:4], z_ref, a_ref)
+    fill_windows(1, (0, 1), pos_ref, g_ref, halo[0:2], halo[2:4], (), z_ref, a_ref)
+    pairs = diagonal_pairs(halo[1], halo[2], halo[3])
     inner = [
         jnp.transpose(in_ref[s * VOX:(s + 1) * VOX, :].astype(jnp.float32)).astype(jnp.bfloat16)
         for s in range(BLK_DEV)
@@ -153,6 +179,11 @@
         rows = slice(e1 * BE * BE, e1 * BE * BE + VOX)
         total = jnp.dot(inner[0], a_ref[0, rows, :], preferred_element_type=jnp.float32)
         total = total + jnp.dot(inner[1], a_ref[1, rows, :], preferred_element_type=jnp.float32)
+        if e1 in pairs:
+            lhs, rhs = pairs[e1]
+            lhs = jnp.concatenate([lhs, jnp.zeros((C - lhs.shape[0], C), jnp.float32)])
+            rhs = jnp.concatenate([rhs, jnp.zeros((C - rhs.shape[0], SIDE), jnp.bfloat16)])
+            total = total + jnp.dot(lhs.T.astype(jnp.bfloat16), rhs, preferred_element_type=jnp.float32)
         total = total * scale
         for j in range(9):
             k = KV - 1 - (9 * e1 + j)
@@ -194,8 +225,8 @@
 
 
 def conv_kernel(field, slot, pos_ref, own_ref, mask_ref, w_ref, *refs):
-    halo, out_ref, done_ref, z_ref, a_ref = refs[:4], *refs[-4:]
-    fill_windows(field, (slot,), pos_ref, own_ref, halo[0:2], halo[2:4], z_ref, a_ref)
+    halo, out_ref, done_ref, z_ref, a_ref = refs[:6], *refs[-4:]
+    fill_windows(field, (slot,), pos_ref, own_ref, halo[0:2], halo[2:4], halo[4:6], z_ref, a_ref)
     total = None
     for e1 in range(3):
         rows = slice(e1 * BE * BE, e1 * BE * BE + VOX)
@@ -222,9 +253,9 @@
     field = pltpu.VMEM((BLK_DEV, VOX, C), jnp.bfloat16)
     return pl.pallas_call(
         prep_kernel,
-        out_shape=[bf16(BLK_DEV * VOX, C)] * 3 + [bf16(FACE + TAG, C)] * 2,
+        out_shape=[bf16(BLK_DEV * VOX, C)] * 3 + [bf16(FACE + TAG, C)] * 4,
         in_specs=[pl.BlockSpec(memory_space=pltpu.HBM)] * 4,
-        out_specs=[VMEM] * 5,
+        out_specs=[VMEM] * 7,
         scratch_shapes=[
             pltpu.SMEM((BLK_DEV,), jnp.int32),
             pltpu.VMEM((BLK_DEV, VOX), jnp.int32),
@@ -237,15 +268,15 @@
     )(block_pos, occupancy, features, out_grad)
 
 
-def y_faces(block_pos, own_in, own_grad, low, high):
-    return pl.pallas_call(
-        y_faces_kernel,
-        out_shape=[bf16(FACE + 2 * EDGE + 3 * TAG, C)] * 2,
-        in_specs=[SMEM] + [VMEM] * 4,
+def edges(low, high, after):
+    return pl.pallas_call(
+        edges_kernel,
+        out_shape=[bf16(2 * EDGE + 2 * TAG, C)] * 2,
+        in_specs=[VMEM] * 2 + [ANY],
         out_specs=[VMEM] * 2,
         compiler_params=PARAMS,
-        name="y_faces",
-    )(block_pos, own_in, own_grad, low, high)
+        name="edges",
+    )(low, high, after)
 
 
 def turn(weights, after):
@@ -374,9 +405,8 @@
 def body(features, occupancy, block_pos, kernel, out_grad):
     groups, tiles = lax.axis_size("group"), lax.axis_size("tile")
     core = (lax.axis_index("tile") & 1).astype(jnp.int32).reshape(1)
-    own_in, own_grad, mask, xlo, xhi = prep(block_pos, occupancy, features, out_grad)
+    own_in, own_grad, mask, xlo, xhi, ylo, yhi = prep(block_pos, occupancy, features, out_grad)
     x_from = (shifted(xhi, groups, tiles, 1, 0), shifted(xlo, groups, tiles, -1, 0))
-    ylo, yhi = y_faces(block_pos, own_in, own_grad, *x_from)
     y_from = (shifted(yhi, groups, tiles, 0, 1), shifted(ylo, groups, tiles, 0, -1))
     halo = (*x_from, *y_from)
     weights = kernel.reshape(KV * C, C)
@@ -391,12 +421,14 @@
         )
 
     got = across(send, CORE)
-    conv_out, done = convolved(0, 0, None, send)
-    value, = small(sum_halves_kernel, [16 * CODED], [keep, got], [done])
+    clo, chi = edges(*x_from, send)
+    halo += (shifted(chi, groups, tiles, 0, 1), shifted(clo, groups, tiles, 0, -1))
+    value, = small(sum_halves_kernel, [16 * CODED], [keep, got], [clo])
     value, = small(sum_blocks_kernel, [4 * CODED], [exchange(value, AXES, XY_SETS)])
     value, = small(sum_blocks_kernel, [CODED], [exchange(value, "tile", Z_LO_SETS)])
     got = across(value, Z_HI_BITS[0])
-    conv_out, done = convolved(0, 1, conv_out, value)
+    conv_out, done = convolved(0, 0, None, value)
+    conv_out, done = convolved(0, 1, conv_out, done)
     value, = small(sum_blocks_kernel, [CODED], [value, got], [done])
     got = across(value, Z_HI_BITS[1])
     feature_grad, done = convolved(1, 0, None, value)

time: 114 us -> 111 us (0.974)
  starting transfers between devices: 35.5 us -> 44.5 us
  waiting for transfers between devices: 17.8 us -> 10.3 us
  blocking collectives: 40.7 us -> 33.4 us
  local copies, waits for them, and re-layouts: 3.24 us -> 5.06 us
    ppermute x4 -> x6, waiting for transfers between devices: 15.4 us -> 6.78 us  [shifted(): return lax.ppermute(value, AXES, pairs)]
    all_to_all x3 -> x2, blocking collectives: 40.7 us -> 33.4 us  [exchange(): lax.all_to_all(value.reshape(count, -1, C), axis, 0, 0, axis_index_groups...]
    ppermute x4 -> x6, starting transfers between devices: 16.8 us -> 22.6 us  [shifted(): return lax.ppermute(value, AXES, pairs)]
    all_to_all x0 -> x1, starting transfers between devices: none -> 3.33 us  [exchange(): lax.all_to_all(value.reshape(count, -1, C), axis, 0, 0, axis_index_groups...]
    unnamed x12 -> x16, local copies, waits for them, and re-layouts: 3.24 us -> 5.06 us
  transfers between devices with their start and end apart: 8 -> 11, of which waited for: 4 -> 3; matrix products, arithmetic and copies ran while one was open for 0% -> 0% of each run, Pallas kernels for 9% -> 9%
where the time goes in v3:
time: 111 us; the launch traced here: 110 us
  starting transfers between devices  44.5 us (40%)
  blocking collectives  33.4 us (30%)
  Pallas kernels  15.8 us (14%)
  waiting for transfers between devices  10.3 us (9%)
  local copies, waits for them, and re-layouts  5.06 us (5%)
    all_to_all x2, blocking collectives, exchange(): lax.all_to_all(value.reshape(count, -1, C), axis, 0, 0, axis_index_groups...  33.4 us
    ppermute x6, starting transfers between devices, shifted(): return lax.ppermute(value, AXES, pairs)  22.6 us
    ppermute x4, starting transfers between devices, across(): return lax.ppermute(value, AXES, [(i, i ^ mask) for i in range(count)])  18.6 us
    pallas_call x4, Pallas kernels, conv(): pl.pallas_call(kernel, grid=(1,), out_shape=[bf16(BLK_DEV, VOX, C), jax.S...  9.51 us
    ppermute x6, waiting for transfers between devices, shifted(): return lax.ppermute(value, AXES, pairs)  6.78 us
    unnamed x16, local copies, waits for them, and re-layouts  5.06 us
    ppermute x4, waiting for transfers between devices, across(): return lax.ppermute(value, AXES, [(i, i ^ mask) for i in range(count)])  3.5 us
    all_to_all x1, starting transfers between devices, exchange(): lax.all_to_all(value.reshape(count, -1, C), axis, 0, 0, axis_index_groups...  3.33 us
  transfers between devices with their start and end apart: 11, of which 3 were waited for; matrix products, arithmetic and copies ran while one was open for 0% of the time, Pallas kernels for 9%

profile of v3, /device:TPU:1, one launch (start us, length us, event | category | flops | bytes accessed | tf_op | source)
XLA Modules:
  0.0 109.9 jit_solution(2381685808155046136)
XLA Ops:
  1.6 0.9 copy-done.3
  4.7 9.6 %collective-permute-start = (bf16[272,128]{1,0:T(8,128)(2,1)S(1)}, bf16[272,128]{1,0:T(8,128)(2,1)S(1)}, u32[]{:S(2)}, u32[]{:S(2)}) collective-permute-start(bf16[272,128]{1,0:T(8,128)(2,1)S(1)} %get-tuple-element.25), channel_id=1, source_target_pairs={{0,32},{1,33},{2,34},{3,35},{4,36},{5,37},{6,38},{7,39},{8,40},{9,... | collective-permute-start | bytes 208904 | tf_op jit(solution)/shard_map/ppermute | solution.py:391
  14.3 1.3 %collective-permute-start.1 = (bf16[272,128]{1,0:T(8,128)(2,1)S(1)}, bf16[272,128]{1,0:T(8,128)(2,1)S(1)}, u32[]{:S(2)}, u32[]{:S(2)}) collective-permute-start(bf16[272,128]{1,0:T(8,128)(2,1)S(1)} %get-tuple-element.26), channel_id=1, source_target_pairs={{32,0},{33,1},{34,2},{35,3},{36,4},{37,5},{38,6},{39,7},{40,8},{41... | collective-permute-start | bytes 208904 | tf_op jit(solution)/shard_map/ppermute | solution.py:391
  15.6 2.9 %collective-permute-start.3 = (bf16[272,128]{1,0:T(8,128)(2,1)S(1)}, bf16[272,128]{1,0:T(8,128)(2,1)S(1)}, u32[]{:S(2)}, u32[]{:S(2)}) collective-permute-start(bf16[272,128]{1,0:T(8,128)(2,1)S(1)} %get-tuple-element.28), channel_id=1, source_target_pairs={{1,0},{2,1},{3,2},{4,3},{5,4},{6,5},{7,6},{8,7},{9,8},{10,9},{11,1... | collective-permute-start | bytes 208904 | tf_op jit(solution)/shard_map/ppermute | solution.py:391
  18.5 3.0 %collective-permute-start.2 = (bf16[272,128]{1,0:T(8,128)(2,1)S(1)}, bf16[272,128]{1,0:T(8,128)(2,1)S(1)}, u32[]{:S(2)}, u32[]{:S(2)}) collective-permute-start(bf16[272,128]{1,0:T(8,128)(2,1)S(1)} %get-tuple-element.27.after_ref), channel_id=1, source_target_pairs={{0,1},{1,2},{2,3},{3,4},{4,5},{5,6},{6,7},{7,8},{8,9},{9,10},{10,1... | collective-permute-start | bytes 208904 | tf_op jit(solution)/shard_map/ppermute | solution.py:391
  21.5 1.2 %copy-done = bf16[27,128,128]{2,1,0:T(8,128)(2,1)S(1)} copy-done((bf16[27,128,128]{2,1,0:T(8,128)(2,1)S(1)}, bf16[27,128,128]{2,1,0:T(8,128)(2,1)}, u32[]{:S(2)}) %copy-start) | copy-done | bytes 884760
  23.0 6.8 %collective-permute-done.1.refs_5_.high_ref = bf16[272,128]{1,0:T(8,128)(2,1)S(1)} collective-permute-done((bf16[272,128]{1,0:T(8,128)(2,1)S(1)}, bf16[272,128]{1,0:T(8,128)(2,1)S(1)}, u32[]{:S(2)}, u32[]{:S(2)}) %collective-permute-start.1) | collective-permute-done | bytes 69664 | tf_op jit(solution)/shard_map/ppermute | solution.py:391
  30.5 2.3 %kernel_gradient.1 = (f32[1792,128]{1,0:T(8,128)S(1)}, f32[1792,128]{1,0:T(8,128)S(1)}) custom-call(s32[2]{0:T(128)S(1)} %copy-done.6, s32[1]{0:T(128)} %bitcast.1.refs_1_.core_ref, bf16[1024,128]{1,0:T(8,128)(2,1)S(1)} %get-tuple-element.23.refs_2_.refs_1_, bf16[1024,128]{1,0:T(8,128)(2,1)S(1)} %get-tuple-element.29.refs_3_.refs_1_, ...), custom_call_target="tpu_custom_call" | custom-call | tf_op jit(solution)/shard_map/kernel_gradient/pallas_call | solution.py:308
  32.8 2.9 %collective-permute-start.6 = (f32[1792,128]{1,0:T(8,128)S(1)}, f32[1792,128]{1,0:T(8,128)S(1)}, u32[]{:S(2)}, u32[]{:S(2)}) collective-permute-start(f32[1792,128]{1,0:T(8,128)S(1)} %get-tuple-element.31.after_ref), channel_id=1, source_target_pairs={{0,1},{1,0},{2,3},{3,2},{4,5},{5,4},{6,7},{7,6},{8,9},{9,8},{10,11... | collective-permute-start | bytes 2752520 | tf_op jit(solution)/shard_map/ppermute | solution.py:396
  35.7 2.1 %collective-permute-done.6.refs_1_ = f32[1792,128]{1,0:T(8,128)S(1)} collective-permute-done((f32[1792,128]{1,0:T(8,128)S(1)}, f32[1792,128]{1,0:T(8,128)S(1)}, u32[]{:S(2)}, u32[]{:S(2)}) %collective-permute-start.6) | collective-permute-done | bytes 917536 | tf_op jit(solution)/shard_map/ppermute | solution.py:396
  38.1 17.3 %all_to_all.15 = s16[16,128,128]{2,1,0:T(8,128)(2,1)S(1)} all-to-all(s16[16,128,128]{2,1,0:T(8,128)(2,1)S(1)} %bitcast.14), channel_id=1, replica_groups={{0,2,4,6,128,130,132,134,256,258,260,262,384,386,388,390},{1,3,5,7,129,..., dimensions={0} | all-to-all | bytes 1048576 | tf_op jit(solution)/shard_map/all_to_all | solution.py:401
  56.2 3.3 %all-to-all-start.1 = ((s16[4,128,128]{2,1,0:T(8,128)(2,1)}), s16[4,128,128]{2,1,0:T(8,128)(2,1)S(1)}, u32[]{:S(2)}, u32[]{:S(2)}) async-start(s16[4,128,128]{2,1,0:T(8,128)(2,1)} %bitcast.4), calls=%async_computation.1 | async-start | bytes 262144 | tf_op jit(solution)/shard_map/all_to_all | solution.py:401
  59.6 3.9 %collective-permute-start.4 = (bf16[96,128]{1,0:T(8,128)(2,1)S(1)}, bf16[96,128]{1,0:T(8,128)(2,1)S(1)}, u32[]{:S(2)}, u32[]{:S(2)}) collective-permute-start(bf16[96,128]{1,0:T(8,128)(2,1)S(1)} %get-tuple-element.32), channel_id=1, source_target_pairs={{0,1},{1,2},{2,3},{3,4},{4,5},{5,6},{6,7},{7,8},{8,9},{9,10},{10,1... | collective-permute-start | bytes 73736 | tf_op jit(solution)/shard_map/ppermute | solution.py:391
  63.4 1.9 %collective-permute-start.5 = (bf16[96,128]{1,0:T(8,128)(2,1)S(1)}, bf16[96,128]{1,0:T(8,128)(2,1)S(1)}, u32[]{:S(2)}, u32[]{:S(2)}) collective-permute-start(bf16[96,128]{1,0:T(8,128)(2,1)S(1)} %get-tuple-element.33.refs_2_), channel_id=1, source_target_pairs={{1,0},{2,1},{3,2},{4,3},{5,4},{6,5},{7,6},{8,7},{9,8},{10,9},{11,1... | collective-permute-start | bytes 73736 | tf_op jit(solution)/shard_map/ppermute | solution.py:391
  65.4 7.2 %collective-permute-start.7 = (s16[128,128]{1,0:T(8,128)(2,1)S(1)}, s16[128,128]{1,0:T(8,128)(2,1)S(1)}, u32[]{:S(2)}, u32[]{:S(2)}) collective-permute-start(s16[128,128]{1,0:T(8,128)(2,1)S(1)} %sum_blocks.5.refs_10_.refs_0_), channel_id=1, source_target_pairs={{0,32},{1,33},{2,34},{3,35},{4,36},{5,37},{6,38},{7,39},{8,40},{9,... | collective-permute-start | bytes 98312 | tf_op jit(solution)/shard_map/ppermute | solution.py:396
  72.7 2.4 %convolution.2 = (bf16[2,512,128]{2,1,0:T(8,128)(2,1)}, f32[8,128]{1,0:T(8,128)S(1)}) custom-call(s32[2]{0:T(128)S(1)} %copy-done.7, bf16[1024,128]{1,0:T(8,128)(2,1)S(1)} %get-tuple-element.23.refs_2_.refs_1_, bf16[1024,128]{1,0:T(8,128)(2,1)S(1)} %get-tuple-element.24.refs_2_, bf16[3456,128]{1,0:T(8,128)(2,1)S(1)} %bitcast.16, ...), custom_call_target="tpu_custom_call" | custom-call | flops 1811939328 | bytes 2000000 | tf_op jit(solution)/shard_map/convolution/pallas_call | solution.py:337
  75.0 2.4 %convolution.3 = (bf16[2,512,128]{2,1,0:T(8,128)(2,1)}, f32[8,128]{1,0:T(8,128)S(1)}) custom-call(s32[2]{0:T(128)S(1)} %copy-done.7, bf16[1024,128]{1,0:T(8,128)(2,1)S(1)} %get-tuple-element.23.refs_2_.refs_1_, bf16[1024,128]{1,0:T(8,128)(2,1)S(1)} %get-tuple-element.24.refs_2_, bf16[3456,128]{1,0:T(8,128)(2,1)S(1)} %bitcast.17, ...), custom_call_target="tpu_custom_call", output_to_operand_aliasing={{0}: (10, {})} | custom-call | flops 1811939328 | bytes 2000000 | tf_op jit(solution)/shard_map/convolution/pallas_call | solution.py:337
  77.5 4.7 %collective-permute-start.8 = (s16[128,128]{1,0:T(8,128)(2,1)S(1)}, s16[128,128]{1,0:T(8,128)(2,1)S(1)}, u32[]{:S(2)}, u32[]{:S(2)}) collective-permute-start(s16[128,128]{1,0:T(8,128)(2,1)S(1)} %sum_blocks.6.refs_10_.refs_0_), channel_id=1, source_target_pairs={{0,96},{1,97},{2,98},{3,99},{4,100},{5,101},{6,102},{7,103},{8,104... | collective-permute-start | bytes 98312 | tf_op jit(solution)/shard_map/ppermute | solution.py:396
  82.2 2.4 %feature_gradient.2 = (bf16[2,512,128]{2,1,0:T(8,128)(2,1)}, f32[8,128]{1,0:T(8,128)S(1)}) custom-call(s32[2]{0:T(128)S(1)} %copy-done.7, bf16[1024,128]{1,0:T(8,128)(2,1)S(1)} %get-tuple-element.29.refs_3_.refs_1_, bf16[1024,128]{1,0:T(8,128)(2,1)S(1)} %get-tuple-element.24.refs_2_, bf16[3456,128]{1,0:T(8,128)(2,1)S(1)} %get-tuple-element.38.refs_3_, ...), custom_call_target="tpu_custom_call" | custom-call | flops 1811939328 | bytes 2000000 | tf_op jit(solution)/shard_map/feature_gradient/pallas_call | solution.py:337
  84.6 1.4 %collective-permute-done.8.refs_1_ = s16[128,128]{1,0:T(8,128)(2,1)S(1)} collective-permute-done((s16[128,128]{1,0:T(8,128)(2,1)S(1)}, s16[128,128]{1,0:T(8,128)(2,1)S(1)}, u32[]{:S(2)}, u32[]{:S(2)}) %collective-permute-start.8) | collective-permute-done | bytes 32800 | tf_op jit(solution)/shard_map/ppermute | solution.py:396
  86.1 16.1 %all_to_all.16 = s16[16,128,128]{2,1,0:T(8,128)(2,1)S(1)} all-to-all(s16[16,128,128]{2,1,0:T(8,128)(2,1)S(1)} %bitcast.10), channel_id=1, replica_groups={{0,2,4,6,128,130,132,134,256,258,260,262,384,386,388,390},{1,3,5,7,129,..., dimensions={0} | all-to-all | bytes 1048576 | tf_op jit(solution)/shard_map/all_to_all | solution.py:401
  102.2 3.8 %collective-permute-start.9 = (s16[2048,128]{1,0:T(8,128)(2,1)S(1)}, s16[2048,128]{1,0:T(8,128)(2,1)S(1)}, u32[]{:S(2)}, u32[]{:S(2)}) collective-permute-start(s16[2048,128]{1,0:T(8,128)(2,1)S(1)} %bitcast.11), channel_id=1, source_target_pairs={{0,1},{1,0},{2,3},{3,2},{4,5},{5,4},{6,7},{7,6},{8,9},{9,8},{10,11... | collective-permute-start | bytes 1572872 | tf_op jit(solution)/shard_map/ppermute | solution.py:396
  106.1 2.4 %feature_gradient.3 = (bf16[2,512,128]{2,1,0:T(8,128)(2,1)}, f32[8,128]{1,0:T(8,128)}) custom-call(s32[2]{0:T(128)S(1)} %copy-done.7, bf16[1024,128]{1,0:T(8,128)(2,1)S(1)} %get-tuple-element.29.refs_3_.refs_1_, bf16[1024,128]{1,0:T(8,128)(2,1)S(1)} %get-tuple-element.24.refs_2_, ...), custom_call_target="tpu_custom_call", output_to_operand_aliasing={{0}: (10, {})} | custom-call | flops 1811939328 | bytes 2000000 | tf_op jit(solution)/shard_map/feature_gradient/pallas_call | solution.py:337
  108.5 1.5 %place_halves.1 = f32[3456,128]{1,0:T(8,128)} custom-call(s32[1]{0:T(128)} %bitcast.1.refs_1_.core_ref, s16[2048,128]{1,0:T(8,128)(2,1)S(1)} %bitcast.13, s16[2048,128]{1,0:T(8,128)(2,1)S(1)} %collective-permute-done.9.far_ref), custom_call_target="tpu_custom_call" | custom-call | tf_op jit(solution)/shard_map/place_halves/pallas_call | solution.py:320
  (30 shorter events, 5.5 us)
Async XLA Ops:
  0.6 1.0 copy-start.2
  1.6 0.9 copy-start.3
  2.5 0.7 copy-start.4
  3.2 0.7 copy-start.5
  4.7 18.3 %collective-permute-start = (bf16[272,128]{1,0:T(8,128)(2,1)S(1)}, bf16[272,128]{1,0:T(8,128)(2,1)S(1)}, u32[]{:S(2)}, u32[]{:S(2)}) collective-permute-start(bf16[272,128]{1,0:T(8,128)(2,1)S(1)} %get-tuple-element.25), channel_id=1, source_target_pairs={{0,32},{1,33},{2,34},{3,35},{4,36},{5,37},{6,38},{7,39},{8,40},{9,... | collective-permute-start | bytes 208904 | tf_op jit(solution)/shard_map/ppermute | solution.py:391
  14.3 15.5 %collective-permute-start.1 = (bf16[272,128]{1,0:T(8,128)(2,1)S(1)}, bf16[272,128]{1,0:T(8,128)(2,1)S(1)}, u32[]{:S(2)}, u32[]{:S(2)}) collective-permute-start(bf16[272,128]{1,0:T(8,128)(2,1)S(1)} %get-tuple-element.26), channel_id=1, source_target_pairs={{32,0},{33,1},{34,2},{35,3},{36,4},{37,5},{38,6},{39,7},{40,8},{41... | collective-permute-start | bytes 208904 | tf_op jit(solution)/shard_map/ppermute | solution.py:391
  15.6 14.2 %collective-permute-start.3 = (bf16[272,128]{1,0:T(8,128)(2,1)S(1)}, bf16[272,128]{1,0:T(8,128)(2,1)S(1)}, u32[]{:S(2)}, u32[]{:S(2)}) collective-permute-start(bf16[272,128]{1,0:T(8,128)(2,1)S(1)} %get-tuple-element.28), channel_id=1, source_target_pairs={{1,0},{2,1},{3,2},{4,3},{5,4},{6,5},{7,6},{8,7},{9,8},{10,9},{11,1... | collective-permute-start | bytes 208904 | tf_op jit(solution)/shard_map/ppermute | solution.py:391
  18.5 11.3 %collective-permute-start.2 = (bf16[272,128]{1,0:T(8,128)(2,1)S(1)}, bf16[272,128]{1,0:T(8,128)(2,1)S(1)}, u32[]{:S(2)}, u32[]{:S(2)}) collective-permute-start(bf16[272,128]{1,0:T(8,128)(2,1)S(1)} %get-tuple-element.27.after_ref), channel_id=1, source_target_pairs={{0,1},{1,2},{2,3},{3,4},{4,5},{5,6},{6,7},{7,8},{8,9},{9,10},{10,1... | collective-permute-start | bytes 208904 | tf_op jit(solution)/shard_map/ppermute | solution.py:391
  21.5 1.2 %copy-start = (bf16[27,128,128]{2,1,0:T(8,128)(2,1)S(1)}, bf16[27,128,128]{2,1,0:T(8,128)(2,1)}, u32[]{:S(2)}) copy-start(bf16[27,128,128]{2,1,0:T(8,128)(2,1)} %param.8) | copy-start | bytes 2654212
  29.8 0.7 copy-start.6
  32.8 5.0 %collective-permute-start.6 = (f32[1792,128]{1,0:T(8,128)S(1)}, f32[1792,128]{1,0:T(8,128)S(1)}, u32[]{:S(2)}, u32[]{:S(2)}) collective-permute-start(f32[1792,128]{1,0:T(8,128)S(1)} %get-tuple-element.31.after_ref), channel_id=1, source_target_pairs={{0,1},{1,0},{2,3},{3,2},{4,5},{5,4},{6,7},{7,6},{8,9},{9,8},{10,11... | collective-permute-start | bytes 2752520 | tf_op jit(solution)/shard_map/ppermute | solution.py:396
  37.7 34.9 %copy-start.1 = (bf16[27,128,128]{2,1,0:T(8,128)(2,1)S(1)}, bf16[27,128,128]{2,1,0:T(8,128)(2,1)}, u32[]{:S(2)}) copy-start(bf16[27,128,128]{2,1,0:T(8,128)(2,1)} %param.8) | copy-start | bytes 2654212
  37.7 34.9 %copy-start.7 = (s32[2]{0:T(128)S(1)}, s32[2]{0:T(128)}, u32[]{:S(2)}) copy-start(s32[2]{0:T(128)} %refs_0_.11) | copy-start | bytes 28
  56.2 9.1 %all-to-all-start.1 = ((s16[4,128,128]{2,1,0:T(8,128)(2,1)}), s16[4,128,128]{2,1,0:T(8,128)(2,1)S(1)}, u32[]{:S(2)}, u32[]{:S(2)}) async-start(s16[4,128,128]{2,1,0:T(8,128)(2,1)} %bitcast.4), calls=%async_computation.1 | async-start | bytes 262144 | tf_op jit(solution)/shard_map/all_to_all | solution.py:401
  59.6 13.1 %collective-permute-start.4 = (bf16[96,128]{1,0:T(8,128)(2,1)S(1)}, bf16[96,128]{1,0:T(8,128)(2,1)S(1)}, u32[]{:S(2)}, u32[]{:S(2)}) collective-permute-start(bf16[96,128]{1,0:T(8,128)(2,1)S(1)} %get-tuple-element.32), channel_id=1, source_target_pairs={{0,1},{1,2},{2,3},{3,4},{4,5},{5,6},{6,7},{7,8},{8,9},{9,10},{10,1... | collective-permute-start | bytes 73736 | tf_op jit(solution)/shard_map/ppermute | solution.py:391
  63.4 9.2 %collective-permute-start.5 = (bf16[96,128]{1,0:T(8,128)(2,1)S(1)}, bf16[96,128]{1,0:T(8,128)(2,1)S(1)}, u32[]{:S(2)}, u32[]{:S(2)}) collective-permute-start(bf16[96,128]{1,0:T(8,128)(2,1)S(1)} %get-tuple-element.33.refs_2_), channel_id=1, source_target_pairs={{1,0},{2,1},{3,2},{4,3},{5,4},{6,5},{7,6},{8,7},{9,8},{10,9},{11,1... | collective-permute-start | bytes 73736 | tf_op jit(solution)/shard_map/ppermute | solution.py:391
  65.4 12.0 %collective-permute-start.7 = (s16[128,128]{1,0:T(8,128)(2,1)S(1)}, s16[128,128]{1,0:T(8,128)(2,1)S(1)}, u32[]{:S(2)}, u32[]{:S(2)}) collective-permute-start(s16[128,128]{1,0:T(8,128)(2,1)S(1)} %sum_blocks.5.refs_10_.refs_0_), channel_id=1, source_target_pairs={{0,32},{1,33},{2,34},{3,35},{4,36},{5,37},{6,38},{7,39},{8,40},{9,... | collective-permute-start | bytes 98312 | tf_op jit(solution)/shard_map/ppermute | solution.py:396
  77.5 8.6 %collective-permute-start.8 = (s16[128,128]{1,0:T(8,128)(2,1)S(1)}, s16[128,128]{1,0:T(8,128)(2,1)S(1)}, u32[]{:S(2)}, u32[]{:S(2)}) collective-permute-start(s16[128,128]{1,0:T(8,128)(2,1)S(1)} %sum_blocks.6.refs_10_.refs_0_), channel_id=1, source_target_pairs={{0,96},{1,97},{2,98},{3,99},{4,100},{5,101},{6,102},{7,103},{8,104... | collective-permute-start | bytes 98312 | tf_op jit(solution)/shard_map/ppermute | solution.py:396
  102.2 6.2 %collective-permute-start.9 = (s16[2048,128]{1,0:T(8,128)(2,1)S(1)}, s16[2048,128]{1,0:T(8,128)(2,1)S(1)}, u32[]{:S(2)}, u32[]{:S(2)}) collective-permute-start(s16[2048,128]{1,0:T(8,128)(2,1)S(1)} %bitcast.11), channel_id=1, source_target_pairs={{0,1},{1,0},{2,3},{3,2},{4,5},{5,4},{6,7},{7,6},{8,9},{9,8},{10,11... | collective-permute-start | bytes 1572872 | tf_op jit(solution)/shard_map/ppermute | solution.py:396

commit v4 on v3

--- a/solution.py
+++ b/solution.py
@@ -32,15 +32,9 @@
 Z_HI_BITS = (32, 96)
 
 
-def tags(pos_ref):
-    return jnp.concatenate(
-        [jnp.full((BE, C), pos_ref[s].astype(jnp.float32), jnp.float32) for s in range(BLK_DEV)]
-    ).astype(jnp.bfloat16)
-
-
 def prep_kernel(*refs):
-    sources, outs, held, sems = refs[:4], refs[4:11], refs[11:15], refs[15]
-    in_ref, g_ref, mask_ref, xlo_ref, xhi_ref, ylo_ref, yhi_ref = outs
+    sources, outs, held, sems = refs[:4], refs[4:12], refs[12:16], refs[16]
+    in_ref, g_ref, mask_ref, tag_ref, xlo_ref, xhi_ref, ylo_ref, yhi_ref = outs
     copies = [pltpu.make_async_copy(src, dst, sems.at[i]) for i, (src, dst) in enumerate(zip(sources, held))]
     for copy in copies:
         copy.start()
@@ -49,8 +43,12 @@
     pos_ref, occ_ref, feat_ref, grad_ref = held
     occ = occ_ref[...].astype(jnp.float32)
     layer = BE * BE
+    tag = jnp.concatenate(
+        [jnp.full((BE, C), pos_ref[s].astype(jnp.float32), jnp.float32) for s in range(BLK_DEV)]
+    ).astype(jnp.bfloat16)
+    tag_ref[...] = tag
     for face in (xlo_ref, xhi_ref, ylo_ref, yhi_ref):
-        face[FACE:FACE + TAG, :] = tags(pos_ref)
+        face[FACE:FACE + TAG, :] = tag
     for s in range(BLK_DEV):
         live = (pos_ref[s] >= 0).astype(jnp.float32)
         mask = jnp.concatenate([
@@ -68,7 +66,7 @@
                 face[at:at + layer, :] = piece.reshape(layer, C).astype(jnp.bfloat16)
 
 
-def edges_kernel(low_ref, high_ref, after_ref, ylo_ref, yhi_ref):
+def edges_kernel(low_ref, high_ref, ylo_ref, yhi_ref):
     layer = BE * BE
     for side, ref in enumerate((low_ref, high_ref)):
         faces = [ref[n * layer:(n + 1) * layer, :].astype(jnp.float32) for n in range(2 * BLK_DEV)]
@@ -106,14 +104,17 @@
     return value
 
 
-def fill_windows(field, slots, pos_ref, own_ref, x_from, y_from, c_from, z_ref, a_ref):
+def fill_windows(field, slots, tag_ref, own_ref, x_from, y_from, c_from, z_ref, a_ref):
     regions = []
     own = [own_ref[n * VOX:(n + 1) * VOX, :].astype(jnp.float32).reshape(BE, BE, BE, C) for n in range(BLK_DEV)]
-    own_tags = [jnp.full((BE, C), pos_ref[n].astype(jnp.float32), jnp.float32) for n in range(BLK_DEV)]
+    own_tags = tags_of(tag_ref, 0)
     inside = slice(1, BE + 1)
     ends = (slice(0, 1), slice(WIN - 1, WIN))
     regions.append((inside, inside, own, own_tags))
     for ref, end in zip(x_from, ends):
+        if ref is None:
+            z_ref[:, end, inside] = jnp.zeros((3, 1, BE, BE, C), jnp.float32)
+            continue
         regions.append((end, inside, face_of(ref, field, (1, BE, BE, C)), tags_of(ref, FACE)))
     for ref, end in zip(y_from, ends):
         regions.append((inside, end, face_of(ref, field, (BE, 1, BE, C)), tags_of(ref, FACE)))
@@ -129,7 +130,7 @@
                 z_ref[:, x, y] = jnp.zeros((3, 1, 1, BE, C), jnp.float32)
 
     for i, s in enumerate(slots):
-        here = pos_ref[s].astype(jnp.float32)
+        here = own_tags[s]
         for xs, ys, data, their_tags in regions:
             flat = [v.reshape(-1, BE, C) for v in data]
             for o3 in range(3):
@@ -141,35 +142,55 @@
                 a_ref[i, :, j * C:(j + 1) * C] = piece.astype(jnp.bfloat16)
 
 
-def diagonal_pairs(x_high, y_low, y_high):
+def lower_pairs(tag_ref, g_ref, x_low, y_low, y_high):
+    last = BE - 1
+    blank = jnp.zeros((1, BE, C), jnp.float32)
+
     def column(ref, field, end):
         return [v[:, end] for v in face_of(ref, field, (1, BE, BE, C))]
 
-    last = BE - 1
-    plans = {
-        0: (((x_high, 0), (y_low, last), 0), ((x_high, last), (y_high, last), 2)),
-        2: (((y_low, last), (x_high, 0), 2), ((y_high, last), (x_high, last), 0)),
-    }
+    inputs, rows = {0: [], 2: []}, {0: [], 2: []}
+    own_tags = tags_of(tag_ref, 0)
+    plane = [
+        g_ref[n * VOX:n * VOX + BE * BE, :].astype(jnp.float32).reshape(BE, BE, C) for n in range(BLK_DEV)
+    ]
+    inputs[2] += face_of(x_low, 0, (BE * BE, C))
+    for here in tags_of(x_low, FACE):
+        lanes = []
+        above = [
+            jnp.concatenate([blank, picked(plane, own_tags, here, e3), blank]) for e3 in range(3)
+        ]
+        for e2 in range(3):
+            lanes += [above[e3][e2:e2 + BE].reshape(BE * BE, C) for e3 in range(3)]
+        rows[2].append(jnp.concatenate(lanes, axis=1))
+    plans = (
+        (2, 2, (x_low, last), (y_high, 0)),
+        (2, 0, (x_low, 0), (y_low, 0)),
+        (0, 0, (y_high, 0), (x_low, last)),
+        (0, 2, (y_low, 0), (x_low, 0)),
+    )
+    for e1, e2, (near, near_end), (far, far_end) in plans:
+        inputs[e1] += [v.reshape(BE, C) for v in column(near, 0, near_end)]
+        data, their_tags = column(far, 1, far_end), tags_of(far, FACE)
+        for here in tags_of(near, FACE):
+            lanes = [blank.reshape(BE, C)] * 9
+            for e3 in range(3):
+                lanes[3 * e2 + e3] = picked(data, their_tags, here, e3).reshape(BE, C)
+            rows[e1].append(jnp.concatenate(lanes, axis=1))
     result = {}
-    for e1, plan in plans.items():
-        inputs, rows = [], []
-        for (near, near_end), (far, far_end), e2 in plan:
-            inputs += [v.reshape(BE, C) for v in column(near, 0, near_end)]
-            data, their_tags = column(far, 1, far_end), tags_of(far, FACE)
-            for here in tags_of(near, FACE):
-                blank = jnp.zeros((BE, C), jnp.float32)
-                lanes = [blank] * 9
-                for e3 in range(3):
-                    lanes[3 * e2 + e3] = picked(data, their_tags, here, e3).reshape(BE, C)
-                rows.append(jnp.concatenate(lanes, axis=1))
-        result[e1] = (jnp.concatenate(inputs), jnp.concatenate(rows).astype(jnp.bfloat16))
+    for e1 in inputs:
+        lhs, rhs = jnp.concatenate(inputs[e1]), jnp.concatenate(rows[e1])
+        more = -lhs.shape[0] % C
+        lhs = jnp.concatenate([lhs, jnp.zeros((more, C), jnp.float32)])
+        rhs = jnp.concatenate([rhs, jnp.zeros((more, SIDE), jnp.float32)])
+        result[e1] = (lhs.T.astype(jnp.bfloat16), rhs.astype(jnp.bfloat16))
     return result
 
 
-def wgrad_kernel(scale, pos_ref, core_ref, in_ref, g_ref, *refs):
-    halo, keep_ref, send_ref, z_ref, a_ref, total_ref = refs[:4], *refs[-5:]
-    fill_windows(1, (0, 1), pos_ref, g_ref, halo[0:2], halo[2:4], (), z_ref, a_ref)
-    pairs = diagonal_pairs(halo[1], halo[2], halo[3])
+def wgrad_kernel(scale, tag_ref, core_ref, in_ref, g_ref, *refs):
+    halo, keep_ref, send_ref, z_ref, a_ref, total_ref = refs[:3], *refs[-5:]
+    fill_windows(1, (0, 1), tag_ref, g_ref, (halo[0], None), halo[1:3], (), z_ref, a_ref)
+    pairs = lower_pairs(tag_ref, g_ref, *halo)
     inner = [
         jnp.transpose(in_ref[s * VOX:(s + 1) * VOX, :].astype(jnp.float32)).astype(jnp.bfloat16)
         for s in range(BLK_DEV)
@@ -180,10 +201,7 @@
         total = jnp.dot(inner[0], a_ref[0, rows, :], preferred_element_type=jnp.float32)
         total = total + jnp.dot(inner[1], a_ref[1, rows, :], preferred_element_type=jnp.float32)
         if e1 in pairs:
-            lhs, rhs = pairs[e1]
-            lhs = jnp.concatenate([lhs, jnp.zeros((C - lhs.shape[0], C), jnp.float32)])
-            rhs = jnp.concatenate([rhs, jnp.zeros((C - rhs.shape[0], SIDE), jnp.bfloat16)])
-            total = total + jnp.dot(lhs.T.astype(jnp.bfloat16), rhs, preferred_element_type=jnp.float32)
+            total = total + jnp.dot(*pairs[e1], preferred_element_type=jnp.float32)
         total = total * scale
         for j in range(9):
             k = KV - 1 - (9 * e1 + j)
@@ -206,7 +224,7 @@
     return code[:CHUNK] * (jnp.exp2(code[CHUNK:CHUNK + 1]) * (1.0 / STEPS))
 
 
-def place_kernel(core_ref, near_ref, far_ref, out_ref):
+def place_kernel(core_ref, near_ref, far_ref, after_ref, out_ref):
     first = core_ref[0] == 0
     for block in range(16):
         near, far = decoded(near_ref, block), decoded(far_ref, block)
@@ -224,9 +242,9 @@
     done_ref[...] = jnp.zeros_like(done_ref)
 
 
-def conv_kernel(field, slot, pos_ref, own_ref, mask_ref, w_ref, *refs):
+def conv_kernel(field, slot, tag_ref, own_ref, mask_ref, w_ref, *refs):
     halo, out_ref, done_ref, z_ref, a_ref = refs[:6], *refs[-4:]
-    fill_windows(field, (slot,), pos_ref, own_ref, halo[0:2], halo[2:4], halo[4:6], z_ref, a_ref)
+    fill_windows(field, (slot,), tag_ref, own_ref, halo[0:2], halo[2:4], halo[4:6], z_ref, a_ref)
     total = None
     for e1 in range(3):
         rows = slice(e1 * BE * BE, e1 * BE * BE + VOX)
@@ -253,9 +271,9 @@
     field = pltpu.VMEM((BLK_DEV, VOX, C), jnp.bfloat16)
     return pl.pallas_call(
         prep_kernel,
-        out_shape=[bf16(BLK_DEV * VOX, C)] * 3 + [bf16(FACE + TAG, C)] * 4,
+        out_shape=[bf16(BLK_DEV * VOX, C)] * 3 + [bf16(TAG, C)] + [bf16(FACE + TAG, C)] * 4,
         in_specs=[pl.BlockSpec(memory_space=pltpu.HBM)] * 4,
-        out_specs=[VMEM] * 7,
+        out_specs=[VMEM] * 8,
         scratch_shapes=[
             pltpu.SMEM((BLK_DEV,), jnp.int32),
             pltpu.VMEM((BLK_DEV, VOX), jnp.int32),
@@ -265,18 +283,18 @@
         ],
         compiler_params=PARAMS,
         name="mask_and_faces",
-    )(block_pos, occupancy, features, out_grad)
-
-
-def edges(low, high, after):
+    )(*[pltpu.with_memory_space_constraint(v, pltpu.HBM) for v in (block_pos, occupancy, features, out_grad)])
+
+
+def edges(low, high):
     return pl.pallas_call(
         edges_kernel,
         out_shape=[bf16(2 * EDGE + 2 * TAG, C)] * 2,
-        in_specs=[VMEM] * 2 + [ANY],
+        in_specs=[VMEM] * 2,
         out_specs=[VMEM] * 2,
         compiler_params=PARAMS,
         name="edges",
-    )(low, high, after)
+    )(low, high)
 
 
 def turn(weights, after):
@@ -300,7 +318,7 @@
     ]
 
 
-def wgrad(scale, block_pos, core, own_in, own_grad, halo, after):
+def wgrad(scale, tag, core, own_in, own_grad, halo, *after):
     def kernel(*refs):
         wgrad_kernel(scale, *refs)
 
@@ -308,37 +326,37 @@
     return pl.pallas_call(
         kernel,
         out_shape=[half, half],
-        in_specs=[SMEM] * 2 + [VMEM] * 6 + [ANY],
+        in_specs=[VMEM, SMEM] + [VMEM] * 5 + [ANY] * len(after),
         out_specs=[VMEM] * 2,
         scratch_shapes=scratch(BLK_DEV) + [pltpu.VMEM((2 * HALF, C), jnp.float32)],
         compiler_params=PARAMS,
         name="kernel_gradient",
-    )(block_pos, core, own_in, own_grad, *halo, after)
-
-
-def place(core, near, far):
+    )(tag, core, own_in, own_grad, *halo, *after)
+
+
+def place(core, near, far, after):
     return pl.pallas_call(
         place_kernel,
         out_shape=jax.ShapeDtypeStruct((KV * C, C), jnp.float32),
-        in_specs=[SMEM] + [VMEM] * 2,
+        in_specs=[SMEM] + [VMEM] * 2 + [ANY],
         out_specs=VMEM,
         compiler_params=PARAMS,
         name="place_halves",
-    )(core, near, far)
-
-
-def conv(field, slot, block_pos, own, mask, weights, halo, before, after):
+    )(core, near, far, after)
+
+
+def conv(field, slot, tag, own, mask, weights, halo, before, after):
     def kernel(*refs):
         conv_kernel(field, slot, *refs)
 
     flops = 2 * KV * VOX * C * C
-    args = (block_pos, own, mask, weights, *halo)
+    args = (tag, own, mask, weights, *halo)
     extra = ([] if before is None else [before]) + list(after)
     return pl.pallas_call(
         kernel,
         grid=(1,),
         out_shape=[bf16(BLK_DEV, VOX, C), jax.ShapeDtypeStruct((BE, C), jnp.float32)],
-        in_specs=[SMEM] + [VMEM] * (len(args) - 1) + [ANY] * len(extra),
+        in_specs=[VMEM] * len(args) + [ANY] * len(extra),
         out_specs=[pl.BlockSpec((1, VOX, C), lambda i: (slot, 0, 0)), VMEM],
         scratch_shapes=scratch(1),
         input_output_aliases={} if before is None else {len(args): 0},
@@ -405,26 +423,26 @@
 def body(features, occupancy, block_pos, kernel, out_grad):
     groups, tiles = lax.axis_size("group"), lax.axis_size("tile")
     core = (lax.axis_index("tile") & 1).astype(jnp.int32).reshape(1)
-    own_in, own_grad, mask, xlo, xhi, ylo, yhi = prep(block_pos, occupancy, features, out_grad)
-    x_from = (shifted(xhi, groups, tiles, 1, 0), shifted(xlo, groups, tiles, -1, 0))
+    own_in, own_grad, mask, tag, xlo, xhi, ylo, yhi = prep(block_pos, occupancy, features, out_grad)
+    from_low = shifted(xhi, groups, tiles, 1, 0)
     y_from = (shifted(yhi, groups, tiles, 0, 1), shifted(ylo, groups, tiles, 0, -1))
-    halo = (*x_from, *y_from)
     weights = kernel.reshape(KV * C, C)
     turned, done = turn(weights, yhi)
     scale = 1.0 / math.sqrt(groups * tiles * BLK_DEV * VOX)
-    keep, send = wgrad(scale, block_pos, core, own_in, own_grad, halo, done)
 
     def convolved(field, slot, before, *after):
         return conv(
-            field, slot, block_pos, (own_in, own_grad)[field], mask, (weights, turned)[field],
-            halo, before, after,
+            field, slot, tag, (own_in, own_grad)[field], mask, (weights, turned)[field], halo, before, after
         )
 
+    x_from = (from_low, shifted(xlo, groups, tiles, -1, 0))
+    clo, chi = edges(*x_from)
+    c_from = (shifted(chi, groups, tiles, 0, 1), shifted(clo, groups, tiles, 0, -1))
+    halo = (*x_from, *y_from, *c_from)
+    keep, send = wgrad(scale, tag, core, own_in, own_grad, (from_low, *y_from), done, clo)
     got = across(send, CORE)
-    clo, chi = edges(*x_from, send)
-    halo += (shifted(chi, groups, tiles, 0, 1), shifted(clo, groups, tiles, 0, -1))
-    value, = small(sum_halves_kernel, [16 * CODED], [keep, got], [clo])
-    value, = small(sum_blocks_kernel, [4 * CODED], [exchange(value, AXES, XY_SETS)])
+    value, = small(sum_halves_kernel, [16 * CODED], [keep, got])
+    value, = small(sum_blocks_kernel, [4 * CODED], [exchange(value, AXES, XY_SETS)], c_from)
     value, = small(sum_blocks_kernel, [CODED], [exchange(value, "tile", Z_LO_SETS)])
     got = across(value, Z_HI_BITS[0])
     conv_out, done = convolved(0, 0, None, value)
@@ -436,7 +454,7 @@
     value = exchange(value, AXES, XY_SETS)
     got = across(value, CORE)
     feature_grad, done = convolved(1, 1, feature_grad, value)
-    total = place(core, value, got)
+    total = place(core, value, got, done)
     return (conv_out, feature_grad, total.reshape(KV, C, C))
 
 

time: 111 us -> 105 us (0.946)
  blocking collectives: 33.4 us -> 23.2 us
  waiting for transfers between devices: 10.3 us -> 15.6 us
  starting transfers between devices: 44.5 us -> 49.4 us
  local copies, waits for them, and re-layouts: 5.06 us -> 1.17 us
  Pallas kernels: 15.8 us -> 13.8 us
    all_to_all x2, blocking collectives: 33.4 us -> 23.2 us  [exchange(): lax.all_to_all(value.reshape(count, -1, C), axis, 0, 0, axis_index_groups...]
    unnamed x16 -> x4, local copies, waits for them, and re-layouts: 5.06 us -> 1.17 us
    ppermute x6, waiting for transfers between devices: 6.78 us -> 10.3 us  [shifted(): return lax.ppermute(value, AXES, pairs)]
    all_to_all x1, starting transfers between devices: 3.33 us -> 6.8 us  [exchange(): lax.all_to_all(value.reshape(count, -1, C), axis, 0, 0, axis_index_groups...]
    pallas_call x4, Pallas kernels: 9.51 us -> 7.38 us  [conv(): pl.pallas_call(kernel, grid=(1,), out_shape=[bf16(BLK_DEV, VOX, C), jax.S...]
    ppermute x4, starting transfers between devices: 18.6 us -> 19.8 us  [across(): return lax.ppermute(value, AXES, [(i, i ^ mask) for i in range(count)])]
    all_to_all x1, waiting for transfers between devices: 0.01 us -> 1.18 us  [exchange(): lax.all_to_all(value.reshape(count, -1, C), axis, 0, 0, axis_index_groups...]
  transfers between devices with their start and end apart: 11 -> 11, of which waited for: 3 -> 5; matrix products, arithmetic and copies ran while one was open for 0% -> 0% of each run, Pallas kernels for 9% -> 7%
where the time goes in v4:
time: 105 us; the launch traced here: 104 us
  starting transfers between devices  49.4 us (47%)
  blocking collectives  23.2 us (22%)
  waiting for transfers between devices  15.6 us (15%)
  Pallas kernels  13.8 us (13%)
  local copies, waits for them, and re-layouts  1.17 us (1%)
    all_to_all x2, blocking collectives, exchange(): lax.all_to_all(value.reshape(count, -1, C), axis, 0, 0, axis_index_groups...  23.2 us
    ppermute x6, starting transfers between devices, shifted(): return lax.ppermute(value, AXES, pairs)  22.8 us
    ppermute x4, starting transfers between devices, across(): return lax.ppermute(value, AXES, [(i, i ^ mask) for i in range(count)])  19.8 us
    ppermute x6, waiting for transfers between devices, shifted(): return lax.ppermute(value, AXES, pairs)  10.3 us
    pallas_call x4, Pallas kernels, conv(): pl.pallas_call(kernel, grid=(1,), out_shape=[bf16(BLK_DEV, VOX, C), jax.S...  7.38 us
    all_to_all x1, starting transfers between devices, exchange(): lax.all_to_all(value.reshape(count, -1, C), axis, 0, 0, axis_index_groups...  6.8 us
    ppermute x4, waiting for transfers between devices, across(): return lax.ppermute(value, AXES, [(i, i ^ mask) for i in range(count)])  4.19 us
  transfers between devices with their start and end apart: 11, of which 5 were waited for; matrix products, arithmetic and copies ran while one was open for 0% of the time, Pallas kernels for 7%

profile of v4, /device:TPU:1, one launch (start us, length us, event | category | flops | bytes accessed | tf_op | source)
XLA Modules:
  0.0 104.1 jit_solution(8180639274347745710)
XLA Ops:
  0.6 1.3 %mask_and_faces.1 = (bf16[1024,128]{1,0:T(8,128)(2,1)S(1)}, bf16[1024,128]{1,0:T(8,128)(2,1)S(1)}, bf16[1024,128]{1,0:T(8,128)(2,1)S(1)}, bf16[16,128]{1,0:T(8,1...) custom-call(s32[2]{0:T(128)} %refs_0_.1, ...), custom_call_target="tpu_custom_call" | custom-call | tf_op jit(solution)/shard_map/mask_and_faces/pallas_call | solution.py:272
  1.9 9.6 %collective-permute-start = (bf16[272,128]{1,0:T(8,128)(2,1)S(1)}, bf16[272,128]{1,0:T(8,128)(2,1)S(1)}, u32[]{:S(2)}, u32[]{:S(2)}) collective-permute-start(bf16[272,128]{1,0:T(8,128)(2,1)S(1)} %get-tuple-element.28), channel_id=1, source_target_pairs={{0,32},{1,33},{2,34},{3,35},{4,36},{5,37},{6,38},{7,39},{8,40},{9,... | collective-permute-start | bytes 208904 | tf_op jit(solution)/shard_map/ppermute | solution.py:409
  11.6 1.3 %collective-permute-start.1 = (bf16[272,128]{1,0:T(8,128)(2,1)S(1)}, bf16[272,128]{1,0:T(8,128)(2,1)S(1)}, u32[]{:S(2)}, u32[]{:S(2)}) collective-permute-start(bf16[272,128]{1,0:T(8,128)(2,1)S(1)} %get-tuple-element.29), channel_id=1, source_target_pairs={{32,0},{33,1},{34,2},{35,3},{36,4},{37,5},{38,6},{39,7},{40,8},{41... | collective-permute-start | bytes 208904 | tf_op jit(solution)/shard_map/ppermute | solution.py:409
  12.9 2.9 %collective-permute-start.3 = (bf16[272,128]{1,0:T(8,128)(2,1)S(1)}, bf16[272,128]{1,0:T(8,128)(2,1)S(1)}, u32[]{:S(2)}, u32[]{:S(2)}) collective-permute-start(bf16[272,128]{1,0:T(8,128)(2,1)S(1)} %get-tuple-element.31), channel_id=1, source_target_pairs={{1,0},{2,1},{3,2},{4,3},{5,4},{6,5},{7,6},{8,7},{9,8},{10,9},{11,1... | collective-permute-start | bytes 208904 | tf_op jit(solution)/shard_map/ppermute | solution.py:409
  15.8 3.0 %collective-permute-start.2 = (bf16[272,128]{1,0:T(8,128)(2,1)S(1)}, bf16[272,128]{1,0:T(8,128)(2,1)S(1)}, u32[]{:S(2)}, u32[]{:S(2)}) collective-permute-start(bf16[272,128]{1,0:T(8,128)(2,1)S(1)} %get-tuple-element.30.after_ref), channel_id=1, source_target_pairs={{0,1},{1,2},{2,3},{3,4},{4,5},{5,6},{6,7},{7,8},{8,9},{9,10},{10,1... | collective-permute-start | bytes 208904 | tf_op jit(solution)/shard_map/ppermute | solution.py:409
  20.3 6.8 %collective-permute-done.1.high_ref.refs_5_ = bf16[272,128]{1,0:T(8,128)(2,1)S(1)} collective-permute-done((bf16[272,128]{1,0:T(8,128)(2,1)S(1)}, bf16[272,128]{1,0:T(8,128)(2,1)S(1)}, u32[]{:S(2)}, u32[]{:S(2)}) %collective-permute-start.1) | collective-permute-done | bytes 69664 | tf_op jit(solution)/shard_map/ppermute | solution.py:409
  27.1 1.9 %kernel_gradient.1 = (f32[1792,128]{1,0:T(8,128)S(1)}, f32[1792,128]{1,0:T(8,128)S(1)}) custom-call(bf16[16,128]{1,0:T(8,128)(2,1)S(1)} %get-tuple-element.25.refs_0_, s32[1]{0:T(128)} %bitcast.1.refs_1_.core_ref, bf16[1024,128]{1,0:T(8,128)(2,1)S(1)} %get-tuple-element.26.refs_2_.refs_1_, bf16[1024,128]{1,0:T(8,128)(2,1)S(1)} %get-tuple-element.34.refs_3_.refs_1_, ...), custom_call_target="tpu_custom_call" | custom-call | tf_op jit(solution)/shard_map/kernel_gradient/pallas_call | solution.py:326
  28.9 2.9 %collective-permute-start.6 = (f32[1792,128]{1,0:T(8,128)S(1)}, f32[1792,128]{1,0:T(8,128)S(1)}, u32[]{:S(2)}, u32[]{:S(2)}) collective-permute-start(f32[1792,128]{1,0:T(8,128)S(1)} %get-tuple-element.37), channel_id=1, source_target_pairs={{0,1},{1,0},{2,3},{3,2},{4,5},{5,4},{6,7},{7,6},{8,9},{9,8},{10,11... | collective-permute-start | bytes 2752520 | tf_op jit(solution)/shard_map/ppermute | solution.py:414
  31.8 2.1 %collective-permute-done.6.refs_1_ = f32[1792,128]{1,0:T(8,128)S(1)} collective-permute-done((f32[1792,128]{1,0:T(8,128)S(1)}, f32[1792,128]{1,0:T(8,128)S(1)}, u32[]{:S(2)}, u32[]{:S(2)}) %collective-permute-start.6) | collective-permute-done | bytes 917536 | tf_op jit(solution)/shard_map/ppermute | solution.py:414
  35.0 6.8 %all-to-all-start = ((s16[16,128,128]{2,1,0:T(8,128)(2,1)}), s16[16,128,128]{2,1,0:T(8,128)(2,1)S(1)}, u32[]{:S(2)}, u32[]{:S(2)}) async-start(s16[16,128,128]{2,1,0:T(8,128)(2,1)} %bitcast.2), calls=%async_computation | async-start | bytes 1048576 | tf_op jit(solution)/shard_map/all_to_all | solution.py:419
  41.8 4.1 %collective-permute-start.4 = (bf16[96,128]{1,0:T(8,128)(2,1)S(1)}, bf16[96,128]{1,0:T(8,128)(2,1)S(1)}, u32[]{:S(2)}, u32[]{:S(2)}) collective-permute-start(bf16[96,128]{1,0:T(8,128)(2,1)S(1)} %get-tuple-element.32), channel_id=1, source_target_pairs={{0,1},{1,2},{2,3},{3,4},{4,5},{5,6},{6,7},{7,8},{8,9},{9,10},{10,1... | collective-permute-start | bytes 73736 | tf_op jit(solution)/shard_map/ppermute | solution.py:409
  45.9 1.9 %collective-permute-start.5 = (bf16[96,128]{1,0:T(8,128)(2,1)S(1)}, bf16[96,128]{1,0:T(8,128)(2,1)S(1)}, u32[]{:S(2)}, u32[]{:S(2)}) collective-permute-start(bf16[96,128]{1,0:T(8,128)(2,1)S(1)} %get-tuple-element.33.refs_8_), channel_id=1, source_target_pairs={{1,0},{2,1},{3,2},{4,3},{5,4},{6,5},{7,6},{8,7},{9,8},{10,9},{11,1... | collective-permute-start | bytes 73736 | tf_op jit(solution)/shard_map/ppermute | solution.py:409
  47.8 3.5 %collective-permute-done.5.refs_2_.refs_9_ = bf16[96,128]{1,0:T(8,128)(2,1)S(1)} collective-permute-done((bf16[96,128]{1,0:T(8,128)(2,1)S(1)}, bf16[96,128]{1,0:T(8,128)(2,1)S(1)}, u32[]{:S(2)}, u32[]{:S(2)}) %collective-permute-start.5) | collective-permute-done | bytes 24608 | tf_op jit(solution)/shard_map/ppermute | solution.py:409
  52.7 7.2 %all_to_all.15 = s16[4,128,128]{2,1,0:T(8,128)(2,1)S(1)} all-to-all(s16[4,128,128]{2,1,0:T(8,128)(2,1)S(1)} %bitcast.18), channel_id=1, replica_groups={{0,8,16,24},{1,9,17,25},{2,10,18,26},{3,11,19,27},{4,12,20,28},{5,13,21..., dimensions={0} | all-to-all | bytes 262144 | tf_op jit(solution)/shard_map/all_to_all | solution.py:419
  60.0 7.6 %collective-permute-start.7 = (s16[128,128]{1,0:T(8,128)(2,1)S(1)}, s16[128,128]{1,0:T(8,128)(2,1)S(1)}, u32[]{:S(2)}, u32[]{:S(2)}) collective-permute-start(s16[128,128]{1,0:T(8,128)(2,1)S(1)} %sum_blocks.5.refs_10_.refs_0_), channel_id=1, source_target_pairs={{0,32},{1,33},{2,34},{3,35},{4,36},{5,37},{6,38},{7,39},{8,40},{9,... | collective-permute-start | bytes 98312 | tf_op jit(solution)/shard_map/ppermute | solution.py:414
  67.6 1.8 %convolution.2 = (bf16[2,512,128]{2,1,0:T(8,128)(2,1)}, f32[8,128]{1,0:T(8,128)S(1)}) custom-call(bf16[16,128]{1,0:T(8,128)(2,1)S(1)} %get-tuple-element.25.refs_0_, bf16[1024,128]{1,0:T(8,128)(2,1)S(1)} %get-tuple-element.26.refs_2_.refs_1_, bf16[1024,128]{1,0:T(8,128)(2,1)S(1)} %get-tuple-element.27.refs_2_, bf16[3456,128]{1,0:T(8,128)(2,1)S(1)} %bitcast.15, ...), custom_call_target="tpu_custom_call" | custom-call | flops 1811939328 | bytes 2000000 | tf_op jit(solution)/shard_map/convolution/pallas_call | solution.py:355
  69.5 1.8 %convolution.3 = (bf16[2,512,128]{2,1,0:T(8,128)(2,1)}, f32[8,128]{1,0:T(8,128)S(1)}) custom-call(bf16[16,128]{1,0:T(8,128)(2,1)S(1)} %get-tuple-element.25.refs_0_, bf16[1024,128]{1,0:T(8,128)(2,1)S(1)} %get-tuple-element.26.refs_2_.refs_1_, bf16[1024,128]{1,0:T(8,128)(2,1)S(1)} %get-tuple-element.27.refs_2_, ...), custom_call_target="tpu_custom_call", output_to_operand_aliasing={{0}: (10, {})} | custom-call | flops 1811939328 | bytes 2000000 | tf_op jit(solution)/shard_map/convolution/pallas_call | solution.py:355
  71.4 4.7 %collective-permute-start.8 = (s16[128,128]{1,0:T(8,128)(2,1)S(1)}, s16[128,128]{1,0:T(8,128)(2,1)S(1)}, u32[]{:S(2)}, u32[]{:S(2)}) collective-permute-start(s16[128,128]{1,0:T(8,128)(2,1)S(1)} %sum_blocks.6.refs_10_.refs_0_), channel_id=1, source_target_pairs={{0,96},{1,97},{2,98},{3,99},{4,100},{5,101},{6,102},{7,103},{8,104... | collective-permute-start | bytes 98312 | tf_op jit(solution)/shard_map/ppermute | solution.py:414
  76.1 1.9 %feature_gradient.2 = (bf16[2,512,128]{2,1,0:T(8,128)(2,1)}, f32[8,128]{1,0:T(8,128)S(1)}) custom-call(bf16[16,128]{1,0:T(8,128)(2,1)S(1)} %get-tuple-element.25.refs_0_, bf16[1024,128]{1,0:T(8,128)(2,1)S(1)} %get-tuple-element.34.refs_3_.refs_1_, bf16[1024,128]{1,0:T(8,128)(2,1)S(1)} %get-tuple-element.27.refs_2_, ...), custom_call_target="tpu_custom_call" | custom-call | flops 1811939328 | bytes 2000000 | tf_op jit(solution)/shard_map/feature_gradient/pallas_call | solution.py:355
  77.9 2.1 %collective-permute-done.8.refs_1_ = s16[128,128]{1,0:T(8,128)(2,1)S(1)} collective-permute-done((s16[128,128]{1,0:T(8,128)(2,1)S(1)}, s16[128,128]{1,0:T(8,128)(2,1)S(1)}, u32[]{:S(2)}, u32[]{:S(2)}) %collective-permute-start.8) | collective-permute-done | bytes 32800 | tf_op jit(solution)/shard_map/ppermute | solution.py:414
  80.1 16.0 %all_to_all.16 = s16[16,128,128]{2,1,0:T(8,128)(2,1)S(1)} all-to-all(s16[16,128,128]{2,1,0:T(8,128)(2,1)S(1)} %bitcast.10), channel_id=1, replica_groups={{0,2,4,6,128,130,132,134,256,258,260,262,384,386,388,390},{1,3,5,7,129,..., dimensions={0} | all-to-all | bytes 1048576 | tf_op jit(solution)/shard_map/all_to_all | solution.py:419
  96.2 4.6 %collective-permute-start.9 = (s16[2048,128]{1,0:T(8,128)(2,1)S(1)}, s16[2048,128]{1,0:T(8,128)(2,1)S(1)}, u32[]{:S(2)}, u32[]{:S(2)}) collective-permute-start(s16[2048,128]{1,0:T(8,128)(2,1)S(1)} %bitcast.11), channel_id=1, source_target_pairs={{0,1},{1,0},{2,3},{3,2},{4,5},{5,4},{6,7},{7,6},{8,9},{9,8},{10,11... | collective-permute-start | bytes 1572872 | tf_op jit(solution)/shard_map/ppermute | solution.py:414
  100.7 1.9 %feature_gradient.3 = (bf16[2,512,128]{2,1,0:T(8,128)(2,1)}, f32[8,128]{1,0:T(8,128)S(1)}) custom-call(bf16[16,128]{1,0:T(8,128)(2,1)S(1)} %get-tuple-element.25.refs_0_, bf16[1024,128]{1,0:T(8,128)(2,1)S(1)} %get-tuple-element.34.refs_3_.refs_1_, bf16[1024,128]{1,0:T(8,128)(2,1)S(1)} %get-tuple-element.27.refs_2_, ...), custom_call_target="tpu_custom_call", output_to_operand_aliasing={{0}: (10, {})} | custom-call | flops 1811939328 | bytes 2000000 | tf_op jit(solution)/shard_map/feature_gradient/pallas_call | solution.py:355
  102.6 1.5 %place_halves.1 = f32[3456,128]{1,0:T(8,128)} custom-call(s32[1]{0:T(128)} %bitcast.1.refs_1_.core_ref, s16[2048,128]{1,0:T(8,128)(2,1)S(1)} %bitcast.13, s16[2048,128]{1,0:T(8,128)(2,1)S(1)} %collective-permute-done.9.far_ref, f32[8,128]{1,0:T(8,128)S(1)} %get-tuple-element.46.after_ref), custom_call_target="tpu_custom_call" | custom-call | tf_op jit(solution)/shard_map/place_halves/pallas_call | solution.py:338
  (18 shorter events, 4.2 us)
Async XLA Ops:
  1.9 18.3 %collective-permute-start = (bf16[272,128]{1,0:T(8,128)(2,1)S(1)}, bf16[272,128]{1,0:T(8,128)(2,1)S(1)}, u32[]{:S(2)}, u32[]{:S(2)}) collective-permute-start(bf16[272,128]{1,0:T(8,128)(2,1)S(1)} %get-tuple-element.28), channel_id=1, source_target_pairs={{0,32},{1,33},{2,34},{3,35},{4,36},{5,37},{6,38},{7,39},{8,40},{9,... | collective-permute-start | bytes 208904 | tf_op jit(solution)/shard_map/ppermute | solution.py:409
  11.6 15.5 %collective-permute-start.1 = (bf16[272,128]{1,0:T(8,128)(2,1)S(1)}, bf16[272,128]{1,0:T(8,128)(2,1)S(1)}, u32[]{:S(2)}, u32[]{:S(2)}) collective-permute-start(bf16[272,128]{1,0:T(8,128)(2,1)S(1)} %get-tuple-element.29), channel_id=1, source_target_pairs={{32,0},{33,1},{34,2},{35,3},{36,4},{37,5},{38,6},{39,7},{40,8},{41... | collective-permute-start | bytes 208904 | tf_op jit(solution)/shard_map/ppermute | solution.py:409
  12.9 14.2 %collective-permute-start.3 = (bf16[272,128]{1,0:T(8,128)(2,1)S(1)}, bf16[272,128]{1,0:T(8,128)(2,1)S(1)}, u32[]{:S(2)}, u32[]{:S(2)}) collective-permute-start(bf16[272,128]{1,0:T(8,128)(2,1)S(1)} %get-tuple-element.31), channel_id=1, source_target_pairs={{1,0},{2,1},{3,2},{4,3},{5,4},{6,5},{7,6},{8,7},{9,8},{10,9},{11,1... | collective-permute-start | bytes 208904 | tf_op jit(solution)/shard_map/ppermute | solution.py:409
  15.8 11.3 %collective-permute-start.2 = (bf16[272,128]{1,0:T(8,128)(2,1)S(1)}, bf16[272,128]{1,0:T(8,128)(2,1)S(1)}, u32[]{:S(2)}, u32[]{:S(2)}) collective-permute-start(bf16[272,128]{1,0:T(8,128)(2,1)S(1)} %get-tuple-element.30.after_ref), channel_id=1, source_target_pairs={{0,1},{1,2},{2,3},{3,4},{4,5},{5,6},{6,7},{7,8},{8,9},{9,10},{10,1... | collective-permute-start | bytes 208904 | tf_op jit(solution)/shard_map/ppermute | solution.py:409
  18.8 1.2 %copy-start = (bf16[27,128,128]{2,1,0:T(8,128)(2,1)S(1)}, bf16[27,128,128]{2,1,0:T(8,128)(2,1)}, u32[]{:S(2)}) copy-start(bf16[27,128,128]{2,1,0:T(8,128)(2,1)} %param.8) | copy-start | bytes 2654212
  28.9 5.0 %collective-permute-start.6 = (f32[1792,128]{1,0:T(8,128)S(1)}, f32[1792,128]{1,0:T(8,128)S(1)}, u32[]{:S(2)}, u32[]{:S(2)}) collective-permute-start(f32[1792,128]{1,0:T(8,128)S(1)} %get-tuple-element.37), channel_id=1, source_target_pairs={{0,1},{1,0},{2,3},{3,2},{4,5},{5,4},{6,7},{7,6},{8,9},{9,8},{10,11... | collective-permute-start | bytes 2752520 | tf_op jit(solution)/shard_map/ppermute | solution.py:414
  33.9 33.7 %copy-start.1 = (bf16[27,128,128]{2,1,0:T(8,128)(2,1)S(1)}, bf16[27,128,128]{2,1,0:T(8,128)(2,1)}, u32[]{:S(2)}) copy-start(bf16[27,128,128]{2,1,0:T(8,128)(2,1)} %param.8) | copy-start | bytes 2654212
  35.0 17.5 %all-to-all-start = ((s16[16,128,128]{2,1,0:T(8,128)(2,1)}), s16[16,128,128]{2,1,0:T(8,128)(2,1)S(1)}, u32[]{:S(2)}, u32[]{:S(2)}) async-start(s16[16,128,128]{2,1,0:T(8,128)(2,1)} %bitcast.2), calls=%async_computation | async-start | bytes 1048576 | tf_op jit(solution)/shard_map/all_to_all | solution.py:419
  41.8 6.0 %collective-permute-start.4 = (bf16[96,128]{1,0:T(8,128)(2,1)S(1)}, bf16[96,128]{1,0:T(8,128)(2,1)S(1)}, u32[]{:S(2)}, u32[]{:S(2)}) collective-permute-start(bf16[96,128]{1,0:T(8,128)(2,1)S(1)} %get-tuple-element.32), channel_id=1, source_target_pairs={{0,1},{1,2},{2,3},{3,4},{4,5},{5,6},{6,7},{7,8},{8,9},{9,10},{10,1... | collective-permute-start | bytes 73736 | tf_op jit(solution)/shard_map/ppermute | solution.py:409
  45.9 5.4 %collective-permute-start.5 = (bf16[96,128]{1,0:T(8,128)(2,1)S(1)}, bf16[96,128]{1,0:T(8,128)(2,1)S(1)}, u32[]{:S(2)}, u32[]{:S(2)}) collective-permute-start(bf16[96,128]{1,0:T(8,128)(2,1)S(1)} %get-tuple-element.33.refs_8_), channel_id=1, source_target_pairs={{1,0},{2,1},{3,2},{4,3},{5,4},{6,5},{7,6},{8,7},{9,8},{10,9},{11,1... | collective-permute-start | bytes 73736 | tf_op jit(solution)/shard_map/ppermute | solution.py:409
  60.0 11.3 %collective-permute-start.7 = (s16[128,128]{1,0:T(8,128)(2,1)S(1)}, s16[128,128]{1,0:T(8,128)(2,1)S(1)}, u32[]{:S(2)}, u32[]{:S(2)}) collective-permute-start(s16[128,128]{1,0:T(8,128)(2,1)S(1)} %sum_blocks.5.refs_10_.refs_0_), channel_id=1, source_target_pairs={{0,32},{1,33},{2,34},{3,35},{4,36},{5,37},{6,38},{7,39},{8,40},{9,... | collective-permute-start | bytes 98312 | tf_op jit(solution)/shard_map/ppermute | solution.py:414
  71.4 8.7 %collective-permute-start.8 = (s16[128,128]{1,0:T(8,128)(2,1)S(1)}, s16[128,128]{1,0:T(8,128)(2,1)S(1)}, u32[]{:S(2)}, u32[]{:S(2)}) collective-permute-start(s16[128,128]{1,0:T(8,128)(2,1)S(1)} %sum_blocks.6.refs_10_.refs_0_), channel_id=1, source_target_pairs={{0,96},{1,97},{2,98},{3,99},{4,100},{5,101},{6,102},{7,103},{8,104... | collective-permute-start | bytes 98312 | tf_op jit(solution)/shard_map/ppermute | solution.py:414
  96.2 6.4 %collective-permute-start.9 = (s16[2048,128]{1,0:T(8,128)(2,1)S(1)}, s16[2048,128]{1,0:T(8,128)(2,1)S(1)}, u32[]{:S(2)}, u32[]{:S(2)}) collective-permute-start(s16[2048,128]{1,0:T(8,128)(2,1)S(1)} %bitcast.11), channel_id=1, source_target_pairs={{0,1},{1,0},{2,3},{3,2},{4,5},{5,4},{6,7},{7,6},{8,9},{9,8},{10,11... | collective-permute-start | bytes 1572872 | tf_op jit(solution)/shard_map/ppermute | solution.py:414

commit v5 on v4

--- a/solution.py
+++ b/solution.py
@@ -19,10 +19,11 @@
 FACE = 2 * BLK_DEV * BE * BE
 EDGE = 2 * BLK_DEV * BE
 TAG = 16
-CHUNK = 112
-CODED = CHUNK + TAG
+CHUNK = 108
+CODED = 112
 STEPS = 32000.0
 HALF = 16 * CHUNK
+SPARE = 8
 CORE = 1
 XY_SETS = [
     [(y * 4 + z_hi) * 32 + z_lo * 8 + x * 2 + core for y in range(4) for x in range(4)]
@@ -195,7 +196,7 @@
         jnp.transpose(in_ref[s * VOX:(s + 1) * VOX, :].astype(jnp.float32)).astype(jnp.bfloat16)
         for s in range(BLK_DEV)
     ]
-    total_ref[KV * C:, :] = jnp.zeros((2 * HALF - KV * C, C), jnp.float32)
+    total_ref[KV * C:, :] = jnp.zeros((SPARE, C), jnp.float32)
     for e1 in range(3):
         rows = slice(e1 * BE * BE, e1 * BE * BE + VOX)
         total = jnp.dot(inner[0], a_ref[0, rows, :], preferred_element_type=jnp.float32)
@@ -207,32 +208,30 @@
             k = KV - 1 - (9 * e1 + j)
             total_ref[k * C:(k + 1) * C, :] = total[:, j * C:(j + 1) * C]
     core = core_ref[0]
-    keep_ref[...] = total_ref[pl.ds(pl.multiple_of(core * HALF, HALF), HALF), :]
-    send_ref[...] = total_ref[pl.ds(pl.multiple_of((1 - core) * HALF, HALF), HALF), :]
+    keep_ref[...] = total_ref[pl.ds(pl.multiple_of(core * HALF, HALF), HALF + SPARE), :]
+    send_ref[...] = total_ref[pl.ds(pl.multiple_of((1 - core) * HALF, HALF), HALF + SPARE), :]
 
 
 def coded(value):
-    top = jnp.maximum(jnp.max(jnp.abs(value), axis=0, keepdims=True), 2.0 ** -120)
-    exponent = jnp.floor(jnp.log2(top)) + 1.0
+    inside = lax.broadcasted_iota(jnp.int32, (CODED, C), 0) < CHUNK
+    size = jnp.where(inside, jnp.abs(value), 0.0)
+    exponent = jnp.floor(jnp.log2(jnp.maximum(jnp.max(size, axis=0, keepdims=True), 2.0 ** -120))) + 1.0
     steps = jnp.floor(value * (jnp.exp2(-exponent) * STEPS) + 0.5)
-    last = jnp.broadcast_to(exponent, (TAG, C))
-    return jnp.concatenate([steps, last]).astype(jnp.int32).astype(jnp.int16)
+    return jnp.where(inside, steps, exponent).astype(jnp.int32).astype(jnp.int16)
 
 
 def decoded(ref, block=0):
     code = ref[block * CODED:(block + 1) * CODED, :].astype(jnp.int32).astype(jnp.float32)
-    return code[:CHUNK] * (jnp.exp2(code[CHUNK:CHUNK + 1]) * (1.0 / STEPS))
+    return code * (jnp.exp2(code[CHUNK:CHUNK + 1]) * (1.0 / STEPS))
 
 
 def place_kernel(core_ref, near_ref, far_ref, after_ref, out_ref):
     first = core_ref[0] == 0
     for block in range(16):
-        near, far = decoded(near_ref, block), decoded(far_ref, block)
+        near, far = decoded(near_ref, block)[:CHUNK], decoded(far_ref, block)[:CHUNK]
         at = block * CHUNK
         out_ref[at:at + CHUNK, :] = jnp.where(first, near, far)
-        size = min(CHUNK, KV * C - HALF - at)
-        if size > 0:
-            out_ref[HALF + at:HALF + at + size, :] = jnp.where(first, far, near)[:size]
+        out_ref[HALF + at:HALF + at + CHUNK, :] = jnp.where(first, far, near)
 
 
 def turn_kernel(w_ref, out_ref, done_ref):
@@ -322,13 +321,13 @@
     def kernel(*refs):
         wgrad_kernel(scale, *refs)
 
-    half = jax.ShapeDtypeStruct((HALF, C), jnp.float32)
+    half = jax.ShapeDtypeStruct((HALF + SPARE, C), jnp.float32)
     return pl.pallas_call(
         kernel,
         out_shape=[half, half],
         in_specs=[VMEM, SMEM] + [VMEM] * 5 + [ANY] * len(after),
         out_specs=[VMEM] * 2,
-        scratch_shapes=scratch(BLK_DEV) + [pltpu.VMEM((2 * HALF, C), jnp.float32)],
+        scratch_shapes=scratch(BLK_DEV) + [pltpu.VMEM((KV * C + SPARE, C), jnp.float32)],
         compiler_params=PARAMS,
         name="kernel_gradient",
     )(tag, core, own_in, own_grad, *halo, *after)
@@ -385,7 +384,7 @@
 
 def sum_halves_kernel(a_ref, b_ref, out_ref):
     for block in range(HALF // CHUNK):
-        rows = slice(block * CHUNK, (block + 1) * CHUNK)
+        rows = slice(block * CHUNK, block * CHUNK + CODED)
         out_ref[block * CODED:(block + 1) * CODED, :] = coded(a_ref[rows, :] + b_ref[rows, :])
 
 

time: 105 us -> 104 us (level)
  no operation moved by 1% of the time
where the time goes in v5:
time: 104 us; the launch traced here: 103 us
  starting transfers between devices  49.1 us (47%)
  blocking collectives  23.5 us (23%)
  waiting for transfers between devices  14.7 us (14%)
  Pallas kernels  13.8 us (13%)
  local copies, waits for them, and re-layouts  1.17 us (1%)
    all_to_all x2, blocking collectives, exchange(): lax.all_to_all(value.reshape(count, -1, C), axis, 0, 0, axis_index_groups...  23.5 us
    ppermute x6, starting transfers between devices, shifted(): return lax.ppermute(value, AXES, pairs)  22.8 us
    ppermute x4, starting transfers between devices, across(): return lax.ppermute(value, AXES, [(i, i ^ mask) for i in range(count)])  19.4 us
    ppermute x6, waiting for transfers between devices, shifted(): return lax.ppermute(value, AXES, pairs)  10.3 us
    pallas_call x4, Pallas kernels, conv(): pl.pallas_call(kernel, grid=(1,), out_shape=[bf16(BLK_DEV, VOX, C), jax.S...  7.38 us
    all_to_all x1, starting transfers between devices, exchange(): lax.all_to_all(value.reshape(count, -1, C), axis, 0, 0, axis_index_groups...  6.8 us
    ppermute x4, waiting for transfers between devices, across(): return lax.ppermute(value, AXES, [(i, i ^ mask) for i in range(count)])  4.02 us
  transfers between devices with their start and end apart: 11, of which 5 were waited for; matrix products, arithmetic and copies ran while one was open for 0% of the time, Pallas kernels for 7%

profile of v5, /device:TPU:1, one launch (start us, length us, event | category | flops | bytes accessed | tf_op | source)
XLA Modules:
  0.0 103.1 jit_solution(17146722532679266658)
XLA Ops:
  0.6 1.3 %mask_and_faces.1 = (bf16[1024,128]{1,0:T(8,128)(2,1)S(1)}, bf16[1024,128]{1,0:T(8,128)(2,1)S(1)}, bf16[1024,128]{1,0:T(8,128)(2,1)S(1)}, bf16[16,128]{1,0:T(8,1...) custom-call(s32[2]{0:T(128)} %refs_0_.1, ...), custom_call_target="tpu_custom_call" | custom-call | tf_op jit(solution)/shard_map/mask_and_faces/pallas_call | solution.py:271
  1.9 9.6 %collective-permute-start = (bf16[272,128]{1,0:T(8,128)(2,1)S(1)}, bf16[272,128]{1,0:T(8,128)(2,1)S(1)}, u32[]{:S(2)}, u32[]{:S(2)}) collective-permute-start(bf16[272,128]{1,0:T(8,128)(2,1)S(1)} %get-tuple-element.28), channel_id=1, source_target_pairs={{0,32},{1,33},{2,34},{3,35},{4,36},{5,37},{6,38},{7,39},{8,40},{9,... | collective-permute-start | bytes 208904 | tf_op jit(solution)/shard_map/ppermute | solution.py:408
  11.6 1.3 %collective-permute-start.1 = (bf16[272,128]{1,0:T(8,128)(2,1)S(1)}, bf16[272,128]{1,0:T(8,128)(2,1)S(1)}, u32[]{:S(2)}, u32[]{:S(2)}) collective-permute-start(bf16[272,128]{1,0:T(8,128)(2,1)S(1)} %get-tuple-element.29), channel_id=1, source_target_pairs={{32,0},{33,1},{34,2},{35,3},{36,4},{37,5},{38,6},{39,7},{40,8},{41... | collective-permute-start | bytes 208904 | tf_op jit(solution)/shard_map/ppermute | solution.py:408
  12.9 2.9 %collective-permute-start.3 = (bf16[272,128]{1,0:T(8,128)(2,1)S(1)}, bf16[272,128]{1,0:T(8,128)(2,1)S(1)}, u32[]{:S(2)}, u32[]{:S(2)}) collective-permute-start(bf16[272,128]{1,0:T(8,128)(2,1)S(1)} %get-tuple-element.31), channel_id=1, source_target_pairs={{1,0},{2,1},{3,2},{4,3},{5,4},{6,5},{7,6},{8,7},{9,8},{10,9},{11,1... | collective-permute-start | bytes 208904 | tf_op jit(solution)/shard_map/ppermute | solution.py:408
  15.8 3.0 %collective-permute-start.2 = (bf16[272,128]{1,0:T(8,128)(2,1)S(1)}, bf16[272,128]{1,0:T(8,128)(2,1)S(1)}, u32[]{:S(2)}, u32[]{:S(2)}) collective-permute-start(bf16[272,128]{1,0:T(8,128)(2,1)S(1)} %get-tuple-element.30.after_ref), channel_id=1, source_target_pairs={{0,1},{1,2},{2,3},{3,4},{4,5},{5,6},{6,7},{7,8},{8,9},{9,10},{10,1... | collective-permute-start | bytes 208904 | tf_op jit(solution)/shard_map/ppermute | solution.py:408
  20.3 6.8 %collective-permute-done.1.high_ref.refs_5_ = bf16[272,128]{1,0:T(8,128)(2,1)S(1)} collective-permute-done((bf16[272,128]{1,0:T(8,128)(2,1)S(1)}, bf16[272,128]{1,0:T(8,128)(2,1)S(1)}, u32[]{:S(2)}, u32[]{:S(2)}) %collective-permute-start.1) | collective-permute-done | bytes 69664 | tf_op jit(solution)/shard_map/ppermute | solution.py:408
  27.1 1.8 %kernel_gradient.1 = (f32[1736,128]{1,0:T(8,128)S(1)}, f32[1736,128]{1,0:T(8,128)S(1)}) custom-call(bf16[16,128]{1,0:T(8,128)(2,1)S(1)} %get-tuple-element.25.refs_0_, s32[1]{0:T(128)} %bitcast.1.refs_1_.core_ref, bf16[1024,128]{1,0:T(8,128)(2,1)S(1)} %get-tuple-element.26.refs_2_.refs_1_, bf16[1024,128]{1,0:T(8,128)(2,1)S(1)} %get-tuple-element.34.refs_3_.refs_1_, ...), custom_call_target="tpu_custom_call" | custom-call | tf_op jit(solution)/shard_map/kernel_gradient/pallas_call | solution.py:325
  28.9 2.9 %collective-permute-start.6 = (f32[1736,128]{1,0:T(8,128)S(1)}, f32[1736,128]{1,0:T(8,128)S(1)}, u32[]{:S(2)}, u32[]{:S(2)}) collective-permute-start(f32[1736,128]{1,0:T(8,128)S(1)} %get-tuple-element.37), channel_id=1, source_target_pairs={{0,1},{1,0},{2,3},{3,2},{4,5},{5,4},{6,7},{7,6},{8,9},{9,8},{10,11... | collective-permute-start | bytes 2666504 | tf_op jit(solution)/shard_map/ppermute | solution.py:413
  31.8 2.0 %collective-permute-done.6.refs_1_ = f32[1736,128]{1,0:T(8,128)S(1)} collective-permute-done((f32[1736,128]{1,0:T(8,128)S(1)}, f32[1736,128]{1,0:T(8,128)S(1)}, u32[]{:S(2)}, u32[]{:S(2)}) %collective-permute-start.6) | collective-permute-done | bytes 888864 | tf_op jit(solution)/shard_map/ppermute | solution.py:413
  35.0 6.8 %all-to-all-start = ((s16[16,112,128]{2,1,0:T(8,128)(2,1)}), s16[16,112,128]{2,1,0:T(8,128)(2,1)S(1)}, u32[]{:S(2)}, u32[]{:S(2)}) async-start(s16[16,112,128]{2,1,0:T(8,128)(2,1)} %bitcast.2), calls=%async_computation | async-start | bytes 917504 | tf_op jit(solution)/shard_map/all_to_all | solution.py:418
  41.8 4.1 %collective-permute-start.4 = (bf16[96,128]{1,0:T(8,128)(2,1)S(1)}, bf16[96,128]{1,0:T(8,128)(2,1)S(1)}, u32[]{:S(2)}, u32[]{:S(2)}) collective-permute-start(bf16[96,128]{1,0:T(8,128)(2,1)S(1)} %get-tuple-element.32), channel_id=1, source_target_pairs={{0,1},{1,2},{2,3},{3,4},{4,5},{5,6},{6,7},{7,8},{8,9},{9,10},{10,1... | collective-permute-start | bytes 73736 | tf_op jit(solution)/shard_map/ppermute | solution.py:408
  45.9 1.9 %collective-permute-start.5 = (bf16[96,128]{1,0:T(8,128)(2,1)S(1)}, bf16[96,128]{1,0:T(8,128)(2,1)S(1)}, u32[]{:S(2)}, u32[]{:S(2)}) collective-permute-start(bf16[96,128]{1,0:T(8,128)(2,1)S(1)} %get-tuple-element.33.refs_8_), channel_id=1, source_target_pairs={{1,0},{2,1},{3,2},{4,3},{5,4},{6,5},{7,6},{8,7},{9,8},{10,9},{11,1... | collective-permute-start | bytes 73736 | tf_op jit(solution)/shard_map/ppermute | solution.py:408
  47.8 3.5 %collective-permute-done.5.refs_2_.refs_9_ = bf16[96,128]{1,0:T(8,128)(2,1)S(1)} collective-permute-done((bf16[96,128]{1,0:T(8,128)(2,1)S(1)}, bf16[96,128]{1,0:T(8,128)(2,1)S(1)}, u32[]{:S(2)}, u32[]{:S(2)}) %collective-permute-start.5) | collective-permute-done | bytes 24608 | tf_op jit(solution)/shard_map/ppermute | solution.py:408
  51.9 7.1 %all_to_all.15 = s16[4,112,128]{2,1,0:T(8,128)(2,1)S(1)} all-to-all(s16[4,112,128]{2,1,0:T(8,128)(2,1)S(1)} %bitcast.17), channel_id=1, replica_groups={{0,8,16,24},{1,9,17,25},{2,10,18,26},{3,11,19,27},{4,12,20,28},{5,13,21..., dimensions={0} | all-to-all | bytes 229376 | tf_op jit(solution)/shard_map/all_to_all | solution.py:418
  59.1 7.7 %collective-permute-start.7 = (s16[112,128]{1,0:T(8,128)(2,1)S(1)}, s16[112,128]{1,0:T(8,128)(2,1)S(1)}, u32[]{:S(2)}, u32[]{:S(2)}) collective-permute-start(s16[112,128]{1,0:T(8,128)(2,1)S(1)} %sum_blocks.5.refs_10_.refs_0_), channel_id=1, source_target_pairs={{0,32},{1,33},{2,34},{3,35},{4,36},{5,37},{6,38},{7,39},{8,40},{9,... | collective-permute-start | bytes 86024 | tf_op jit(solution)/shard_map/ppermute | solution.py:413
  66.8 1.8 %convolution.2 = (bf16[2,512,128]{2,1,0:T(8,128)(2,1)}, f32[8,128]{1,0:T(8,128)S(1)}) custom-call(bf16[16,128]{1,0:T(8,128)(2,1)S(1)} %get-tuple-element.25.refs_0_, bf16[1024,128]{1,0:T(8,128)(2,1)S(1)} %get-tuple-element.26.refs_2_.refs_1_, bf16[1024,128]{1,0:T(8,128)(2,1)S(1)} %get-tuple-element.27.refs_2_, bf16[3456,128]{1,0:T(8,128)(2,1)S(1)} %bitcast.15, ...), custom_call_target="tpu_custom_call" | custom-call | flops 1811939328 | bytes 2000000 | tf_op jit(solution)/shard_map/convolution/pallas_call | solution.py:354
  68.6 1.8 %convolution.3 = (bf16[2,512,128]{2,1,0:T(8,128)(2,1)}, f32[8,128]{1,0:T(8,128)S(1)}) custom-call(bf16[16,128]{1,0:T(8,128)(2,1)S(1)} %get-tuple-element.25.refs_0_, bf16[1024,128]{1,0:T(8,128)(2,1)S(1)} %get-tuple-element.26.refs_2_.refs_1_, bf16[1024,128]{1,0:T(8,128)(2,1)S(1)} %get-tuple-element.27.refs_2_, ...), custom_call_target="tpu_custom_call", output_to_operand_aliasing={{0}: (10, {})} | custom-call | flops 1811939328 | bytes 2000000 | tf_op jit(solution)/shard_map/convolution/pallas_call | solution.py:354
  70.5 4.7 %collective-permute-start.8 = (s16[112,128]{1,0:T(8,128)(2,1)S(1)}, s16[112,128]{1,0:T(8,128)(2,1)S(1)}, u32[]{:S(2)}, u32[]{:S(2)}) collective-permute-start(s16[112,128]{1,0:T(8,128)(2,1)S(1)} %sum_blocks.6.refs_10_.refs_0_), channel_id=1, source_target_pairs={{0,96},{1,97},{2,98},{3,99},{4,100},{5,101},{6,102},{7,103},{8,104... | collective-permute-start | bytes 86024 | tf_op jit(solution)/shard_map/ppermute | solution.py:413
  75.3 1.9 %feature_gradient.2 = (bf16[2,512,128]{2,1,0:T(8,128)(2,1)}, f32[8,128]{1,0:T(8,128)S(1)}) custom-call(bf16[16,128]{1,0:T(8,128)(2,1)S(1)} %get-tuple-element.25.refs_0_, bf16[1024,128]{1,0:T(8,128)(2,1)S(1)} %get-tuple-element.34.refs_3_.refs_1_, bf16[1024,128]{1,0:T(8,128)(2,1)S(1)} %get-tuple-element.27.refs_2_, ...), custom_call_target="tpu_custom_call" | custom-call | flops 1811939328 | bytes 2000000 | tf_op jit(solution)/shard_map/feature_gradient/pallas_call | solution.py:354
  77.1 2.0 %collective-permute-done.8.refs_1_ = s16[112,128]{1,0:T(8,128)(2,1)S(1)} collective-permute-done((s16[112,128]{1,0:T(8,128)(2,1)S(1)}, s16[112,128]{1,0:T(8,128)(2,1)S(1)}, u32[]{:S(2)}, u32[]{:S(2)}) %collective-permute-start.8) | collective-permute-done | bytes 28704 | tf_op jit(solution)/shard_map/ppermute | solution.py:413
  79.2 16.4 %all_to_all.16 = s16[16,112,128]{2,1,0:T(8,128)(2,1)S(1)} all-to-all(s16[16,112,128]{2,1,0:T(8,128)(2,1)S(1)} %bitcast.10), channel_id=1, replica_groups={{0,2,4,6,128,130,132,134,256,258,260,262,384,386,388,390},{1,3,5,7,129,..., dimensions={0} | all-to-all | bytes 917504 | tf_op jit(solution)/shard_map/all_to_all | solution.py:418
  95.6 4.1 %collective-permute-start.9 = (s16[1792,128]{1,0:T(8,128)(2,1)S(1)}, s16[1792,128]{1,0:T(8,128)(2,1)S(1)}, u32[]{:S(2)}, u32[]{:S(2)}) collective-permute-start(s16[1792,128]{1,0:T(8,128)(2,1)S(1)} %bitcast.11), channel_id=1, source_target_pairs={{0,1},{1,0},{2,3},{3,2},{4,5},{5,4},{6,7},{7,6},{8,9},{9,8},{10,11... | collective-permute-start | bytes 1376264 | tf_op jit(solution)/shard_map/ppermute | solution.py:413
  99.7 1.9 %feature_gradient.3 = (bf16[2,512,128]{2,1,0:T(8,128)(2,1)}, f32[8,128]{1,0:T(8,128)S(1)}) custom-call(bf16[16,128]{1,0:T(8,128)(2,1)S(1)} %get-tuple-element.25.refs_0_, bf16[1024,128]{1,0:T(8,128)(2,1)S(1)} %get-tuple-element.34.refs_3_.refs_1_, bf16[1024,128]{1,0:T(8,128)(2,1)S(1)} %get-tuple-element.27.refs_2_, ...), custom_call_target="tpu_custom_call", output_to_operand_aliasing={{0}: (10, {})} | custom-call | flops 1811939328 | bytes 2000000 | tf_op jit(solution)/shard_map/feature_gradient/pallas_call | solution.py:354
  101.6 1.5 %place_halves.1 = f32[3456,128]{1,0:T(8,128)} custom-call(s32[1]{0:T(128)} %bitcast.1.refs_1_.core_ref, s16[1792,128]{1,0:T(8,128)(2,1)S(1)} %bitcast.13, s16[1792,128]{1,0:T(8,128)(2,1)S(1)} %collective-permute-done.9.far_ref, f32[8,128]{1,0:T(8,128)S(1)} %get-tuple-element.46.after_ref), custom_call_target="tpu_custom_call" | custom-call | tf_op jit(solution)/shard_map/place_halves/pallas_call | solution.py:337
  (18 shorter events, 3.4 us)
Async XLA Ops:
  1.9 18.3 %collective-permute-start = (bf16[272,128]{1,0:T(8,128)(2,1)S(1)}, bf16[272,128]{1,0:T(8,128)(2,1)S(1)}, u32[]{:S(2)}, u32[]{:S(2)}) collective-permute-start(bf16[272,128]{1,0:T(8,128)(2,1)S(1)} %get-tuple-element.28), channel_id=1, source_target_pairs={{0,32},{1,33},{2,34},{3,35},{4,36},{5,37},{6,38},{7,39},{8,40},{9,... | collective-permute-start | bytes 208904 | tf_op jit(solution)/shard_map/ppermute | solution.py:408
  11.6 15.5 %collective-permute-start.1 = (bf16[272,128]{1,0:T(8,128)(2,1)S(1)}, bf16[272,128]{1,0:T(8,128)(2,1)S(1)}, u32[]{:S(2)}, u32[]{:S(2)}) collective-permute-start(bf16[272,128]{1,0:T(8,128)(2,1)S(1)} %get-tuple-element.29), channel_id=1, source_target_pairs={{32,0},{33,1},{34,2},{35,3},{36,4},{37,5},{38,6},{39,7},{40,8},{41... | collective-permute-start | bytes 208904 | tf_op jit(solution)/shard_map/ppermute | solution.py:408
  12.9 14.2 %collective-permute-start.3 = (bf16[272,128]{1,0:T(8,128)(2,1)S(1)}, bf16[272,128]{1,0:T(8,128)(2,1)S(1)}, u32[]{:S(2)}, u32[]{:S(2)}) collective-permute-start(bf16[272,128]{1,0:T(8,128)(2,1)S(1)} %get-tuple-element.31), channel_id=1, source_target_pairs={{1,0},{2,1},{3,2},{4,3},{5,4},{6,5},{7,6},{8,7},{9,8},{10,9},{11,1... | collective-permute-start | bytes 208904 | tf_op jit(solution)/shard_map/ppermute | solution.py:408
  15.8 11.3 %collective-permute-start.2 = (bf16[272,128]{1,0:T(8,128)(2,1)S(1)}, bf16[272,128]{1,0:T(8,128)(2,1)S(1)}, u32[]{:S(2)}, u32[]{:S(2)}) collective-permute-start(bf16[272,128]{1,0:T(8,128)(2,1)S(1)} %get-tuple-element.30.after_ref), channel_id=1, source_target_pairs={{0,1},{1,2},{2,3},{3,4},{4,5},{5,6},{6,7},{7,8},{8,9},{9,10},{10,1... | collective-permute-start | bytes 208904 | tf_op jit(solution)/shard_map/ppermute | solution.py:408
  18.8 1.2 %copy-start = (bf16[27,128,128]{2,1,0:T(8,128)(2,1)S(1)}, bf16[27,128,128]{2,1,0:T(8,128)(2,1)}, u32[]{:S(2)}) copy-start(bf16[27,128,128]{2,1,0:T(8,128)(2,1)} %param.8) | copy-start | bytes 2654212
  28.9 4.9 %collective-permute-start.6 = (f32[1736,128]{1,0:T(8,128)S(1)}, f32[1736,128]{1,0:T(8,128)S(1)}, u32[]{:S(2)}, u32[]{:S(2)}) collective-permute-start(f32[1736,128]{1,0:T(8,128)S(1)} %get-tuple-element.37), channel_id=1, source_target_pairs={{0,1},{1,0},{2,3},{3,2},{4,5},{5,4},{6,7},{7,6},{8,9},{9,8},{10,11... | collective-permute-start | bytes 2666504 | tf_op jit(solution)/shard_map/ppermute | solution.py:413
  33.8 33.0 %copy-start.1 = (bf16[27,128,128]{2,1,0:T(8,128)(2,1)S(1)}, bf16[27,128,128]{2,1,0:T(8,128)(2,1)}, u32[]{:S(2)}) copy-start(bf16[27,128,128]{2,1,0:T(8,128)(2,1)} %param.8) | copy-start | bytes 2654212
  35.0 16.7 %all-to-all-start = ((s16[16,112,128]{2,1,0:T(8,128)(2,1)}), s16[16,112,128]{2,1,0:T(8,128)(2,1)S(1)}, u32[]{:S(2)}, u32[]{:S(2)}) async-start(s16[16,112,128]{2,1,0:T(8,128)(2,1)} %bitcast.2), calls=%async_computation | async-start | bytes 917504 | tf_op jit(solution)/shard_map/all_to_all | solution.py:418
  41.8 6.0 %collective-permute-start.4 = (bf16[96,128]{1,0:T(8,128)(2,1)S(1)}, bf16[96,128]{1,0:T(8,128)(2,1)S(1)}, u32[]{:S(2)}, u32[]{:S(2)}) collective-permute-start(bf16[96,128]{1,0:T(8,128)(2,1)S(1)} %get-tuple-element.32), channel_id=1, source_target_pairs={{0,1},{1,2},{2,3},{3,4},{4,5},{5,6},{6,7},{7,8},{8,9},{9,10},{10,1... | collective-permute-start | bytes 73736 | tf_op jit(solution)/shard_map/ppermute | solution.py:408
  45.9 5.4 %collective-permute-start.5 = (bf16[96,128]{1,0:T(8,128)(2,1)S(1)}, bf16[96,128]{1,0:T(8,128)(2,1)S(1)}, u32[]{:S(2)}, u32[]{:S(2)}) collective-permute-start(bf16[96,128]{1,0:T(8,128)(2,1)S(1)} %get-tuple-element.33.refs_8_), channel_id=1, source_target_pairs={{1,0},{2,1},{3,2},{4,3},{5,4},{6,5},{7,6},{8,7},{9,8},{10,9},{11,1... | collective-permute-start | bytes 73736 | tf_op jit(solution)/shard_map/ppermute | solution.py:408
  59.1 11.4 %collective-permute-start.7 = (s16[112,128]{1,0:T(8,128)(2,1)S(1)}, s16[112,128]{1,0:T(8,128)(2,1)S(1)}, u32[]{:S(2)}, u32[]{:S(2)}) collective-permute-start(s16[112,128]{1,0:T(8,128)(2,1)S(1)} %sum_blocks.5.refs_10_.refs_0_), channel_id=1, source_target_pairs={{0,32},{1,33},{2,34},{3,35},{4,36},{5,37},{6,38},{7,39},{8,40},{9,... | collective-permute-start | bytes 86024 | tf_op jit(solution)/shard_map/ppermute | solution.py:413
  70.5 8.5 %collective-permute-start.8 = (s16[112,128]{1,0:T(8,128)(2,1)S(1)}, s16[112,128]{1,0:T(8,128)(2,1)S(1)}, u32[]{:S(2)}, u32[]{:S(2)}) collective-permute-start(s16[112,128]{1,0:T(8,128)(2,1)S(1)} %sum_blocks.6.refs_10_.refs_0_), channel_id=1, source_target_pairs={{0,96},{1,97},{2,98},{3,99},{4,100},{5,101},{6,102},{7,103},{8,104... | collective-permute-start | bytes 86024 | tf_op jit(solution)/shard_map/ppermute | solution.py:413
  95.6 6.0 %collective-permute-start.9 = (s16[1792,128]{1,0:T(8,128)(2,1)S(1)}, s16[1792,128]{1,0:T(8,128)(2,1)S(1)}, u32[]{:S(2)}, u32[]{:S(2)}) collective-permute-start(s16[1792,128]{1,0:T(8,128)(2,1)S(1)} %bitcast.11), channel_id=1, source_target_pairs={{0,1},{1,0},{2,3},{3,2},{4,5},{5,4},{6,7},{7,6},{8,9},{9,8},{10,11... | collective-permute-start | bytes 1376264 | tf_op jit(solution)/shard_map/ppermute | solution.py:413

commit v6 on v5

--- a/solution.py
+++ b/solution.py
@@ -225,13 +225,10 @@
     return code * (jnp.exp2(code[CHUNK:CHUNK + 1]) * (1.0 / STEPS))
 
 
-def place_kernel(core_ref, near_ref, far_ref, after_ref, out_ref):
-    first = core_ref[0] == 0
+def place_half_kernel(half_ref, code_ref, *refs):
+    out_ref = refs[-1]
     for block in range(16):
-        near, far = decoded(near_ref, block)[:CHUNK], decoded(far_ref, block)[:CHUNK]
-        at = block * CHUNK
-        out_ref[at:at + CHUNK, :] = jnp.where(first, near, far)
-        out_ref[HALF + at:HALF + at + CHUNK, :] = jnp.where(first, far, near)
+        out_ref[block * CHUNK:(block + 1) * CHUNK, :] = decoded(code_ref, block)[:CHUNK]
 
 
 def turn_kernel(w_ref, out_ref, done_ref):
@@ -296,6 +293,21 @@
     )(low, high)
 
 
+def passed(value, after):
+    def kernel(value_ref, after_ref, out_ref):
+        pass
+
+    return pl.pallas_call(
+        kernel,
+        out_shape=jax.ShapeDtypeStruct(value.shape, value.dtype),
+        in_specs=[ANY] * 2,
+        out_specs=ANY,
+        input_output_aliases={0: 0},
+        compiler_params=PARAMS,
+        name="passed",
+    )(value, after)
+
+
 def turn(weights, after):
     def kernel(w_ref, after_ref, *refs):
         turn_kernel(w_ref, *refs)
@@ -333,15 +345,21 @@
     )(tag, core, own_in, own_grad, *halo, *after)
 
 
-def place(core, near, far, after):
-    return pl.pallas_call(
-        place_kernel,
+def place_half(half, code, before):
+    extra = [] if before is None else [before]
+    return pl.pallas_call(
+        place_half_kernel,
         out_shape=jax.ShapeDtypeStruct((KV * C, C), jnp.float32),
-        in_specs=[SMEM] + [VMEM] * 2 + [ANY],
-        out_specs=VMEM,
-        compiler_params=PARAMS,
-        name="place_halves",
-    )(core, near, far, after)
+        grid_spec=pltpu.PrefetchScalarGridSpec(
+            num_scalar_prefetch=1,
+            grid=(1,),
+            in_specs=[VMEM] + [ANY] * len(extra),
+            out_specs=pl.BlockSpec((HALF, C), lambda i, half: (half[0], 0)),
+        ),
+        input_output_aliases={} if before is None else {2: 0},
+        compiler_params=PARAMS,
+        name="place_half",
+    )(half, code, *extra)
 
 
 def conv(field, slot, tag, own, mask, weights, halo, before, after):
@@ -445,15 +463,16 @@
     value, = small(sum_blocks_kernel, [CODED], [exchange(value, "tile", Z_LO_SETS)])
     got = across(value, Z_HI_BITS[0])
     conv_out, done = convolved(0, 0, None, value)
-    conv_out, done = convolved(0, 1, conv_out, done)
     value, = small(sum_blocks_kernel, [CODED], [value, got], [done])
     got = across(value, Z_HI_BITS[1])
+    conv_out, done = convolved(0, 1, conv_out, value)
+    value, = small(sum_blocks_kernel, [16 * CODED], [value, got], [done])
     feature_grad, done = convolved(1, 0, None, value)
-    value, = small(sum_blocks_kernel, [16 * CODED], [value, got], [done])
-    value = exchange(value, AXES, XY_SETS)
+    feature_grad, done = convolved(1, 1, feature_grad, done)
+    value = passed(exchange(value, AXES, XY_SETS), done)
     got = across(value, CORE)
-    feature_grad, done = convolved(1, 1, feature_grad, value)
-    total = place(core, value, got, done)
+    total = place_half(core, value, None)
+    total = place_half(1 - core, got, total)
     return (conv_out, feature_grad, total.reshape(KV, C, C))
 
 

time: 104 us -> 103 us (level)
  blocking collectives: 23.5 us -> 7.11 us
  starting transfers between devices: 49.1 us -> 59.1 us
  waiting for transfers between devices: 14.7 us -> 18.8 us
  Pallas kernels: 13.8 us -> 15.1 us
    all_to_all x2 -> x1, blocking collectives: 23.5 us -> 7.11 us  [exchange(): lax.all_to_all(value.reshape(count, -1, C), axis, 0, 0, axis_index_groups...]
    all_to_all x1 -> x2, starting transfers between devices: 6.8 us -> 14.3 us  [exchange(): lax.all_to_all(value.reshape(count, -1, C), axis, 0, 0, axis_index_groups...]
    all_to_all x1 -> x2, waiting for transfers between devices: 0.39 us -> 6.09 us  [exchange(): lax.all_to_all(value.reshape(count, -1, C), axis, 0, 0, axis_index_groups...]
    ppermute x4, starting transfers between devices: 19.4 us -> 22.2 us  [across(): return lax.ppermute(value, AXES, [(i, i ^ mask) for i in range(count)])]
    ppermute x4, waiting for transfers between devices: 4.02 us -> 2.45 us  [across(): return lax.ppermute(value, AXES, [(i, i ^ mask) for i in range(count)])]
  transfers between devices with their start and end apart: 11 -> 12, of which waited for: 5 -> 6; matrix products, arithmetic and copies ran while one was open for 0% -> 0% of each run, Pallas kernels for 7% -> 9%
where the time goes in v6:
time: 103 us; the launch traced here: 102 us
  starting transfers between devices  59.1 us (57%)
  waiting for transfers between devices  18.8 us (18%)
  Pallas kernels  15.1 us (15%)
  blocking collectives  7.11 us (7%)
  local copies, waits for them, and re-layouts  1.17 us (1%)
    ppermute x6, starting transfers between devices, shifted(): return lax.ppermute(value, AXES, pairs)  22.6 us
    ppermute x4, starting transfers between devices, across(): return lax.ppermute(value, AXES, [(i, i ^ mask) for i in range(count)])  22.2 us
    all_to_all x2, starting transfers between devices, exchange(): lax.all_to_all(value.reshape(count, -1, C), axis, 0, 0, axis_index_groups...  14.3 us
    ppermute x6, waiting for transfers between devices, shifted(): return lax.ppermute(value, AXES, pairs)  10.3 us
    pallas_call x4, Pallas kernels, conv(): pl.pallas_call(kernel, grid=(1,), out_shape=[bf16(BLK_DEV, VOX, C), jax.S...  7.38 us
    all_to_all x1, blocking collectives, exchange(): lax.all_to_all(value.reshape(count, -1, C), axis, 0, 0, axis_index_groups...  7.11 us
    all_to_all x2, waiting for transfers between devices, exchange(): lax.all_to_all(value.reshape(count, -1, C), axis, 0, 0, axis_index_groups...  6.09 us
    ppermute x4, waiting for transfers between devices, across(): return lax.ppermute(value, AXES, [(i, i ^ mask) for i in range(count)])  2.45 us
  transfers between devices with their start and end apart: 12, of which 6 were waited for; matrix products, arithmetic and copies ran while one was open for 0% of the time, Pallas kernels for 9%

profile of v6, /device:TPU:1, one launch (start us, length us, event | category | flops | bytes accessed | tf_op | source)
XLA Modules:
  0.0 102.2 jit_solution(17161118405783323001)
XLA Ops:
  0.6 1.3 %mask_and_faces.1 = (bf16[1024,128]{1,0:T(8,128)(2,1)S(1)}, bf16[1024,128]{1,0:T(8,128)(2,1)S(1)}, bf16[1024,128]{1,0:T(8,128)(2,1)S(1)}, bf16[16,128]{1,0:T(8,1...) custom-call(s32[2]{0:T(128)} %refs_0_.1, ...), custom_call_target="tpu_custom_call" | custom-call | tf_op jit(solution)/shard_map/mask_and_faces/pallas_call | solution.py:268
  1.9 9.6 %collective-permute-start = (bf16[272,128]{1,0:T(8,128)(2,1)S(1)}, bf16[272,128]{1,0:T(8,128)(2,1)S(1)}, u32[]{:S(2)}, u32[]{:S(2)}) collective-permute-start(bf16[272,128]{1,0:T(8,128)(2,1)S(1)} %get-tuple-element.28), channel_id=1, source_target_pairs={{0,32},{1,33},{2,34},{3,35},{4,36},{5,37},{6,38},{7,39},{8,40},{9,... | collective-permute-start | bytes 208904 | tf_op jit(solution)/shard_map/ppermute | solution.py:426
  11.6 1.3 %collective-permute-start.1 = (bf16[272,128]{1,0:T(8,128)(2,1)S(1)}, bf16[272,128]{1,0:T(8,128)(2,1)S(1)}, u32[]{:S(2)}, u32[]{:S(2)}) collective-permute-start(bf16[272,128]{1,0:T(8,128)(2,1)S(1)} %get-tuple-element.29), channel_id=1, source_target_pairs={{32,0},{33,1},{34,2},{35,3},{36,4},{37,5},{38,6},{39,7},{40,8},{41... | collective-permute-start | bytes 208904 | tf_op jit(solution)/shard_map/ppermute | solution.py:426
  12.9 4.0 %collective-permute-start.2 = (bf16[272,128]{1,0:T(8,128)(2,1)S(1)}, bf16[272,128]{1,0:T(8,128)(2,1)S(1)}, u32[]{:S(2)}, u32[]{:S(2)}) collective-permute-start(bf16[272,128]{1,0:T(8,128)(2,1)S(1)} %get-tuple-element.30.after_ref), channel_id=1, source_target_pairs={{0,1},{1,2},{2,3},{3,4},{4,5},{5,6},{6,7},{7,8},{8,9},{9,10},{10,1... | collective-permute-start | bytes 208904 | tf_op jit(solution)/shard_map/ppermute | solution.py:426
  16.9 1.9 %collective-permute-start.3 = (bf16[272,128]{1,0:T(8,128)(2,1)S(1)}, bf16[272,128]{1,0:T(8,128)(2,1)S(1)}, u32[]{:S(2)}, u32[]{:S(2)}) collective-permute-start(bf16[272,128]{1,0:T(8,128)(2,1)S(1)} %get-tuple-element.31), channel_id=1, source_target_pairs={{1,0},{2,1},{3,2},{4,3},{5,4},{6,5},{7,6},{8,7},{9,8},{10,9},{11,1... | collective-permute-start | bytes 208904 | tf_op jit(solution)/shard_map/ppermute | solution.py:426
  18.8 1.2 %copy-done = bf16[27,128,128]{2,1,0:T(8,128)(2,1)S(1)} copy-done((bf16[27,128,128]{2,1,0:T(8,128)(2,1)S(1)}, bf16[27,128,128]{2,1,0:T(8,128)(2,1)}, u32[]{:S(2)}) %copy-start) | copy-done | bytes 884760
  20.3 6.8 %collective-permute-done.1.high_ref.refs_5_ = bf16[272,128]{1,0:T(8,128)(2,1)S(1)} collective-permute-done((bf16[272,128]{1,0:T(8,128)(2,1)S(1)}, bf16[272,128]{1,0:T(8,128)(2,1)S(1)}, u32[]{:S(2)}, u32[]{:S(2)}) %collective-permute-start.1) | collective-permute-done | bytes 69664 | tf_op jit(solution)/shard_map/ppermute | solution.py:426
  27.1 1.8 %kernel_gradient.1 = (f32[1736,128]{1,0:T(8,128)S(1)}, f32[1736,128]{1,0:T(8,128)S(1)}) custom-call(bf16[16,128]{1,0:T(8,128)(2,1)S(1)} %get-tuple-element.25.refs_0_, s32[1]{0:T(128)} %bitcast.1.refs_1_.half_ref, bf16[1024,128]{1,0:T(8,128)(2,1)S(1)} %get-tuple-element.26.refs_2_.refs_1_, bf16[1024,128]{1,0:T(8,128)(2,1)S(1)} %get-tuple-element.34.refs_3_.refs_1_, ...), custom_call_target="tpu_custom_call" | custom-call | tf_op jit(solution)/shard_map/kernel_gradient/pallas_call | solution.py:337
  28.9 3.0 %collective-permute-start.6 = (f32[1736,128]{1,0:T(8,128)S(1)}, f32[1736,128]{1,0:T(8,128)S(1)}, u32[]{:S(2)}, u32[]{:S(2)}) collective-permute-start(f32[1736,128]{1,0:T(8,128)S(1)} %get-tuple-element.37), channel_id=1, source_target_pairs={{0,1},{1,0},{2,3},{3,2},{4,5},{5,4},{6,7},{7,6},{8,9},{9,8},{10,11... | collective-permute-start | bytes 2666504 | tf_op jit(solution)/shard_map/ppermute | solution.py:431
  31.9 2.0 %collective-permute-done.6.refs_1_ = f32[1736,128]{1,0:T(8,128)S(1)} collective-permute-done((f32[1736,128]{1,0:T(8,128)S(1)}, f32[1736,128]{1,0:T(8,128)S(1)}, u32[]{:S(2)}, u32[]{:S(2)}) %collective-permute-start.6) | collective-permute-done | bytes 888864 | tf_op jit(solution)/shard_map/ppermute | solution.py:431
  35.0 7.0 %all-to-all-start = ((s16[16,112,128]{2,1,0:T(8,128)(2,1)}), s16[16,112,128]{2,1,0:T(8,128)(2,1)S(1)}, u32[]{:S(2)}, u32[]{:S(2)}) async-start(s16[16,112,128]{2,1,0:T(8,128)(2,1)} %bitcast.2), calls=%async_computation | async-start | bytes 917504 | tf_op jit(solution)/shard_map/all_to_all | solution.py:436
  42.1 3.9 %collective-permute-start.4 = (bf16[96,128]{1,0:T(8,128)(2,1)S(1)}, bf16[96,128]{1,0:T(8,128)(2,1)S(1)}, u32[]{:S(2)}, u32[]{:S(2)}) collective-permute-start(bf16[96,128]{1,0:T(8,128)(2,1)S(1)} %get-tuple-element.32), channel_id=1, source_target_pairs={{0,1},{1,2},{2,3},{3,4},{4,5},{5,6},{6,7},{7,8},{8,9},{9,10},{10,1... | collective-permute-start | bytes 73736 | tf_op jit(solution)/shard_map/ppermute | solution.py:426
  45.9 1.9 %collective-permute-start.5 = (bf16[96,128]{1,0:T(8,128)(2,1)S(1)}, bf16[96,128]{1,0:T(8,128)(2,1)S(1)}, u32[]{:S(2)}, u32[]{:S(2)}) collective-permute-start(bf16[96,128]{1,0:T(8,128)(2,1)S(1)} %get-tuple-element.33.refs_8_), channel_id=1, source_target_pairs={{1,0},{2,1},{3,2},{4,3},{5,4},{6,5},{7,6},{8,7},{9,8},{10,9},{11,1... | collective-permute-start | bytes 73736 | tf_op jit(solution)/shard_map/ppermute | solution.py:426
  47.9 3.5 %collective-permute-done.5.refs_2_.refs_9_ = bf16[96,128]{1,0:T(8,128)(2,1)S(1)} collective-permute-done((bf16[96,128]{1,0:T(8,128)(2,1)S(1)}, bf16[96,128]{1,0:T(8,128)(2,1)S(1)}, u32[]{:S(2)}, u32[]{:S(2)}) %collective-permute-start.5) | collective-permute-done | bytes 24608 | tf_op jit(solution)/shard_map/ppermute | solution.py:426
  52.5 7.1 %all_to_all.15 = s16[4,112,128]{2,1,0:T(8,128)(2,1)S(1)} all-to-all(s16[4,112,128]{2,1,0:T(8,128)(2,1)S(1)} %bitcast.14), channel_id=1, replica_groups={{0,8,16,24},{1,9,17,25},{2,10,18,26},{3,11,19,27},{4,12,20,28},{5,13,21..., dimensions={0} | all-to-all | bytes 229376 | tf_op jit(solution)/shard_map/all_to_all | solution.py:436
  59.7 7.1 %collective-permute-start.7 = (s16[112,128]{1,0:T(8,128)(2,1)S(1)}, s16[112,128]{1,0:T(8,128)(2,1)S(1)}, u32[]{:S(2)}, u32[]{:S(2)}) collective-permute-start(s16[112,128]{1,0:T(8,128)(2,1)S(1)} %sum_blocks.5.refs_10_.refs_0_), channel_id=1, source_target_pairs={{0,32},{1,33},{2,34},{3,35},{4,36},{5,37},{6,38},{7,39},{8,40},{9,... | collective-permute-start | bytes 86024 | tf_op jit(solution)/shard_map/ppermute | solution.py:431
  66.8 1.8 %convolution.2 = (bf16[2,512,128]{2,1,0:T(8,128)(2,1)}, f32[8,128]{1,0:T(8,128)S(1)}) custom-call(bf16[16,128]{1,0:T(8,128)(2,1)S(1)} %get-tuple-element.25.refs_0_, bf16[1024,128]{1,0:T(8,128)(2,1)S(1)} %get-tuple-element.26.refs_2_.refs_1_, bf16[1024,128]{1,0:T(8,128)(2,1)S(1)} %get-tuple-element.27.refs_2_, bf16[3456,128]{1,0:T(8,128)(2,1)S(1)} %bitcast.12, ...), custom_call_target="tpu_custom_call" | custom-call | flops 1811939328 | bytes 2000000 | tf_op jit(solution)/shard_map/convolution/pallas_call | solution.py:372
  68.7 7.1 %collective-permute-start.8 = (s16[112,128]{1,0:T(8,128)(2,1)S(1)}, s16[112,128]{1,0:T(8,128)(2,1)S(1)}, u32[]{:S(2)}, u32[]{:S(2)}) collective-permute-start(s16[112,128]{1,0:T(8,128)(2,1)S(1)} %sum_blocks.6.refs_11_.refs_0_), channel_id=1, source_target_pairs={{0,96},{1,97},{2,98},{3,99},{4,100},{5,101},{6,102},{7,103},{8,104... | collective-permute-start | bytes 86024 | tf_op jit(solution)/shard_map/ppermute | solution.py:431
  75.8 1.8 %convolution.3 = (bf16[2,512,128]{2,1,0:T(8,128)(2,1)}, f32[8,128]{1,0:T(8,128)S(1)}) custom-call(bf16[16,128]{1,0:T(8,128)(2,1)S(1)} %get-tuple-element.25.refs_0_, bf16[1024,128]{1,0:T(8,128)(2,1)S(1)} %get-tuple-element.26.refs_2_.refs_1_, bf16[1024,128]{1,0:T(8,128)(2,1)S(1)} %get-tuple-element.27.refs_2_, ...), custom_call_target="tpu_custom_call", output_to_operand_aliasing={{0}: (10, {})} | custom-call | flops 1811939328 | bytes 2000000 | tf_op jit(solution)/shard_map/convolution/pallas_call | solution.py:372
  78.6 7.3 %all-to-all-start.2 = ((s16[16,112,128]{2,1,0:T(8,128)(2,1)}), s16[16,112,128]{2,1,0:T(8,128)(2,1)S(1)}, u32[]{:S(2)}, u32[]{:S(2)}) async-start(s16[16,112,128]{2,1,0:T(8,128)(2,1)} %bitcast.6), calls=%async_computation.2 | async-start | bytes 917504 | tf_op jit(solution)/shard_map/all_to_all | solution.py:436
  85.9 1.8 %feature_gradient.2 = (bf16[2,512,128]{2,1,0:T(8,128)(2,1)}, f32[8,128]{1,0:T(8,128)S(1)}) custom-call(bf16[16,128]{1,0:T(8,128)(2,1)S(1)} %get-tuple-element.25.refs_0_, bf16[1024,128]{1,0:T(8,128)(2,1)S(1)} %get-tuple-element.34.refs_3_.refs_1_, bf16[1024,128]{1,0:T(8,128)(2,1)S(1)} %get-tuple-element.27.refs_2_, ...), custom_call_target="tpu_custom_call" | custom-call | flops 1811939328 | bytes 2000000 | tf_op jit(solution)/shard_map/feature_gradient/pallas_call | solution.py:372
  87.7 1.8 %feature_gradient.3 = (bf16[2,512,128]{2,1,0:T(8,128)(2,1)}, f32[8,128]{1,0:T(8,128)S(1)}) custom-call(bf16[16,128]{1,0:T(8,128)(2,1)S(1)} %get-tuple-element.25.refs_0_, bf16[1024,128]{1,0:T(8,128)(2,1)S(1)} %get-tuple-element.34.refs_3_.refs_1_, bf16[1024,128]{1,0:T(8,128)(2,1)S(1)} %get-tuple-element.27.refs_2_, ...), custom_call_target="tpu_custom_call", output_to_operand_aliasing={{0}: (10, {})} | custom-call | flops 1811939328 | bytes 2000000 | tf_op jit(solution)/shard_map/feature_gradient/pallas_call | solution.py:372
  89.5 5.2 %all-to-all-done.2 = s16[16,112,128]{2,1,0:T(8,128)(2,1)S(1)} async-done(((s16[16,112,128]{2,1,0:T(8,128)(2,1)}), s16[16,112,128]{2,1,0:T(8,128)(2,1)S(1)}, u32[]{:S(2)}, u32[]{:S(2)}) %all-to-all-start.2) | async-done | bytes 458784 | tf_op jit(solution)/shard_map/all_to_all | solution.py:436
  94.7 5.0 %collective-permute-start.9 = (s16[1792,128]{1,0:T(8,128)(2,1)S(1)}, s16[1792,128]{1,0:T(8,128)(2,1)S(1)}, u32[]{:S(2)}, u32[]{:S(2)}) collective-permute-start(s16[1792,128]{1,0:T(8,128)(2,1)S(1)} %passed.1.code_ref), channel_id=1, source_target_pairs={{0,1},{1,0},{2,3},{3,2},{4,5},{5,4},{6,7},{7,6},{8,9},{9,8},{10,11... | collective-permute-start | bytes 1376264 | tf_op jit(solution)/shard_map/ppermute | solution.py:431
  (21 shorter events, 6.0 us)
Async XLA Ops:
  1.9 18.3 %collective-permute-start = (bf16[272,128]{1,0:T(8,128)(2,1)S(1)}, bf16[272,128]{1,0:T(8,128)(2,1)S(1)}, u32[]{:S(2)}, u32[]{:S(2)}) collective-permute-start(bf16[272,128]{1,0:T(8,128)(2,1)S(1)} %get-tuple-element.28), channel_id=1, source_target_pairs={{0,32},{1,33},{2,34},{3,35},{4,36},{5,37},{6,38},{7,39},{8,40},{9,... | collective-permute-start | bytes 208904 | tf_op jit(solution)/shard_map/ppermute | solution.py:426
  11.6 15.5 %collective-permute-start.1 = (bf16[272,128]{1,0:T(8,128)(2,1)S(1)}, bf16[272,128]{1,0:T(8,128)(2,1)S(1)}, u32[]{:S(2)}, u32[]{:S(2)}) collective-permute-start(bf16[272,128]{1,0:T(8,128)(2,1)S(1)} %get-tuple-element.29), channel_id=1, source_target_pairs={{32,0},{33,1},{34,2},{35,3},{36,4},{37,5},{38,6},{39,7},{40,8},{41... | collective-permute-start | bytes 208904 | tf_op jit(solution)/shard_map/ppermute | solution.py:426
  12.9 14.2 %collective-permute-start.2 = (bf16[272,128]{1,0:T(8,128)(2,1)S(1)}, bf16[272,128]{1,0:T(8,128)(2,1)S(1)}, u32[]{:S(2)}, u32[]{:S(2)}) collective-permute-start(bf16[272,128]{1,0:T(8,128)(2,1)S(1)} %get-tuple-element.30.after_ref), channel_id=1, source_target_pairs={{0,1},{1,2},{2,3},{3,4},{4,5},{5,6},{6,7},{7,8},{8,9},{9,10},{10,1... | collective-permute-start | bytes 208904 | tf_op jit(solution)/shard_map/ppermute | solution.py:426
  16.9 10.2 %collective-permute-start.3 = (bf16[272,128]{1,0:T(8,128)(2,1)S(1)}, bf16[272,128]{1,0:T(8,128)(2,1)S(1)}, u32[]{:S(2)}, u32[]{:S(2)}) collective-permute-start(bf16[272,128]{1,0:T(8,128)(2,1)S(1)} %get-tuple-element.31), channel_id=1, source_target_pairs={{1,0},{2,1},{3,2},{4,3},{5,4},{6,5},{7,6},{8,7},{9,8},{10,9},{11,1... | collective-permute-start | bytes 208904 | tf_op jit(solution)/shard_map/ppermute | solution.py:426
  18.8 1.2 %copy-start = (bf16[27,128,128]{2,1,0:T(8,128)(2,1)S(1)}, bf16[27,128,128]{2,1,0:T(8,128)(2,1)}, u32[]{:S(2)}) copy-start(bf16[27,128,128]{2,1,0:T(8,128)(2,1)} %param.8) | copy-start | bytes 2654212
  28.9 5.0 %collective-permute-start.6 = (f32[1736,128]{1,0:T(8,128)S(1)}, f32[1736,128]{1,0:T(8,128)S(1)}, u32[]{:S(2)}, u32[]{:S(2)}) collective-permute-start(f32[1736,128]{1,0:T(8,128)S(1)} %get-tuple-element.37), channel_id=1, source_target_pairs={{0,1},{1,0},{2,3},{3,2},{4,5},{5,4},{6,7},{7,6},{8,9},{9,8},{10,11... | collective-permute-start | bytes 2666504 | tf_op jit(solution)/shard_map/ppermute | solution.py:431
  33.9 32.9 %copy-start.1 = (bf16[27,128,128]{2,1,0:T(8,128)(2,1)S(1)}, bf16[27,128,128]{2,1,0:T(8,128)(2,1)}, u32[]{:S(2)}) copy-start(bf16[27,128,128]{2,1,0:T(8,128)(2,1)} %param.8) | copy-start | bytes 2654212
  35.0 17.2 %all-to-all-start = ((s16[16,112,128]{2,1,0:T(8,128)(2,1)}), s16[16,112,128]{2,1,0:T(8,128)(2,1)S(1)}, u32[]{:S(2)}, u32[]{:S(2)}) async-start(s16[16,112,128]{2,1,0:T(8,128)(2,1)} %bitcast.2), calls=%async_computation | async-start | bytes 917504 | tf_op jit(solution)/shard_map/all_to_all | solution.py:436
  42.1 5.8 %collective-permute-start.4 = (bf16[96,128]{1,0:T(8,128)(2,1)S(1)}, bf16[96,128]{1,0:T(8,128)(2,1)S(1)}, u32[]{:S(2)}, u32[]{:S(2)}) collective-permute-start(bf16[96,128]{1,0:T(8,128)(2,1)S(1)} %get-tuple-element.32), channel_id=1, source_target_pairs={{0,1},{1,2},{2,3},{3,4},{4,5},{5,6},{6,7},{7,8},{8,9},{9,10},{10,1... | collective-permute-start | bytes 73736 | tf_op jit(solution)/shard_map/ppermute | solution.py:426
  45.9 5.4 %collective-permute-start.5 = (bf16[96,128]{1,0:T(8,128)(2,1)S(1)}, bf16[96,128]{1,0:T(8,128)(2,1)S(1)}, u32[]{:S(2)}, u32[]{:S(2)}) collective-permute-start(bf16[96,128]{1,0:T(8,128)(2,1)S(1)} %get-tuple-element.33.refs_8_), channel_id=1, source_target_pairs={{1,0},{2,1},{3,2},{4,3},{5,4},{6,5},{7,6},{8,7},{9,8},{10,9},{11,1... | collective-permute-start | bytes 73736 | tf_op jit(solution)/shard_map/ppermute | solution.py:426
  59.7 9.0 %collective-permute-start.7 = (s16[112,128]{1,0:T(8,128)(2,1)S(1)}, s16[112,128]{1,0:T(8,128)(2,1)S(1)}, u32[]{:S(2)}, u32[]{:S(2)}) collective-permute-start(s16[112,128]{1,0:T(8,128)(2,1)S(1)} %sum_blocks.5.refs_10_.refs_0_), channel_id=1, source_target_pairs={{0,32},{1,33},{2,34},{3,35},{4,36},{5,37},{6,38},{7,39},{8,40},{9,... | collective-permute-start | bytes 86024 | tf_op jit(solution)/shard_map/ppermute | solution.py:431
  68.7 9.0 %collective-permute-start.8 = (s16[112,128]{1,0:T(8,128)(2,1)S(1)}, s16[112,128]{1,0:T(8,128)(2,1)S(1)}, u32[]{:S(2)}, u32[]{:S(2)}) collective-permute-start(s16[112,128]{1,0:T(8,128)(2,1)S(1)} %sum_blocks.6.refs_11_.refs_0_), channel_id=1, source_target_pairs={{0,96},{1,97},{2,98},{3,99},{4,100},{5,101},{6,102},{7,103},{8,104... | collective-permute-start | bytes 86024 | tf_op jit(solution)/shard_map/ppermute | solution.py:431
  78.6 16.2 %all-to-all-start.2 = ((s16[16,112,128]{2,1,0:T(8,128)(2,1)}), s16[16,112,128]{2,1,0:T(8,128)(2,1)S(1)}, u32[]{:S(2)}, u32[]{:S(2)}) async-start(s16[16,112,128]{2,1,0:T(8,128)(2,1)} %bitcast.6), calls=%async_computation.2 | async-start | bytes 917504 | tf_op jit(solution)/shard_map/all_to_all | solution.py:436
  94.7 6.4 %collective-permute-start.9 = (s16[1792,128]{1,0:T(8,128)(2,1)S(1)}, s16[1792,128]{1,0:T(8,128)(2,1)S(1)}, u32[]{:S(2)}, u32[]{:S(2)}) collective-permute-start(s16[1792,128]{1,0:T(8,128)(2,1)S(1)} %passed.1.code_ref), channel_id=1, source_target_pairs={{0,1},{1,0},{2,3},{3,2},{4,5},{5,4},{6,7},{7,6},{8,9},{9,8},{10,11... | collective-permute-start | bytes 1376264 | tf_op jit(solution)/shard_map/ppermute | solution.py:431

commit v7 on v6

--- a/solution.py
+++ b/solution.py
@@ -209,7 +209,12 @@
             total_ref[k * C:(k + 1) * C, :] = total[:, j * C:(j + 1) * C]
     core = core_ref[0]
     keep_ref[...] = total_ref[pl.ds(pl.multiple_of(core * HALF, HALF), HALF + SPARE), :]
-    send_ref[...] = total_ref[pl.ds(pl.multiple_of((1 - core) * HALF, HALF), HALF + SPARE), :]
+    for block in range(16):
+        at = block * CHUNK
+        other = jnp.where(
+            core == 0, total_ref[HALF + at:HALF + at + CODED, :], total_ref[at:at + CODED, :]
+        )
+        send_ref[block * CODED:(block + 1) * CODED, :] = coded(other)
 
 
 def coded(value):
@@ -336,7 +341,7 @@
     half = jax.ShapeDtypeStruct((HALF + SPARE, C), jnp.float32)
     return pl.pallas_call(
         kernel,
-        out_shape=[half, half],
+        out_shape=[half, jax.ShapeDtypeStruct((16 * CODED, C), jnp.int16)],
         in_specs=[VMEM, SMEM] + [VMEM] * 5 + [ANY] * len(after),
         out_specs=[VMEM] * 2,
         scratch_shapes=scratch(BLK_DEV) + [pltpu.VMEM((KV * C + SPARE, C), jnp.float32)],
@@ -403,7 +408,7 @@
 def sum_halves_kernel(a_ref, b_ref, out_ref):
     for block in range(HALF // CHUNK):
         rows = slice(block * CHUNK, block * CHUNK + CODED)
-        out_ref[block * CODED:(block + 1) * CODED, :] = coded(a_ref[rows, :] + b_ref[rows, :])
+        out_ref[block * CODED:(block + 1) * CODED, :] = coded(a_ref[rows, :] + decoded(b_ref, block))
 
 
 def sum_blocks_kernel(*refs):
@@ -456,7 +461,7 @@
     clo, chi = edges(*x_from)
     c_from = (shifted(chi, groups, tiles, 0, 1), shifted(clo, groups, tiles, 0, -1))
     halo = (*x_from, *y_from, *c_from)
-    keep, send = wgrad(scale, tag, core, own_in, own_grad, (from_low, *y_from), done, clo)
+    keep, send = wgrad(scale, tag, core, own_in, own_grad, (from_low, *y_from), done, x_from[1])
     got = across(send, CORE)
     value, = small(sum_halves_kernel, [16 * CODED], [keep, got])
     value, = small(sum_blocks_kernel, [4 * CODED], [exchange(value, AXES, XY_SETS)], c_from)

time: 103 us -> 103 us (level)
  transfers between devices with their start and end apart: 12 -> 12, of which waited for: 6 -> 7; matrix products, arithmetic and copies ran while one was open for 0% -> 0% of each run, Pallas kernels for 9% -> 9%
where the time goes in v7:
time: 103 us; the launch traced here: 102 us
  starting transfers between devices  59.2 us (57%)
  waiting for transfers between devices  18.1 us (18%)
  Pallas kernels  15.5 us (15%)
  blocking collectives  7.13 us (7%)
  local copies, waits for them, and re-layouts  1.17 us (1%)
    ppermute x6, starting transfers between devices, shifted(): return lax.ppermute(value, AXES, pairs)  22.8 us
    ppermute x4, starting transfers between devices, across(): return lax.ppermute(value, AXES, [(i, i ^ mask) for i in range(count)])  21.9 us
    all_to_all x2, starting transfers between devices, exchange(): lax.all_to_all(value.reshape(count, -1, C), axis, 0, 0, axis_index_groups...  14.5 us
    ppermute x6, waiting for transfers between devices, shifted(): return lax.ppermute(value, AXES, pairs)  10.3 us
    pallas_call x4, Pallas kernels, conv(): pl.pallas_call(kernel, grid=(1,), out_shape=[bf16(BLK_DEV, VOX, C), jax.S...  7.37 us
    all_to_all x1, blocking collectives, exchange(): lax.all_to_all(value.reshape(count, -1, C), axis, 0, 0, axis_index_groups...  7.13 us
    all_to_all x2, waiting for transfers between devices, exchange(): lax.all_to_all(value.reshape(count, -1, C), axis, 0, 0, axis_index_groups...  5.53 us
    pallas_call x5, Pallas kernels, small(): pl.pallas_call(inner, out_shape=many, in_specs=[VMEM] * len(args) + [ANY]...  2.37 us
  transfers between devices with their start and end apart: 12, of which 7 were waited for; matrix products, arithmetic and copies ran while one was open for 0% of the time, Pallas kernels for 9%

profile of v7, /device:TPU:1, one launch (start us, length us, event | category | flops | bytes accessed | tf_op | source)
XLA Modules:
  0.0 101.9 jit_solution(8786704256892147151)
XLA Ops:
  0.6 1.3 %mask_and_faces.1 = (bf16[1024,128]{1,0:T(8,128)(2,1)S(1)}, bf16[1024,128]{1,0:T(8,128)(2,1)S(1)}, bf16[1024,128]{1,0:T(8,128)(2,1)S(1)}, bf16[16,128]{1,0:T(8,1...) custom-call(s32[2]{0:T(128)} %refs_0_.1, ...), custom_call_target="tpu_custom_call" | custom-call | tf_op jit(solution)/shard_map/mask_and_faces/pallas_call | solution.py:273
  1.9 9.6 %collective-permute-start = (bf16[272,128]{1,0:T(8,128)(2,1)S(1)}, bf16[272,128]{1,0:T(8,128)(2,1)S(1)}, u32[]{:S(2)}, u32[]{:S(2)}) collective-permute-start(bf16[272,128]{1,0:T(8,128)(2,1)S(1)} %get-tuple-element.28), channel_id=1, source_target_pairs={{0,32},{1,33},{2,34},{3,35},{4,36},{5,37},{6,38},{7,39},{8,40},{9,... | collective-permute-start | bytes 208904 | tf_op jit(solution)/shard_map/ppermute | solution.py:431
  11.6 1.3 %collective-permute-start.1 = (bf16[272,128]{1,0:T(8,128)(2,1)S(1)}, bf16[272,128]{1,0:T(8,128)(2,1)S(1)}, u32[]{:S(2)}, u32[]{:S(2)}) collective-permute-start(bf16[272,128]{1,0:T(8,128)(2,1)S(1)} %get-tuple-element.29), channel_id=1, source_target_pairs={{32,0},{33,1},{34,2},{35,3},{36,4},{37,5},{38,6},{39,7},{40,8},{41... | collective-permute-start | bytes 208904 | tf_op jit(solution)/shard_map/ppermute | solution.py:431
  12.9 2.9 %collective-permute-start.3 = (bf16[272,128]{1,0:T(8,128)(2,1)S(1)}, bf16[272,128]{1,0:T(8,128)(2,1)S(1)}, u32[]{:S(2)}, u32[]{:S(2)}) collective-permute-start(bf16[272,128]{1,0:T(8,128)(2,1)S(1)} %get-tuple-element.31), channel_id=1, source_target_pairs={{1,0},{2,1},{3,2},{4,3},{5,4},{6,5},{7,6},{8,7},{9,8},{10,9},{11,1... | collective-permute-start | bytes 208904 | tf_op jit(solution)/shard_map/ppermute | solution.py:431
  15.8 3.0 %collective-permute-start.2 = (bf16[272,128]{1,0:T(8,128)(2,1)S(1)}, bf16[272,128]{1,0:T(8,128)(2,1)S(1)}, u32[]{:S(2)}, u32[]{:S(2)}) collective-permute-start(bf16[272,128]{1,0:T(8,128)(2,1)S(1)} %get-tuple-element.30.after_ref), channel_id=1, source_target_pairs={{0,1},{1,2},{2,3},{3,4},{4,5},{5,6},{6,7},{7,8},{8,9},{9,10},{10,1... | collective-permute-start | bytes 208904 | tf_op jit(solution)/shard_map/ppermute | solution.py:431
  20.3 6.8 %collective-permute-done.1.high_ref.refs_8_.refs_5_ = bf16[272,128]{1,0:T(8,128)(2,1)S(1)} collective-permute-done((bf16[272,128]{1,0:T(8,128)(2,1)S(1)}, bf16[272,128]{1,0:T(8,128)(2,1)S(1)}, u32[]{:S(2)}, u32[]{:S(2)}) %collective-permute-start.1) | collective-permute-done | bytes 69664 | tf_op jit(solution)/shard_map/ppermute | solution.py:431
  27.1 2.1 %kernel_gradient.1 = (f32[1736,128]{1,0:T(8,128)S(1)}, s16[1792,128]{1,0:T(8,128)(2,1)S(1)}) custom-call(bf16[16,128]{1,0:T(8,128)(2,1)S(1)} %get-tuple-element.25.refs_0_, s32[1]{0:T(128)} %bitcast.1.refs_1_.half_ref, bf16[1024,128]{1,0:T(8,128)(2,1)S(1)} %get-tuple-element.26.refs_2_.refs_1_, bf16[1024,128]{1,0:T(8,128)(2,1)S(1)} %get-tuple-element.34.refs_3_.refs_1_, ...), custom_call_target="tpu_custom_call" | custom-call | tf_op jit(solution)/shard_map/kernel_gradient/pallas_call | solution.py:342
  29.1 2.9 %collective-permute-start.6 = (s16[1792,128]{1,0:T(8,128)(2,1)S(1)}, s16[1792,128]{1,0:T(8,128)(2,1)S(1)}, u32[]{:S(2)}, u32[]{:S(2)}) collective-permute-start(s16[1792,128]{1,0:T(8,128)(2,1)S(1)} %get-tuple-element.37), channel_id=1, source_target_pairs={{0,1},{1,0},{2,3},{3,2},{4,5},{5,4},{6,7},{7,6},{8,9},{9,8},{10,11... | collective-permute-start | bytes 1376264 | tf_op jit(solution)/shard_map/ppermute | solution.py:436
  32.0 1.4 %collective-permute-done.6.refs_1_ = s16[1792,128]{1,0:T(8,128)(2,1)S(1)} collective-permute-done((s16[1792,128]{1,0:T(8,128)(2,1)S(1)}, s16[1792,128]{1,0:T(8,128)(2,1)S(1)}, u32[]{:S(2)}, u32[]{:S(2)}) %collective-permute-start.6) | collective-permute-done | bytes 458784 | tf_op jit(solution)/shard_map/ppermute | solution.py:436
  33.4 1.2 %sum_halves.1 = s16[1792,128]{1,0:T(8,128)(2,1)} custom-call(f32[1736,128]{1,0:T(8,128)S(1)} %get-tuple-element.36.refs_0_, s16[1792,128]{1,0:T(8,128)(2,1)S(1)} %collective-permute-done.6.refs_1_), custom_call_target="tpu_custom_call" | custom-call | tf_op jit(solution)/shard_map/sum_halves/pallas_call | solution.py:398
  34.6 6.8 %all-to-all-start = ((s16[16,112,128]{2,1,0:T(8,128)(2,1)}), s16[16,112,128]{2,1,0:T(8,128)(2,1)S(1)}, u32[]{:S(2)}, u32[]{:S(2)}) async-start(s16[16,112,128]{2,1,0:T(8,128)(2,1)} %bitcast.2), calls=%async_computation | async-start | bytes 917504 | tf_op jit(solution)/shard_map/all_to_all | solution.py:441
  41.4 4.1 %collective-permute-start.4 = (bf16[96,128]{1,0:T(8,128)(2,1)S(1)}, bf16[96,128]{1,0:T(8,128)(2,1)S(1)}, u32[]{:S(2)}, u32[]{:S(2)}) collective-permute-start(bf16[96,128]{1,0:T(8,128)(2,1)S(1)} %get-tuple-element.32), channel_id=1, source_target_pairs={{0,1},{1,2},{2,3},{3,4},{4,5},{5,6},{6,7},{7,8},{8,9},{9,10},{10,1... | collective-permute-start | bytes 73736 | tf_op jit(solution)/shard_map/ppermute | solution.py:431
  45.5 1.9 %collective-permute-start.5 = (bf16[96,128]{1,0:T(8,128)(2,1)S(1)}, bf16[96,128]{1,0:T(8,128)(2,1)S(1)}, u32[]{:S(2)}, u32[]{:S(2)}) collective-permute-start(bf16[96,128]{1,0:T(8,128)(2,1)S(1)} %get-tuple-element.33), channel_id=1, source_target_pairs={{1,0},{2,1},{3,2},{4,3},{5,4},{6,5},{7,6},{8,7},{9,8},{10,9},{11,1... | collective-permute-start | bytes 73736 | tf_op jit(solution)/shard_map/ppermute | solution.py:431
  47.5 3.5 %collective-permute-done.5.refs_2_.refs_9_ = bf16[96,128]{1,0:T(8,128)(2,1)S(1)} collective-permute-done((bf16[96,128]{1,0:T(8,128)(2,1)S(1)}, bf16[96,128]{1,0:T(8,128)(2,1)S(1)}, u32[]{:S(2)}, u32[]{:S(2)}) %collective-permute-start.5) | collective-permute-done | bytes 24608 | tf_op jit(solution)/shard_map/ppermute | solution.py:431
  51.5 7.1 %all_to_all.15 = s16[4,112,128]{2,1,0:T(8,128)(2,1)S(1)} all-to-all(s16[4,112,128]{2,1,0:T(8,128)(2,1)S(1)} %bitcast.14), channel_id=1, replica_groups={{0,8,16,24},{1,9,17,25},{2,10,18,26},{3,11,19,27},{4,12,20,28},{5,13,21..., dimensions={0} | all-to-all | bytes 229376 | tf_op jit(solution)/shard_map/all_to_all | solution.py:441
  58.7 7.7 %collective-permute-start.7 = (s16[112,128]{1,0:T(8,128)(2,1)S(1)}, s16[112,128]{1,0:T(8,128)(2,1)S(1)}, u32[]{:S(2)}, u32[]{:S(2)}) collective-permute-start(s16[112,128]{1,0:T(8,128)(2,1)S(1)} %sum_blocks.5.refs_10_.refs_0_), channel_id=1, source_target_pairs={{0,32},{1,33},{2,34},{3,35},{4,36},{5,37},{6,38},{7,39},{8,40},{9,... | collective-permute-start | bytes 86024 | tf_op jit(solution)/shard_map/ppermute | solution.py:436
  66.5 1.8 %convolution.2 = (bf16[2,512,128]{2,1,0:T(8,128)(2,1)}, f32[8,128]{1,0:T(8,128)S(1)}) custom-call(bf16[16,128]{1,0:T(8,128)(2,1)S(1)} %get-tuple-element.25.refs_0_, bf16[1024,128]{1,0:T(8,128)(2,1)S(1)} %get-tuple-element.26.refs_2_.refs_1_, bf16[1024,128]{1,0:T(8,128)(2,1)S(1)} %get-tuple-element.27.refs_2_, bf16[3456,128]{1,0:T(8,128)(2,1)S(1)} %bitcast.12, ...), custom_call_target="tpu_custom_call" | custom-call | flops 1811939328 | bytes 2000000 | tf_op jit(solution)/shard_map/convolution/pallas_call | solution.py:377
  68.4 6.2 %collective-permute-start.8 = (s16[112,128]{1,0:T(8,128)(2,1)S(1)}, s16[112,128]{1,0:T(8,128)(2,1)S(1)}, u32[]{:S(2)}, u32[]{:S(2)}) collective-permute-start(s16[112,128]{1,0:T(8,128)(2,1)S(1)} %sum_blocks.6.refs_11_.refs_0_), channel_id=1, source_target_pairs={{0,96},{1,97},{2,98},{3,99},{4,100},{5,101},{6,102},{7,103},{8,104... | collective-permute-start | bytes 86024 | tf_op jit(solution)/shard_map/ppermute | solution.py:436
  74.6 1.8 %convolution.3 = (bf16[2,512,128]{2,1,0:T(8,128)(2,1)}, f32[8,128]{1,0:T(8,128)S(1)}) custom-call(bf16[16,128]{1,0:T(8,128)(2,1)S(1)} %get-tuple-element.25.refs_0_, bf16[1024,128]{1,0:T(8,128)(2,1)S(1)} %get-tuple-element.26.refs_2_.refs_1_, bf16[1024,128]{1,0:T(8,128)(2,1)S(1)} %get-tuple-element.27.refs_2_, ...), custom_call_target="tpu_custom_call", output_to_operand_aliasing={{0}: (10, {})} | custom-call | flops 1811939328 | bytes 2000000 | tf_op jit(solution)/shard_map/convolution/pallas_call | solution.py:377
  77.8 7.7 %all-to-all-start.2 = ((s16[16,112,128]{2,1,0:T(8,128)(2,1)}), s16[16,112,128]{2,1,0:T(8,128)(2,1)S(1)}, u32[]{:S(2)}, u32[]{:S(2)}) async-start(s16[16,112,128]{2,1,0:T(8,128)(2,1)} %bitcast.6), calls=%async_computation.2 | async-start | bytes 917504 | tf_op jit(solution)/shard_map/all_to_all | solution.py:441
  85.5 1.8 %feature_gradient.2 = (bf16[2,512,128]{2,1,0:T(8,128)(2,1)}, f32[8,128]{1,0:T(8,128)S(1)}) custom-call(bf16[16,128]{1,0:T(8,128)(2,1)S(1)} %get-tuple-element.25.refs_0_, bf16[1024,128]{1,0:T(8,128)(2,1)S(1)} %get-tuple-element.34.refs_3_.refs_1_, bf16[1024,128]{1,0:T(8,128)(2,1)S(1)} %get-tuple-element.27.refs_2_, ...), custom_call_target="tpu_custom_call" | custom-call | flops 1811939328 | bytes 2000000 | tf_op jit(solution)/shard_map/feature_gradient/pallas_call | solution.py:377
  87.3 1.8 %feature_gradient.3 = (bf16[2,512,128]{2,1,0:T(8,128)(2,1)}, f32[8,128]{1,0:T(8,128)S(1)}) custom-call(bf16[16,128]{1,0:T(8,128)(2,1)S(1)} %get-tuple-element.25.refs_0_, bf16[1024,128]{1,0:T(8,128)(2,1)S(1)} %get-tuple-element.34.refs_3_.refs_1_, bf16[1024,128]{1,0:T(8,128)(2,1)S(1)} %get-tuple-element.27.refs_2_, ...), custom_call_target="tpu_custom_call", output_to_operand_aliasing={{0}: (10, {})} | custom-call | flops 1811939328 | bytes 2000000 | tf_op jit(solution)/shard_map/feature_gradient/pallas_call | solution.py:377
  89.2 5.2 %all-to-all-done.2 = s16[16,112,128]{2,1,0:T(8,128)(2,1)S(1)} async-done(((s16[16,112,128]{2,1,0:T(8,128)(2,1)}), s16[16,112,128]{2,1,0:T(8,128)(2,1)S(1)}, u32[]{:S(2)}, u32[]{:S(2)}) %all-to-all-start.2) | async-done | bytes 458784 | tf_op jit(solution)/shard_map/all_to_all | solution.py:441
  94.3 5.1 %collective-permute-start.9 = (s16[1792,128]{1,0:T(8,128)(2,1)S(1)}, s16[1792,128]{1,0:T(8,128)(2,1)S(1)}, u32[]{:S(2)}, u32[]{:S(2)}) collective-permute-start(s16[1792,128]{1,0:T(8,128)(2,1)S(1)} %passed.1.code_ref), channel_id=1, source_target_pairs={{0,1},{1,0},{2,3},{3,2},{4,5},{5,4},{6,7},{7,6},{8,9},{9,8},{10,11... | collective-permute-start | bytes 1376264 | tf_op jit(solution)/shard_map/ppermute | solution.py:436
  (21 shorter events, 5.9 us)
Async XLA Ops:
  1.9 18.3 %collective-permute-start = (bf16[272,128]{1,0:T(8,128)(2,1)S(1)}, bf16[272,128]{1,0:T(8,128)(2,1)S(1)}, u32[]{:S(2)}, u32[]{:S(2)}) collective-permute-start(bf16[272,128]{1,0:T(8,128)(2,1)S(1)} %get-tuple-element.28), channel_id=1, source_target_pairs={{0,32},{1,33},{2,34},{3,35},{4,36},{5,37},{6,38},{7,39},{8,40},{9,... | collective-permute-start | bytes 208904 | tf_op jit(solution)/shard_map/ppermute | solution.py:431
  11.6 15.5 %collective-permute-start.1 = (bf16[272,128]{1,0:T(8,128)(2,1)S(1)}, bf16[272,128]{1,0:T(8,128)(2,1)S(1)}, u32[]{:S(2)}, u32[]{:S(2)}) collective-permute-start(bf16[272,128]{1,0:T(8,128)(2,1)S(1)} %get-tuple-element.29), channel_id=1, source_target_pairs={{32,0},{33,1},{34,2},{35,3},{36,4},{37,5},{38,6},{39,7},{40,8},{41... | collective-permute-start | bytes 208904 | tf_op jit(solution)/shard_map/ppermute | solution.py:431
  12.9 14.2 %collective-permute-start.3 = (bf16[272,128]{1,0:T(8,128)(2,1)S(1)}, bf16[272,128]{1,0:T(8,128)(2,1)S(1)}, u32[]{:S(2)}, u32[]{:S(2)}) collective-permute-start(bf16[272,128]{1,0:T(8,128)(2,1)S(1)} %get-tuple-element.31), channel_id=1, source_target_pairs={{1,0},{2,1},{3,2},{4,3},{5,4},{6,5},{7,6},{8,7},{9,8},{10,9},{11,1... | collective-permute-start | bytes 208904 | tf_op jit(solution)/shard_map/ppermute | solution.py:431
  15.8 11.3 %collective-permute-start.2 = (bf16[272,128]{1,0:T(8,128)(2,1)S(1)}, bf16[272,128]{1,0:T(8,128)(2,1)S(1)}, u32[]{:S(2)}, u32[]{:S(2)}) collective-permute-start(bf16[272,128]{1,0:T(8,128)(2,1)S(1)} %get-tuple-element.30.after_ref), channel_id=1, source_target_pairs={{0,1},{1,2},{2,3},{3,4},{4,5},{5,6},{6,7},{7,8},{8,9},{9,10},{10,1... | collective-permute-start | bytes 208904 | tf_op jit(solution)/shard_map/ppermute | solution.py:431
  18.8 1.2 %copy-start = (bf16[27,128,128]{2,1,0:T(8,128)(2,1)S(1)}, bf16[27,128,128]{2,1,0:T(8,128)(2,1)}, u32[]{:S(2)}) copy-start(bf16[27,128,128]{2,1,0:T(8,128)(2,1)} %param.8) | copy-start | bytes 2654212
  29.1 4.3 %collective-permute-start.6 = (s16[1792,128]{1,0:T(8,128)(2,1)S(1)}, s16[1792,128]{1,0:T(8,128)(2,1)S(1)}, u32[]{:S(2)}, u32[]{:S(2)}) collective-permute-start(s16[1792,128]{1,0:T(8,128)(2,1)S(1)} %get-tuple-element.37), channel_id=1, source_target_pairs={{0,1},{1,0},{2,3},{3,2},{4,5},{5,4},{6,7},{7,6},{8,9},{9,8},{10,11... | collective-permute-start | bytes 1376264 | tf_op jit(solution)/shard_map/ppermute | solution.py:436
  33.4 33.0 %copy-start.1 = (bf16[27,128,128]{2,1,0:T(8,128)(2,1)S(1)}, bf16[27,128,128]{2,1,0:T(8,128)(2,1)}, u32[]{:S(2)}) copy-start(bf16[27,128,128]{2,1,0:T(8,128)(2,1)} %param.8) | copy-start | bytes 2654212
  34.6 16.7 %all-to-all-start = ((s16[16,112,128]{2,1,0:T(8,128)(2,1)}), s16[16,112,128]{2,1,0:T(8,128)(2,1)S(1)}, u32[]{:S(2)}, u32[]{:S(2)}) async-start(s16[16,112,128]{2,1,0:T(8,128)(2,1)} %bitcast.2), calls=%async_computation | async-start | bytes 917504 | tf_op jit(solution)/shard_map/all_to_all | solution.py:441
  41.4 6.0 %collective-permute-start.4 = (bf16[96,128]{1,0:T(8,128)(2,1)S(1)}, bf16[96,128]{1,0:T(8,128)(2,1)S(1)}, u32[]{:S(2)}, u32[]{:S(2)}) collective-permute-start(bf16[96,128]{1,0:T(8,128)(2,1)S(1)} %get-tuple-element.32), channel_id=1, source_target_pairs={{0,1},{1,2},{2,3},{3,4},{4,5},{5,6},{6,7},{7,8},{8,9},{9,10},{10,1... | collective-permute-start | bytes 73736 | tf_op jit(solution)/shard_map/ppermute | solution.py:431
  45.5 5.4 %collective-permute-start.5 = (bf16[96,128]{1,0:T(8,128)(2,1)S(1)}, bf16[96,128]{1,0:T(8,128)(2,1)S(1)}, u32[]{:S(2)}, u32[]{:S(2)}) collective-permute-start(bf16[96,128]{1,0:T(8,128)(2,1)S(1)} %get-tuple-element.33), channel_id=1, source_target_pairs={{1,0},{2,1},{3,2},{4,3},{5,4},{6,5},{7,6},{8,7},{9,8},{10,9},{11,1... | collective-permute-start | bytes 73736 | tf_op jit(solution)/shard_map/ppermute | solution.py:431
  58.7 9.6 %collective-permute-start.7 = (s16[112,128]{1,0:T(8,128)(2,1)S(1)}, s16[112,128]{1,0:T(8,128)(2,1)S(1)}, u32[]{:S(2)}, u32[]{:S(2)}) collective-permute-start(s16[112,128]{1,0:T(8,128)(2,1)S(1)} %sum_blocks.5.refs_10_.refs_0_), channel_id=1, source_target_pairs={{0,32},{1,33},{2,34},{3,35},{4,36},{5,37},{6,38},{7,39},{8,40},{9,... | collective-permute-start | bytes 86024 | tf_op jit(solution)/shard_map/ppermute | solution.py:436
  68.4 8.5 %collective-permute-start.8 = (s16[112,128]{1,0:T(8,128)(2,1)S(1)}, s16[112,128]{1,0:T(8,128)(2,1)S(1)}, u32[]{:S(2)}, u32[]{:S(2)}) collective-permute-start(s16[112,128]{1,0:T(8,128)(2,1)S(1)} %sum_blocks.6.refs_11_.refs_0_), channel_id=1, source_target_pairs={{0,96},{1,97},{2,98},{3,99},{4,100},{5,101},{6,102},{7,103},{8,104... | collective-permute-start | bytes 86024 | tf_op jit(solution)/shard_map/ppermute | solution.py:436
  77.8 16.5 %all-to-all-start.2 = ((s16[16,112,128]{2,1,0:T(8,128)(2,1)}), s16[16,112,128]{2,1,0:T(8,128)(2,1)S(1)}, u32[]{:S(2)}, u32[]{:S(2)}) async-start(s16[16,112,128]{2,1,0:T(8,128)(2,1)} %bitcast.6), calls=%async_computation.2 | async-start | bytes 917504 | tf_op jit(solution)/shard_map/all_to_all | solution.py:441
  94.3 6.5 %collective-permute-start.9 = (s16[1792,128]{1,0:T(8,128)(2,1)S(1)}, s16[1792,128]{1,0:T(8,128)(2,1)S(1)}, u32[]{:S(2)}, u32[]{:S(2)}) collective-permute-start(s16[1792,128]{1,0:T(8,128)(2,1)S(1)} %passed.1.code_ref), channel_id=1, source_target_pairs={{0,1},{1,0},{2,3},{3,2},{4,5},{5,4},{6,7},{7,6},{8,9},{9,8},{10,11... | collective-permute-start | bytes 1376264 | tf_op jit(solution)/shard_map/ppermute | solution.py:436
